TPU v7x, 128 devices: a whole 4x4x4 slice. The times are simulated.
128 devices in a mesh: grp: 4 (over y_hi, core), seq: 32 (over y_lo, x, z).
Axes of the slice: x: 4, y: 4 (y_hi: 2, y_lo: 2; y = y_hi * 2 + y_lo), z: 4, core: 2. Of those that a mesh axis runs over, the one named last changes fastest.
Arguments:
- queries: bfloat16 [65536, 1024], P(('grp', 'seq')), may hold values from -200 to 200
- keys: bfloat16 [65536, 1024], P(('grp', 'seq')), may hold values from -5 to 5
- values: bfloat16 [65536, 1024], P(('grp', 'seq')), may hold values from -6 to 6
- out_grad: bfloat16 [65536, 1024], P(('grp', 'seq')), may hold values from -6 to 6
Outputs:
- attended: bfloat16 [65536, 1024], P(('grp', 'seq'))
- grad_queries: bfloat16 [65536, 1024], P(('grp', 'seq'))
- grad_keys: bfloat16 [65536, 1024], P(('grp', 'seq'))
- grad_values: bfloat16 [65536, 1024], P(('grp', 'seq'))
All inputs are finite; a program needn't handle non-finite values.
Results may differ from a plain program's by a relative error of at most 0.02.
Values may be sent and summed in bfloat16 or wider, within the bound.
No kernel may reach another device: no remote copies, remote signals or barrier semaphores. Data moves between devices by JAX's collectives and lax.ppermute only.
A program may use at most 128 MiB of HBM per device.

v0:
```python
import math

import jax
import jax.numpy as jnp
from jax import lax
from jax.sharding import PartitionSpec as P

H = 16
HD = 64
BLOCK = 512
P1 = 4
P2 = 32
RATIO = 8


EPS = 1e-06
NEG = -1e30


def extended(cells, sides, width):
    for axis, dim in sides:
        count = lax.axis_size(axis)
        ends = count - 1
        head = lax.slice_in_dim(cells, 0, width, axis=dim)
        tail = lax.slice_in_dim(cells, cells.shape[dim] - width, cells.shape[dim], axis=dim)
        cells = jnp.concatenate(
            [
                lax.ppermute(tail, axis, [(i, (i + 1) % count) for i in range(ends)]),
                cells,
                lax.ppermute(head, axis, [((i + 1) % count, i) for i in range(ends)]),
            ],
            axis=dim,
        )
    return cells


def shifted(block, axis, distance):
    devices = range(lax.axis_size(axis))
    route = [(i - distance, i) for i in devices if i - distance in devices]
    return lax.ppermute(block, axis, route)


def keep_bf16(value):
    rounded = lax.optimization_barrier(value.astype(jnp.bfloat16)).astype(jnp.float32)
    return value + lax.stop_gradient(rounded - value)


def pool_rows(stacked, factor):
    count_rows = stacked.shape[1] // factor
    return jnp.mean(
        stacked.reshape(2, count_rows, factor, stacked.shape[2]), axis=2, dtype=jnp.float32
    )


def normalize(pooled):
    shaped = pooled.reshape(pooled.shape[:-1] + (H, HD))
    scaled = shaped * lax.rsqrt(jnp.mean(shaped * shaped, axis=-1, keepdims=True) + EPS)
    return keep_bf16(scaled.reshape(pooled.shape))


def summary_back(pooled, upstream, factor):
    unused, pullback = jax.vjp(normalize, pooled)
    return jnp.repeat(pullback(upstream)[0] / factor, factor, axis=1)


def attend_block(query_rows, grad_rows, key_rows, value_rows, key_live):
    score_scale = 1.0 / math.sqrt(HD)
    pair_width = 2 * HD

    def one_pair(pair_index, totals):
        out_total, query_total, key_total, value_total = totals
        offset = pair_index * pair_width

        def take_pair(matrix):
            return lax.dynamic_slice_in_dim(matrix, offset, pair_width, 1).reshape(
                matrix.shape[0], 2, HD
            )

        query_part = take_pair(query_rows)
        grad_part = take_pair(grad_rows)
        key_part = take_pair(key_rows)
        value_part = take_pair(value_rows)
        scores = (
            jnp.einsum("qhd,khd->hqk", query_part, key_part, preferred_element_type=jnp.float32)
            * score_scale
        )
        scores = jnp.where(key_live[None, None, :], scores, NEG)
        largest = jnp.max(scores, axis=-1, keepdims=True)
        unnormed = jnp.exp(scores - largest)
        attn_probs = unnormed / jnp.sum(unnormed, axis=-1, keepdims=True)
        probs_low = attn_probs.astype(jnp.bfloat16)
        out_part = jnp.einsum(
            "hqk,khd->qhd", probs_low, value_part, preferred_element_type=jnp.float32
        )
        prob_grad = jnp.einsum(
            "qhd,khd->hqk", grad_part, value_part, preferred_element_type=jnp.float32
        )
        row_delta = jnp.sum(attn_probs * prob_grad, axis=-1, keepdims=True)
        score_grad = (attn_probs * (prob_grad - row_delta) * score_scale).astype(jnp.bfloat16)
        query_grad = jnp.einsum(
            "hqk,khd->qhd", score_grad, key_part, preferred_element_type=jnp.float32
        )
        key_grad = jnp.einsum(
            "hqk,qhd->khd", score_grad, query_part, preferred_element_type=jnp.float32
        )
        value_grad = jnp.einsum(
            "hqk,qhd->khd", probs_low, grad_part, preferred_element_type=jnp.float32
        )
        rows_q = query_rows.shape[0]
        rows_k = key_rows.shape[0]
        out_total = lax.dynamic_update_slice_in_dim(
            out_total, out_part.reshape(rows_q, pair_width), offset, 1
        )
        query_total = lax.dynamic_update_slice_in_dim(
            query_total, query_grad.reshape(rows_q, pair_width), offset, 1
        )
        key_total = lax.dynamic_update_slice_in_dim(
            key_total, key_grad.reshape(rows_k, pair_width), offset, 1
        )
        value_total = lax.dynamic_update_slice_in_dim(
            value_total, value_grad.reshape(rows_k, pair_width), offset, 1
        )
        return (out_total, query_total, key_total, value_total)

    query_zero = jnp.zeros(query_rows.shape, jnp.float32)
    key_zero = jnp.zeros(key_rows.shape, jnp.float32)
    return lax.fori_loop(0, H // 2, one_pair, (query_zero, query_zero, key_zero, key_zero))


def per_device(queries, keys, values, out_grad):
    frames = queries.shape[0]
    width_all = queries.shape[1]
    blocks = frames // BLOCK
    near_len = BLOCK // P1
    seq_count = lax.axis_size("seq")
    grp_count = lax.axis_size("grp")
    device = lax.axis_index("grp") * seq_count + lax.axis_index("seq")
    total_blocks = blocks * seq_count * grp_count
    stacked_kv = jnp.stack([keys, values])
    near_pooled = pool_rows(stacked_kv, P1)
    near_local = normalize(near_pooled).astype(jnp.bfloat16)
    near_ext = extended(near_local, ((("grp", "seq"), 1),), near_len)
    group_pooled = pool_rows(stacked_kv, P2)
    group_local = normalize(group_pooled).astype(jnp.bfloat16)
    group_all = lax.all_gather(group_local, "seq", axis=1, tiled=True)
    top_pooled = pool_rows(group_local, RATIO)
    top_local = normalize(top_pooled).astype(jnp.bfloat16)
    top_all = lax.all_gather(top_local, ("grp", "seq"), axis=1, tiled=True)
    group_len = group_all.shape[1]
    top_len = top_all.shape[1]
    key_count = BLOCK + 2 * near_len + group_len + top_len
    position = jnp.arange(key_count, dtype=jnp.int32)
    in_before = jnp.logical_and(position >= BLOCK, position < BLOCK + near_len)
    in_after = jnp.logical_and(position >= BLOCK + near_len, position < BLOCK + 2 * near_len)
    lower = BLOCK + 2 * near_len

    def step(totals, block_index):
        group_grad, top_grad = totals
        before_rows = lax.dynamic_slice_in_dim(near_ext, block_index * near_len, near_len, 1)
        after_rows = lax.dynamic_slice_in_dim(near_ext, (block_index + 2) * near_len, near_len, 1)
        key_sets = jnp.concatenate(
            [stacked_kv, before_rows, after_rows, group_all, top_all], axis=1
        )
        number = device * blocks + block_index
        key_live = jnp.logical_not(
            jnp.logical_or(
                jnp.logical_and(in_before, number == 0),
                jnp.logical_and(in_after, number == total_blocks - 1),
            )
        )
        output, query_grad, key_grad, value_grad = attend_block(
            queries, out_grad, key_sets[0], key_sets[1], key_live
        )
        pair_grad = jnp.stack([key_grad, value_grad])
        group_grad = group_grad + pair_grad[:, lower : lower + group_len]
        top_grad = top_grad + pair_grad[:, lower + group_len :]
        outs = (
            output.astype(jnp.bfloat16),
            query_grad.astype(jnp.bfloat16),
            pair_grad[:, :BLOCK],
            pair_grad[:, BLOCK : BLOCK + near_len],
            pair_grad[:, BLOCK + near_len : lower],
        )
        return ((group_grad, top_grad), outs)

    start_totals = (
        jnp.zeros((2, group_len, width_all), jnp.float32),
        jnp.zeros((2, top_len, width_all), jnp.float32),
    )
    (group_grad, top_grad), stacked_outs = lax.scan(
        step, start_totals, jnp.arange(blocks, dtype=jnp.int32)
    )
    attended_blocks, query_blocks, diag_grads, before_grads, after_grads = stacked_outs
    zero_pad = jnp.zeros((2, 2, near_len, width_all), jnp.float32)
    ext_grads = jnp.concatenate([before_grads, zero_pad]) + jnp.concatenate([zero_pad, after_grads])
    lower_rim = ext_grads[0]
    upper_rim = ext_grads[blocks + 1]
    from_next = shifted(lower_rim.astype(jnp.bfloat16), ("grp", "seq"), -1).astype(lower_rim.dtype)
    from_prev = shifted(upper_rim.astype(jnp.bfloat16), ("grp", "seq"), 1).astype(upper_rim.dtype)
    inner = ext_grads[1 : blocks + 1]
    inner = inner.at[0].add(from_prev)
    inner = inner.at[blocks - 1].add(from_next)
    near_grad = jnp.moveaxis(inner, 1, 0).reshape(2, frames // P1, width_all)
    top_own = lax.psum_scatter(top_grad, ("grp", "seq"), scatter_dimension=1, tiled=True)
    extra = summary_back(top_pooled, top_own, RATIO)
    group_own = (
        lax.psum_scatter(
            group_grad.astype(jnp.bfloat16), "seq", scatter_dimension=1, tiled=True
        ).astype(jnp.float32)
        + extra
    )
    diag_total = jnp.moveaxis(diag_grads, 1, 0).reshape(2, frames, width_all)
    kv_grad = (
        diag_total
        + summary_back(near_pooled, near_grad, P1)
        + summary_back(group_pooled, group_own, P2)
    )
    return (
        attended_blocks.reshape(frames, width_all),
        query_blocks.reshape(frames, width_all),
        kv_grad[0].astype(jnp.bfloat16),
        kv_grad[1].astype(jnp.bfloat16),
    )


def solution(mesh):
    in_specs = (
        P(("grp", "seq"), None),
        P(("grp", "seq"), None),
        P(("grp", "seq"), None),
        P(("grp", "seq"), None),
    )
    out_specs = (
        P(("grp", "seq"), None),
        P(("grp", "seq"), None),
        P(("grp", "seq"), None),
        P(("grp", "seq"), None),
    )
    return jax.shard_map(
        per_device, mesh=mesh, in_specs=in_specs, out_specs=out_specs, check_vma=False
    )
```

profile of v0, /device:TPU:1, one launch (start us, length us, event | category | flops | bytes accessed | tf_op | source)
XLA Modules:
  0.0 1328.8 jit_solution(14760284862054534043)
XLA Ops:
  16.6 4.4 convert_reduce_fusion.1
  27.9 4.4 collective-permute-start
  32.3 7.8 collective-permute-start.1
  42.8 9.7 collective-permute-done
  55.3 94.9 %all-gather.3.cloned.1.call-done = bf16[2,512,1024]{2,0,1:T(2,128)(2,1)} async-done(((bf16[2,16,1024]{2,0,1:T(2,128)(2,1)}), bf16[2,512,1024]{2,0,1:T(2,128)(2,1)}) %all-gather.3.cloned.1.call-update) | async-done | bytes 2097168 | tf_op jit(solution)/shard_map/all_gather | solution.py:145
  150.2 3.6 copy_dynamic-update-slice_fusion
  153.8 309.7 %all-gather.5.cloned.1.call-done = bf16[2,256,1024]{2,0,1:T(2,128)(2,1)} async-done(((bf16[2,2,1024]{2,0,1:T(2,128)(2,1)}), bf16[2,256,1024]{2,0,1:T(2,128)(2,1)}) %all-gather.5.cloned.1.call-update) | async-done | bytes 1048592 | tf_op jit(solution)/shard_map/all_gather | solution.py:148
  466.0 6.3 slice_bitcast_fusion
  477.9 3.5 broadcast.203.clone
  481.4 375.7 %while.38 = (s32[]{:T(128)}, bf16[512,1024]{1,0:T(8,128)(2,1)}, bf16[512,1024]{1,0:T(8,128)(2,1)}, f32[1536,1024]{1,0:T(8,128)}, f32[1536,1024]{1,0:T(8,128)}, /...) while((s32[]{:T(128)}, bf16[512,1024]{1,0:T(8,128)(2,1)}, ...), condition=%wide.region_10.0_spmd.clone, body=%wide.region_6.10_spmd.clone.sunk | while | flops 1654680064 | bytes 54290644 | solution.py:127
  485.9 3.6 fusion.119
  489.6 4.5 fusion.121
  496.5 13.6 %fusion.122 = bf16[2,64,512]{2,1,0:T(8,128)(2,1)S(1)} fusion(bf16[1536,2,64]{0,2,1:T(8,128)(2,1)S(1)} %bitcast.144, f32[2,512,1536]{2,1,0:T(8,128)} %fusion.119, f32[2,512,1536]{2,1,0:T(8,128)} %get-tuple-element.467, f32[2,512]{1,0:T(2,128)S(1)} %get-tuple-element.468), kind=kOutput, calls=%fused_computation.13.clone.1 | convolution fusion | flops 212339200 | bytes 13111296 | tf_op jit(solution)/shard_map/while/body/eval_jaxpr/while/body/eval_jaxpr/hqk,khd->qhd/dot_general | solution.py:100
  510.1 13.3 %fusion.125 = f32[2,64,1536]{2,1,0:T(8,128)S(1)} fusion(bf16[512,2,64]{0,2,1:T(8,128)(2,1)S(1)} %bitcast.155, f32[2,512,1536]{2,1,0:T(8,128)} %fusion.119, f32[2,512,1536]{2,1,0:T(8,128)} %get-tuple-element.467, f32[2,512]{1,0:T(2,128)S(1)} %get-tuple-element.468), kind=kOutput, calls=%fused_computation.12.clone.1 | convolution fusion | flops 212339200 | bytes 13504512 | tf_op jit(solution)/shard_map/while/body/eval_jaxpr/while/body/eval_jaxpr/hqk,qhd->khd/dot_general | solution.py:103
  532.9 3.6 fusion.119
  536.5 4.5 fusion.121
  543.4 13.6 %fusion.122 = bf16[2,64,512]{2,1,0:T(8,128)(2,1)S(1)} fusion(bf16[1536,2,64]{0,2,1:T(8,128)(2,1)S(1)} %bitcast.144, f32[2,512,1536]{2,1,0:T(8,128)} %fusion.119, f32[2,512,1536]{2,1,0:T(8,128)} %get-tuple-element.467, f32[2,512]{1,0:T(2,128)S(1)} %get-tuple-element.468), kind=kOutput, calls=%fused_computation.13.clone.1 | convolution fusion | flops 212339200 | bytes 13111296 | tf_op jit(solution)/shard_map/while/body/eval_jaxpr/while/body/eval_jaxpr/hqk,khd->qhd/dot_general | solution.py:100
  557.0 13.3 %fusion.125 = f32[2,64,1536]{2,1,0:T(8,128)S(1)} fusion(bf16[512,2,64]{0,2,1:T(8,128)(2,1)S(1)} %bitcast.155, f32[2,512,1536]{2,1,0:T(8,128)} %fusion.119, f32[2,512,1536]{2,1,0:T(8,128)} %get-tuple-element.467, f32[2,512]{1,0:T(2,128)S(1)} %get-tuple-element.468), kind=kOutput, calls=%fused_computation.12.clone.1 | convolution fusion | flops 212339200 | bytes 13504512 | tf_op jit(solution)/shard_map/while/body/eval_jaxpr/while/body/eval_jaxpr/hqk,qhd->khd/dot_general | solution.py:103
  579.8 3.6 fusion.119
  583.5 4.5 fusion.121
  590.4 13.6 %fusion.122 = bf16[2,64,512]{2,1,0:T(8,128)(2,1)S(1)} fusion(bf16[1536,2,64]{0,2,1:T(8,128)(2,1)S(1)} %bitcast.144, f32[2,512,1536]{2,1,0:T(8,128)} %fusion.119, f32[2,512,1536]{2,1,0:T(8,128)} %get-tuple-element.467, f32[2,512]{1,0:T(2,128)S(1)} %get-tuple-element.468), kind=kOutput, calls=%fused_computation.13.clone.1 | convolution fusion | flops 212339200 | bytes 13111296 | tf_op jit(solution)/shard_map/while/body/eval_jaxpr/while/body/eval_jaxpr/hqk,khd->qhd/dot_general | solution.py:100
  604.0 13.3 %fusion.125 = f32[2,64,1536]{2,1,0:T(8,128)S(1)} fusion(bf16[512,2,64]{0,2,1:T(8,128)(2,1)S(1)} %bitcast.155, f32[2,512,1536]{2,1,0:T(8,128)} %fusion.119, f32[2,512,1536]{2,1,0:T(8,128)} %get-tuple-element.467, f32[2,512]{1,0:T(2,128)S(1)} %get-tuple-element.468), kind=kOutput, calls=%fused_computation.12.clone.1 | convolution fusion | flops 212339200 | bytes 13504512 | tf_op jit(solution)/shard_map/while/body/eval_jaxpr/while/body/eval_jaxpr/hqk,qhd->khd/dot_general | solution.py:103
  626.8 3.6 fusion.119
  630.5 4.5 fusion.121
  637.4 13.6 %fusion.122 = bf16[2,64,512]{2,1,0:T(8,128)(2,1)S(1)} fusion(bf16[1536,2,64]{0,2,1:T(8,128)(2,1)S(1)} %bitcast.144, f32[2,512,1536]{2,1,0:T(8,128)} %fusion.119, f32[2,512,1536]{2,1,0:T(8,128)} %get-tuple-element.467, f32[2,512]{1,0:T(2,128)S(1)} %get-tuple-element.468), kind=kOutput, calls=%fused_computation.13.clone.1 | convolution fusion | flops 212339200 | bytes 13111296 | tf_op jit(solution)/shard_map/while/body/eval_jaxpr/while/body/eval_jaxpr/hqk,khd->qhd/dot_general | solution.py:100
  651.0 13.3 %fusion.125 = f32[2,64,1536]{2,1,0:T(8,128)S(1)} fusion(bf16[512,2,64]{0,2,1:T(8,128)(2,1)S(1)} %bitcast.155, f32[2,512,1536]{2,1,0:T(8,128)} %fusion.119, f32[2,512,1536]{2,1,0:T(8,128)} %get-tuple-element.467, f32[2,512]{1,0:T(2,128)S(1)} %get-tuple-element.468), kind=kOutput, calls=%fused_computation.12.clone.1 | convolution fusion | flops 212339200 | bytes 13504512 | tf_op jit(solution)/shard_map/while/body/eval_jaxpr/while/body/eval_jaxpr/hqk,qhd->khd/dot_general | solution.py:103
  673.8 3.6 fusion.119
  677.4 4.6 fusion.121
  684.4 13.6 %fusion.122 = bf16[2,64,512]{2,1,0:T(8,128)(2,1)S(1)} fusion(bf16[1536,2,64]{0,2,1:T(8,128)(2,1)S(1)} %bitcast.144, f32[2,512,1536]{2,1,0:T(8,128)} %fusion.119, f32[2,512,1536]{2,1,0:T(8,128)} %get-tuple-element.467, f32[2,512]{1,0:T(2,128)S(1)} %get-tuple-element.468), kind=kOutput, calls=%fused_computation.13.clone.1 | convolution fusion | flops 212339200 | bytes 13111296 | tf_op jit(solution)/shard_map/while/body/eval_jaxpr/while/body/eval_jaxpr/hqk,khd->qhd/dot_general | solution.py:100
  698.0 13.3 %fusion.125 = f32[2,64,1536]{2,1,0:T(8,128)S(1)} fusion(bf16[512,2,64]{0,2,1:T(8,128)(2,1)S(1)} %bitcast.155, f32[2,512,1536]{2,1,0:T(8,128)} %fusion.119, f32[2,512,1536]{2,1,0:T(8,128)} %get-tuple-element.467, f32[2,512]{1,0:T(2,128)S(1)} %get-tuple-element.468), kind=kOutput, calls=%fused_computation.12.clone.1 | convolution fusion | flops 212339200 | bytes 13504512 | tf_op jit(solution)/shard_map/while/body/eval_jaxpr/while/body/eval_jaxpr/hqk,qhd->khd/dot_general | solution.py:103
  720.8 3.6 fusion.119
  724.4 4.5 fusion.121
  731.4 13.6 %fusion.122 = bf16[2,64,512]{2,1,0:T(8,128)(2,1)S(1)} fusion(bf16[1536,2,64]{0,2,1:T(8,128)(2,1)S(1)} %bitcast.144, f32[2,512,1536]{2,1,0:T(8,128)} %fusion.119, f32[2,512,1536]{2,1,0:T(8,128)} %get-tuple-element.467, f32[2,512]{1,0:T(2,128)S(1)} %get-tuple-element.468), kind=kOutput, calls=%fused_computation.13.clone.1 | convolution fusion | flops 212339200 | bytes 13111296 | tf_op jit(solution)/shard_map/while/body/eval_jaxpr/while/body/eval_jaxpr/hqk,khd->qhd/dot_general | solution.py:100
  745.0 13.3 %fusion.125 = f32[2,64,1536]{2,1,0:T(8,128)S(1)} fusion(bf16[512,2,64]{0,2,1:T(8,128)(2,1)S(1)} %bitcast.155, f32[2,512,1536]{2,1,0:T(8,128)} %fusion.119, f32[2,512,1536]{2,1,0:T(8,128)} %get-tuple-element.467, f32[2,512]{1,0:T(2,128)S(1)} %get-tuple-element.468), kind=kOutput, calls=%fused_computation.12.clone.1 | convolution fusion | flops 212339200 | bytes 13504512 | tf_op jit(solution)/shard_map/while/body/eval_jaxpr/while/body/eval_jaxpr/hqk,qhd->khd/dot_general | solution.py:103
  767.8 3.6 fusion.119
  771.4 4.5 fusion.121
  778.4 13.6 %fusion.122 = bf16[2,64,512]{2,1,0:T(8,128)(2,1)S(1)} fusion(bf16[1536,2,64]{0,2,1:T(8,128)(2,1)S(1)} %bitcast.144, f32[2,512,1536]{2,1,0:T(8,128)} %fusion.119, f32[2,512,1536]{2,1,0:T(8,128)} %get-tuple-element.467, f32[2,512]{1,0:T(2,128)S(1)} %get-tuple-element.468), kind=kOutput, calls=%fused_computation.13.clone.1 | convolution fusion | flops 212339200 | bytes 13111296 | tf_op jit(solution)/shard_map/while/body/eval_jaxpr/while/body/eval_jaxpr/hqk,khd->qhd/dot_general | solution.py:100
  791.9 13.3 %fusion.125 = f32[2,64,1536]{2,1,0:T(8,128)S(1)} fusion(bf16[512,2,64]{0,2,1:T(8,128)(2,1)S(1)} %bitcast.155, f32[2,512,1536]{2,1,0:T(8,128)} %fusion.119, f32[2,512,1536]{2,1,0:T(8,128)} %get-tuple-element.467, f32[2,512]{1,0:T(2,128)S(1)} %get-tuple-element.468), kind=kOutput, calls=%fused_computation.12.clone.1 | convolution fusion | flops 212339200 | bytes 13504512 | tf_op jit(solution)/shard_map/while/body/eval_jaxpr/while/body/eval_jaxpr/hqk,qhd->khd/dot_general | solution.py:103
  814.8 3.6 fusion.119
  818.4 4.6 fusion.121
  825.4 13.6 %fusion.122 = bf16[2,64,512]{2,1,0:T(8,128)(2,1)S(1)} fusion(bf16[1536,2,64]{0,2,1:T(8,128)(2,1)S(1)} %bitcast.144, f32[2,512,1536]{2,1,0:T(8,128)} %fusion.119, f32[2,512,1536]{2,1,0:T(8,128)} %get-tuple-element.467, f32[2,512]{1,0:T(2,128)S(1)} %get-tuple-element.468), kind=kOutput, calls=%fused_computation.13.clone.1 | convolution fusion | flops 212339200 | bytes 13111296 | tf_op jit(solution)/shard_map/while/body/eval_jaxpr/while/body/eval_jaxpr/hqk,khd->qhd/dot_general | solution.py:100
  838.9 13.3 %fusion.125 = f32[2,64,1536]{2,1,0:T(8,128)S(1)} fusion(bf16[512,2,64]{0,2,1:T(8,128)(2,1)S(1)} %bitcast.155, f32[2,512,1536]{2,1,0:T(8,128)} %fusion.119, f32[2,512,1536]{2,1,0:T(8,128)} %get-tuple-element.467, f32[2,512]{1,0:T(2,128)S(1)} %get-tuple-element.468), kind=kOutput, calls=%fused_computation.12.clone.1 | convolution fusion | flops 212339200 | bytes 13504512 | tf_op jit(solution)/shard_map/while/body/eval_jaxpr/while/body/eval_jaxpr/hqk,qhd->khd/dot_general | solution.py:103
  865.7 3.6 collective-permute-start.2
  869.3 6.2 collective-permute-start.3
  878.1 3.5 copy.82
  882.9 3.9 collective-permute-done.2
  899.8 123.5 %all-reduce.9.cloned.1.call-done = f32[2,256,1024]{2,0,1:T(2,128)} async-done(((f32[2,256,1024]{2,0,1:T(2,128)}), f32[2,256,1024]{2,0,1:T(2,128)}) %all-reduce.9.cloned.1.call-update) | async-done | bytes 2097168
  1024.5 290.3 %all-reduce.7.cloned.1.call-done = bf16[2,512,1024]{2,0,1:T(2,128)(2,1)} async-done(((bf16[2,512,1024]{2,0,1:T(2,128)(2,1)}), bf16[2,512,1024]{2,0,1:T(2,128)(2,1)}) %all-reduce.7.cloned.1.call-update) | async-done | bytes 2097168
  (262 shorter events, 157.6 us)
Async XLA Ops:
  7.2 8.2 copy-start.7
  7.2 143.0 %all-gather.3.cloned.1.call-start = ((), (), s32[]{:S(2)}) async-start(), calls=%async_computation | async-start | bytes 2162688 | tf_op jit(solution)/shard_map/all_gather | solution.py:145
  9.4 11.6 copy-start.8
  9.7 0.6 copy-start.18
  10.6 10.4 copy-start.10
  10.7 10.3 copy-start.12
  11.4 452.1 %all-gather.5.cloned.1.call-start = ((), (), s32[]{:S(2)}) async-start(), calls=%async_computation.1 | async-start | bytes 1056768 | tf_op jit(solution)/shard_map/all_gather | solution.py:148
  11.7 0.5 copy-start.20
  12.4 8.6 copy-start.14
  13.1 1010.2 %all-reduce.9.cloned.1.call-start = ((), (), s32[]{:S(2)}) async-start(), calls=%async_computation.3 | async-start | bytes 4194304
  21.0 6.9 copy-start
  23.7 1.3 copy-start.5
  23.9 1.2 copy-start.16
  26.6 127.1 %copy-start.2 = (f32[2,128,1024]{2,1,0:T(8,128)}, f32[2,128,1024]{2,1,0:T(8,128)S(1)}, u32[]{:S(2)}) copy-start(f32[2,128,1024]{2,1,0:T(8,128)S(1)} %copy.64) | copy-start | bytes 3145732
  27.9 24.6 %collective-permute-start = (bf16[2,128,1024]{2,1,0:T(8,128)(2,1)}, bf16[2,128,1024]{2,1,0:T(8,128)(2,1)}, u32[]{:S(2)}, u32[]{:S(2)}) collective-permute-start(bf16[2,128,1024]{2,1,0:T(8,128)(2,1)} %fusion.42), channel_id=1, source_target_pairs={{0,1},{1,2},{2,3},{3,4},{4,5},{5,6},{6,7},{7,8},{8,9},{9,10},{10,1... | collective-permute-start | bytes 1572872 | tf_op jit(solution)/shard_map/ppermute | solution.py:28
  32.3 22.1 %collective-permute-start.1 = (bf16[2,128,1024]{2,1,0:T(8,128)(2,1)}, bf16[2,128,1024]{2,1,0:T(8,128)(2,1)S(1)}, u32[]{:S(2)}, u32[]{:S(2)}) collective-permute-start(bf16[2,128,1024]{2,1,0:T(8,128)(2,1)} %fusion.42), channel_id=1, source_target_pairs={{1,0},{2,1},{3,2},{4,3},{5,4},{6,5},{7,6},{8,7},{9,8},{10,9},{11,1... | collective-permute-start | bytes 1572872 | tf_op jit(solution)/shard_map/ppermute | solution.py:30
  861.8 453.0 %all-reduce.7.cloned.1.call-start = ((), (), s32[]{:S(2)}) async-start(), calls=%async_computation.2 | async-start | bytes 4194304
  863.5 1.0 copy-start.4
  865.7 21.1 %collective-permute-start.2 = (bf16[2,128,1024]{2,1,0:T(8,128)(2,1)}, bf16[2,128,1024]{2,1,0:T(8,128)(2,1)}, u32[]{:S(2)}, u32[]{:S(2)}) collective-permute-start(bf16[2,128,1024]{2,1,0:T(8,128)(2,1)} %get-tuple-element.392), channel_id=1, source_target_pairs={{0,1},{1,2},{2,3},{3,4},{4,5},{5,6},{6,7},{7,8},{8,9},{9,10},{10,1... | collective-permute-start | bytes 1572872 | tf_op jit(solution)/shard_map/ppermute | solution.py:40
  869.3 17.5 %collective-permute-start.3 = (bf16[2,128,1024]{2,1,0:T(8,128)(2,1)}, bf16[2,128,1024]{2,1,0:T(8,128)(2,1)}, u32[]{:S(2)}, u32[]{:S(2)}) collective-permute-start(bf16[2,128,1024]{2,1,0:T(8,128)(2,1)} %get-tuple-element.393), channel_id=1, source_target_pairs={{1,0},{2,1},{3,2},{4,3},{5,4},{6,5},{7,6},{8,7},{9,8},{10,9},{11,1... | collective-permute-start | bytes 1572872 | tf_op jit(solution)/shard_map/ppermute | solution.py:40
  878.1 3.5 copy-start.22
  881.6 12.0 copy-start.17
  881.6 15.7 %copy-start.1 = (f32[2,128,1024]{2,1,0:T(8,128)S(1)}, f32[2,128,1024]{2,1,0:T(8,128)}, u32[]{:S(2)}) copy-start(f32[2,128,1024]{2,1,0:T(8,128)} %copy-done) | copy-start | bytes 3145732
  881.6 15.7 %copy-start.3 = (f32[2,128,1024]{2,1,0:T(8,128)S(1)}, f32[2,128,1024]{2,1,0:T(8,128)}, u32[]{:S(2)}) copy-start(f32[2,128,1024]{2,1,0:T(8,128)} %copy-done.2) | copy-start | bytes 3145732
  889.2 8.1 copy-start.6
  891.8 132.2 %copy-start.13 = (f32[2,2,1024]{2,1,0:T(2,128)S(1)}, f32[2,2,1024]{2,1,0:T(2,128)}, u32[]{:S(2)}) copy-start(f32[2,2,1024]{2,1,0:T(2,128)} %copy-done.12) | copy-start | bytes 49156
  891.8 132.4 %copy-start.21 = (f32[2,2,16]{2,1,0:T(2,128)S(1)}, f32[2,2,16]{2,1,0:T(2,128)}, u32[]{:S(2)}) copy-start(f32[2,2,16]{2,1,0:T(2,128)} %copy-done.20) | copy-start | bytes 772
  891.8 132.6 %copy-start.15 = (f32[2,2,1024]{2,1,0:T(2,128)S(1)}, f32[2,2,1024]{2,1,0:T(2,128)}, u32[]{:S(2)}) copy-start(f32[2,2,1024]{2,1,0:T(2,128)} %copy-done.14) | copy-start | bytes 49156
  891.8 423.8 %copy-start.9 = (f32[2,16,1024]{2,1,0:T(8,128)S(1)}, f32[2,16,1024]{2,1,0:T(8,128)}, u32[]{:S(2)}) copy-start(f32[2,16,1024]{2,1,0:T(8,128)} %copy-done.8) | copy-start | bytes 393220
  893.6 422.3 %copy-start.19 = (f32[2,16,16]{2,1,0:T(8,128)S(1)}, f32[2,16,16]{2,1,0:T(8,128)}, u32[]{:S(2)}) copy-start(f32[2,16,16]{2,1,0:T(8,128)} %copy-done.18) | copy-start | bytes 6148
  893.6 422.6 %copy-start.11 = (f32[2,16,1024]{2,1,0:T(8,128)S(1)}, f32[2,16,1024]{2,1,0:T(8,128)}, u32[]{:S(2)}) copy-start(f32[2,16,1024]{2,1,0:T(8,128)} %copy-done.10) | copy-start | bytes 393220
Sparse Core Ops, SparseCore 0:
  11.5 138.6 all-gather.2
  152.4 311.0 all-gather.4
  861.9 161.3 all-reduce.8
  1025.6 289.0 all-reduce.6
where the time goes:
time: 1350 us; the launch traced here: 1330 us
  waiting for transfers between devices  832 us (62%)
  matrix products  317 us (23%)
  local copies, waits for them, and re-layouts  114 us (8%)
  other arithmetic  27.7 us (2%)
  starting transfers between devices  22.1 us (2%)
  between operations  15 us (1%)
    unnamed x6, waiting for transfers between devices  414 us
    all_gather x1, waiting for transfers between devices, per_device(): top_all = lax.all_gather(top_local, ('grp', 'seq'), axis=1, tiled=True)  310 us
    dot_general x8, matrix products, one_pair(): jnp.einsum('hqk,khd->qhd', score_grad, key_part, preferred_element_type=j...  108 us
    dot_general x8, matrix products, one_pair(): jnp.einsum('hqk,qhd->khd', score_grad, query_part, preferred_element_type...  106 us
    all_gather x1, waiting for transfers between devices, per_device(): group_all = lax.all_gather(group_local, 'seq', axis=1, tiled=True)  94.9 us
    sub x8, matrix products, one_pair(): unnormed = jnp.exp(scores - largest)  36.4 us
    dynamic_slice x64, local copies, waits for them, and re-layouts, take_pair(): lax.dynamic_slice_in_dim(matrix, offset, pair_width, 1)  35.8 us
    dot_general x8, matrix products, one_pair(): jnp.einsum('qhd,khd->hqk', grad_part, value_part, preferred_element_type=...  29 us
  transfers between devices with their start and end apart: 8, of which 6 were waited for; matrix products, arithmetic and copies ran while one was open for 4% of the time, Pallas kernels for 0%

commit v1 on v0

v1 whole, which is shorter than its diff:
```python
import math

import jax
import jax.numpy as jnp
from jax import lax
from jax.experimental import pallas as pl
from jax.experimental.pallas import tpu as pltpu
from jax.sharding import PartitionSpec as P

D = 1024
H = 16
HD = 64
PAIR = 2 * HD
BLOCK = 512
P1 = 4
P2 = 32
RATIO = 8
NEAR = BLOCK // P1
OWN = BLOCK // P2
N_SEQ = 32
GROUP = OWN * N_SEQ
TOP = 256
KEYS = BLOCK + 2 * NEAR + GROUP + TOP
CHUNK = 256

EPS = 1e-06
NEG = -1e30
LOG2E = math.log2(math.e)

F32 = jnp.float32
BF16 = jnp.bfloat16


def dot(a, b):
    return jnp.dot(a, b, preferred_element_type=F32)


def pieces(x, count):
    parts = []
    for _ in range(count):
        low = x.astype(BF16)
        parts.append(low)
        x = x - low.astype(F32)
    return parts


def pool_matrix(rows, cols, factor):
    row = lax.broadcasted_iota(jnp.int32, (rows, cols), 0)
    col = lax.broadcasted_iota(jnp.int32, (rows, cols), 1)
    return jnp.where(col // factor == row, 1.0, 0.0).astype(BF16)


def spread_matrix(rows, cols, factor):
    row = lax.broadcasted_iota(jnp.int32, (rows, cols), 0)
    col = lax.broadcasted_iota(jnp.int32, (rows, cols), 1)
    return jnp.where(row // factor == col, 1.0, 0.0).astype(BF16)


def head_means(x):
    width = 256
    row = lax.broadcasted_iota(jnp.int32, (width, width), 0)
    col = lax.broadcasted_iota(jnp.int32, (width, width), 1)
    same = jnp.where(row // HD == col // HD, 1.0, 0.0).astype(BF16)
    tiles = []
    for start in range(0, x.shape[1], width):
        tile = x[:, start : start + width]
        tiles.append(sum(dot(part, same) for part in pieces(tile, 3)))
    return jnp.concatenate(tiles, axis=1) * (1.0 / HD)


def normalize(pooled):
    return pooled * lax.rsqrt(head_means(pooled * pooled) + EPS)


def normalize_back(pooled, upstream):
    scale = lax.rsqrt(head_means(pooled * pooled) + EPS)
    inner = head_means(pooled * upstream)
    return scale * (upstream - pooled * (scale * scale * inner))


def top_pool(rows):
    return jnp.mean(rows.astype(F32).reshape(rows.shape[0] // RATIO, RATIO, rows.shape[1]), axis=1)


def summaries_kernel(k_ref, v_ref, near_ref, group_ref, top_ref):
    for index, ref in enumerate((k_ref, v_ref)):
        rows = ref[...]
        near = dot(pool_matrix(NEAR, BLOCK, P1), rows) * (1.0 / P1)
        near_ref[index] = normalize(near).astype(BF16)
        group = dot(pool_matrix(OWN, BLOCK, P2), rows) * (1.0 / P2)
        group = normalize(group).astype(BF16)
        group_ref[index] = group
        top_ref[index] = normalize(top_pool(group)).astype(BF16)


def summaries(keys, values):
    return pl.pallas_call(
        summaries_kernel,
        out_shape=(
            jax.ShapeDtypeStruct((2, NEAR, D), BF16),
            jax.ShapeDtypeStruct((2, OWN, D), BF16),
            jax.ShapeDtypeStruct((2, OWN // RATIO, D), BF16),
        ),
        compiler_params=pltpu.CompilerParams(vmem_limit_bytes=48 * 1024 * 1024),
        name="summaries",
    )(keys, values)


def finish_kernel(k_ref, v_ref, diag_ref, prev_ref, next_ref, group_ref, top_ref, dk_ref, dv_ref):
    for index, (ref, out_ref) in enumerate(((k_ref, dk_ref), (v_ref, dv_ref))):
        rows = ref[...]
        near = dot(pool_matrix(NEAR, BLOCK, P1), rows) * (1.0 / P1)
        near_up = prev_ref[index].astype(F32) + next_ref[index].astype(F32)
        near_back = normalize_back(near, near_up) * (1.0 / P1)
        group = dot(pool_matrix(OWN, BLOCK, P2), rows) * (1.0 / P2)
        group_low = normalize(group).astype(BF16)
        top_back = normalize_back(top_pool(group_low), top_ref[index]) * (1.0 / RATIO)
        top_back = jnp.broadcast_to(top_back[:, None, :], (OWN // RATIO, RATIO, D)).reshape(OWN, D)
        group_back = normalize_back(group, group_ref[index] + top_back) * (1.0 / P2)
        total = diag_ref[index]
        for part in pieces(near_back, 2):
            total = total + dot(spread_matrix(BLOCK, NEAR, P1), part)
        for part in pieces(group_back, 2):
            total = total + dot(spread_matrix(BLOCK, OWN, P2), part)
        out_ref[...] = total.astype(BF16)


def finish(keys, values, diag, from_prev, from_next, group, top):
    return pl.pallas_call(
        finish_kernel,
        out_shape=(
            jax.ShapeDtypeStruct((BLOCK, D), BF16),
            jax.ShapeDtypeStruct((BLOCK, D), BF16),
        ),
        compiler_params=pltpu.CompilerParams(vmem_limit_bytes=56 * 1024 * 1024),
        name="finish",
    )(keys, values, diag, from_prev, from_next, group, top)


def attend_kernel(
    live_ref, q_ref, g_ref, k_ref, v_ref, before_ref, after_ref, group_ref, top_ref,
    out_ref, dq_ref, diag_ref, dbefore_ref, dafter_ref, dgroup_ref, dtop_ref,
    kcat, vcat, scores, weights, sgrad,
):
    for index, (cat, own) in enumerate(((kcat, k_ref), (vcat, v_ref))):
        cat[0:BLOCK] = own[...]
        cat[BLOCK : BLOCK + NEAR] = before_ref[index]
        cat[BLOCK + NEAR : BLOCK + 2 * NEAR] = after_ref[index]
        low = BLOCK + 2 * NEAR
        cat[low : low + GROUP] = group_ref[:, index].reshape(GROUP, PAIR)
        cat[low + GROUP :] = top_ref[index]
    queries = q_ref[...]
    q_t = queries.T
    g_t = g_ref[...].T
    v_t = vcat[...].T
    k_t = kcat[...].T
    zeros_t = jnp.zeros((HD, BLOCK), BF16)
    ones_t = jnp.ones((HD, KEYS), BF16)
    chunks = range(0, KEYS, CHUNK)
    lane = lax.broadcasted_iota(jnp.int32, (CHUNK, PAIR), 1)
    near_row = lax.broadcasted_iota(jnp.int32, (CHUNK, 1), 0)
    near_bias = jnp.where(near_row < NEAR, live_ref[0], live_ref[1])
    row64 = lax.broadcasted_iota(jnp.int32, (HD, BLOCK), 0)

    def around(head, mine, other):
        return jnp.concatenate([mine, other] if head == 0 else [other, mine], axis=0)

    out_t, dq_t, gs_t = [], [], []
    for head in range(2):
        cut = slice(head * HD, head * HD + HD)
        mine = (lane < HD) if head == 0 else (lane >= HD)
        q_head = around(head, q_t[cut], zeros_t)
        largest = None
        for start in chunks:
            part = dot(kcat[start : start + CHUNK], q_head)
            if start == BLOCK:
                part = part + near_bias
            scores[start : start + CHUNK] = part
            top = jnp.max(part.reshape(CHUNK // 8, 8, BLOCK), axis=0)
            largest = top if largest is None else jnp.maximum(largest, top)
        largest = jnp.max(largest, axis=0, keepdims=True)
        for start in chunks:
            part = (scores[start : start + CHUNK] - largest) * (LOG2E / math.sqrt(HD))
            weights[head, start : start + CHUNK] = jnp.exp2(part).astype(BF16)
        v_head = around(head, v_t[cut], ones_t)
        both = dot(v_head, weights[head])
        other = HD if head == 0 else 0
        inverse = 1.0 / both[other : other + 1]
        attended = both[cut] * inverse
        out_t.append(attended)
        scaled = (g_t[cut].astype(F32) * inverse).astype(BF16)
        gs_t.append(scaled)
        delta = jnp.sum(scaled.astype(F32) * attended, axis=0, keepdims=True)
        extra = jnp.zeros((HD, BLOCK), F32)
        for place, piece in enumerate(pieces(-delta, 3)):
            extra = jnp.where(row64 == place, piece.astype(F32), extra)
        g_head = around(head, scaled, extra.astype(BF16))
        for start in chunks:
            v_part = jnp.where(mine, vcat[start : start + CHUNK], jnp.ones((), BF16))
            part = dot(v_part, g_head)
            part = part * weights[head, start : start + CHUNK].astype(F32)
            sgrad[head, start : start + CHUNK] = part.astype(BF16)
        dq_t.append(dot(k_t, sgrad[head])[cut])
    out_ref[...] = jnp.concatenate(out_t, axis=0).T.astype(BF16)
    dq_ref[...] = (jnp.concatenate(dq_t, axis=0).T * (1.0 / math.sqrt(HD))).astype(BF16)
    scaled = jnp.concatenate(gs_t, axis=0).T
    qlane = lax.broadcasted_iota(jnp.int32, (BLOCK, PAIR), 1)
    zero = jnp.zeros((), BF16)
    q_low, q_high = jnp.where(qlane < HD, queries, zero), jnp.where(qlane < HD, zero, queries)
    g_low, g_high = jnp.where(qlane < HD, scaled, zero), jnp.where(qlane < HD, zero, scaled)
    for start in chunks:
        cut = slice(start, start + CHUNK)
        dk = (dot(sgrad[0, cut], q_low) + dot(sgrad[1, cut], q_high)) * (1.0 / math.sqrt(HD))
        dv = dot(weights[0, cut], g_low) + dot(weights[1, cut], g_high)
        for index, value in enumerate((dk, dv)):
            if start < BLOCK:
                diag_ref[index, cut] = value
            elif start < BLOCK + 2 * NEAR:
                dbefore_ref[index] = value[:NEAR].astype(BF16)
                dafter_ref[index] = value[NEAR:].astype(BF16)
            elif start < BLOCK + 2 * NEAR + GROUP:
                at = (start - BLOCK - 2 * NEAR) // OWN
                dgroup_ref[at : at + CHUNK // OWN, index] = value.astype(BF16).reshape(
                    CHUNK // OWN, OWN, PAIR
                )
            else:
                dtop_ref[index] = value.astype(BF16)


def attend(live, queries, out_grad, keys, values, before, after, group, top):
    def rows(count):
        return pl.BlockSpec((count, PAIR), lambda p: (0, p))

    def stacked(count):
        return pl.BlockSpec((2, count, PAIR), lambda p: (0, 0, p))

    spread = pl.BlockSpec((N_SEQ, 2, OWN, PAIR), lambda p: (0, 0, 0, p))
    return pl.pallas_call(
        attend_kernel,
        grid=(H // 2,),
        in_specs=[pl.BlockSpec(memory_space=pltpu.SMEM)]
        + [rows(BLOCK)] * 4
        + [stacked(NEAR)] * 2
        + [spread, stacked(TOP)],
        out_specs=[rows(BLOCK)] * 2 + [stacked(BLOCK)] + [stacked(NEAR)] * 2 + [spread, stacked(TOP)],
        out_shape=(
            jax.ShapeDtypeStruct((BLOCK, D), BF16),
            jax.ShapeDtypeStruct((BLOCK, D), BF16),
            jax.ShapeDtypeStruct((2, BLOCK, D), F32),
            jax.ShapeDtypeStruct((2, NEAR, D), BF16),
            jax.ShapeDtypeStruct((2, NEAR, D), BF16),
            jax.ShapeDtypeStruct((N_SEQ, 2, OWN, D), BF16),
            jax.ShapeDtypeStruct((2, TOP, D), BF16),
        ),
        scratch_shapes=[
            pltpu.VMEM((KEYS, PAIR), BF16),
            pltpu.VMEM((KEYS, PAIR), BF16),
            pltpu.VMEM((KEYS, BLOCK), F32),
            pltpu.VMEM((2, KEYS, BLOCK), BF16),
            pltpu.VMEM((2, KEYS, BLOCK), BF16),
        ],
        compiler_params=pltpu.CompilerParams(vmem_limit_bytes=56 * 1024 * 1024),
        name="attend",
    )(live, queries, out_grad, keys, values, before, after, group, top)


def shifted(block, distance):
    count = lax.axis_size(("grp", "seq"))
    route = [(i, i + distance) for i in range(count) if 0 <= i + distance < count]
    return lax.ppermute(block, ("grp", "seq"), route)


def grp_swap(block, bit):
    return lax.ppermute(block, "grp", [(i, i ^ bit) for i in range(4)])


def per_device(queries, keys, values, out_grad):
    device = lax.axis_index("grp") * N_SEQ + lax.axis_index("seq")
    count = lax.axis_size(("grp", "seq"))
    near, group, top = summaries(keys, values)
    before = shifted(near, 1)
    after = shifted(near, -1)
    top_pair = jnp.stack([top, grp_swap(top, 2)], axis=1)
    payload = jnp.concatenate([group.reshape(2 * OWN, D), top_pair.reshape(8, D)], axis=0)
    everyone = jnp.broadcast_to(payload[None], (N_SEQ,) + payload.shape)
    everyone = lax.all_to_all(everyone, "seq", 0, 0, tiled=True)
    group_all = everyone[:, : 2 * OWN].reshape(N_SEQ, 2, OWN, D)
    top_mine = everyone[:, 2 * OWN :]
    top_other = grp_swap(top_mine, 1)
    top_all = jnp.stack([top_mine, top_other]).reshape(2, N_SEQ, 2, 4, D)
    top_all = top_all.transpose(2, 0, 1, 3, 4).reshape(2, TOP, D)
    live = jnp.stack(
        [jnp.where(device == 0, NEG, 0.0), jnp.where(device == count - 1, NEG, 0.0)]
    ).astype(F32)
    out, dq, diag, dbefore, dafter, dgroup, dtop = attend(
        live, queries, out_grad, keys, values, before, after, group_all, top_all
    )
    from_next = shifted(dbefore, -1)
    from_prev = shifted(dafter, 1)
    dtop = dtop.reshape(2, 2, N_SEQ, 4, D).transpose(1, 2, 0, 3, 4).reshape(2, N_SEQ, 8, D)
    dtop_mine = (dtop[0].astype(F32) + grp_swap(dtop[1], 1).astype(F32)).astype(BF16)
    returned = jnp.concatenate([dgroup.reshape(N_SEQ, 2 * OWN, D), dtop_mine], axis=1)
    returned = lax.all_to_all(returned, "seq", 0, 0, tiled=True)
    summed = jnp.sum(returned.astype(F32), axis=0)
    group_up = summed[: 2 * OWN].reshape(2, OWN, D)
    top_up = summed[2 * OWN :].reshape(2, 2, 2, D)
    top_up = top_up[:, 0] + grp_swap(top_up[:, 1], 2)
    dk, dv = finish(keys, values, diag, from_prev, from_next, group_up, top_up)
    return out, dq, dk, dv


def solution(mesh):
    spec = P(("grp", "seq"), None)
    return jax.shard_map(
        per_device, mesh=mesh, in_specs=(spec,) * 4, out_specs=(spec,) * 4, check_vma=False
    )
```

time: 1350 us -> 197 us (0.15); the launches traced: 1330 us -> 197 us
  waiting for transfers between devices: 832 us -> 51 us
  matrix products: 317 us -> 0 us
  local copies, waits for them, and re-layouts: 114 us -> 11.1 us
  Pallas kernels: 0 us -> 59.6 us
  blocking collectives: 0 us -> 40.1 us
  other arithmetic: 27.7 us -> 5.05 us
  between operations: 15 us -> 0.84 us
    unnamed x6 -> x0, waiting for transfers between devices: 414 us -> none
    all_gather x2 -> x0, waiting for transfers between devices: 405 us -> none  [the longest x1 310 us: per_device(): top_all = lax.all_gather(top_local, ('grp', 'seq'), axis=1, tiled=True)]
    dot_general x40 -> x0, matrix products: 280 us -> none  [the longest x8 108 us: one_pair(): jnp.einsum('hqk,khd->qhd', score_grad, key_part, preferred_element_type=j...]
    pallas_call x0 -> x3, Pallas kernels: none -> 59.6 us  [the longest x1 47.6 us: attend(): pl.pallas_call(attend_kernel, grid=(H // 2,), in_specs=[pl.BlockSpec(memo...]
    all_to_all x0 -> x1, blocking collectives: none -> 40.1 us  [per_device(): everyone = lax.all_to_all(everyone, 'seq', 0, 0, tiled=True)]
    sub x8 -> x0, matrix products: 36.4 us -> none  [one_pair(): unnormed = jnp.exp(scores - largest)]
    dynamic_slice x64 -> x0, local copies, waits for them, and re-layouts: 35.8 us -> none  [take_pair(): lax.dynamic_slice_in_dim(matrix, offset, pair_width, 1)]
    all_to_all x0 -> x1, waiting for transfers between devices: none -> 26.4 us  [per_device(): returned = lax.all_to_all(returned, 'seq', 0, 0, tiled=True)]
  transfers between devices with their start and end apart: 8 -> 9, of which waited for: 6 -> 7; matrix products, arithmetic and copies ran while one was open for 4% -> 4% of each run, Pallas kernels for 0% -> 0%
where the time goes in v1:
time: 197 us
  Pallas kernels  59.6 us (30%)
  waiting for transfers between devices  51 us (26%)
  blocking collectives  40.1 us (20%)
  starting transfers between devices  29.3 us (15%)
  local copies, waits for them, and re-layouts  11.1 us (6%)
  other arithmetic  5.05 us (3%)
    pallas_call x1, Pallas kernels, attend(): pl.pallas_call(attend_kernel, grid=(H // 2,), in_specs=[pl.BlockSpec(memo...  47.6 us
    all_to_all x1, blocking collectives, per_device(): everyone = lax.all_to_all(everyone, 'seq', 0, 0, tiled=True)  40.1 us
    all_to_all x1, waiting for transfers between devices, per_device(): returned = lax.all_to_all(returned, 'seq', 0, 0, tiled=True)  26.4 us
    ppermute x4, waiting for transfers between devices, shifted(): return lax.ppermute(block, ('grp', 'seq'), route)  19.5 us
    ppermute x4, starting transfers between devices, shifted(): return lax.ppermute(block, ('grp', 'seq'), route)  16.1 us
    pallas_call x1, Pallas kernels, finish(): pl.pallas_call(finish_kernel, out_shape=(jax.ShapeDtypeStruct((BLOCK, D),...  9.86 us
    ppermute x4, starting transfers between devices, grp_swap(): return lax.ppermute(block, 'grp', [(i, i ^ bit) for i in range(4)])  9.13 us
    ppermute x4, waiting for transfers between devices, grp_swap(): return lax.ppermute(block, 'grp', [(i, i ^ bit) for i in range(4)])  5.03 us
  transfers between devices with their start and end apart: 9, of which 7 were waited for; matrix products, arithmetic and copies ran while one was open for 4% of the time, Pallas kernels for 0%

profile of v1, /device:TPU:1, one launch (start us, length us, event | category | flops | bytes accessed | tf_op | source)
XLA Modules:
  0.0 196.9 jit_solution(17188699635400280546)
XLA Ops:
  0.6 0.0 copy-start
  0.6 1.2 copy-done
  1.9 0.0 copy-start.1
  1.9 1.2 copy-done.1
  3.1 2.1 %summaries.1 = (bf16[2,128,1024]{2,1,0:T(8,128)(2,1)S(1)}, bf16[2,16,1024]{2,1,0:T(8,128)(2,1)S(1)}, bf16[2,2,1024]{2,1,0:T(2,128)(2,1)S(1)}) custom-call(bf16[512,1024]{1,0:T(8,128)(2,1)S(1)} %copy-done, bf16[512,1024]{1,0:T(8,128)(2,1)S(1)} %copy-done.1), custom_call_target="tpu_custom_call" | custom-call | tf_op jit(solution)/shard_map/summaries/pallas_call | solution.py:97
  5.2 3.8 %collective-permute-start.2 = (bf16[2,2,1024]{2,1,0:T(2,128)(2,1)S(1)}, bf16[2,2,1024]{2,1,0:T(2,128)(2,1)S(1)}, u32[]{:S(2)}, u32[]{:S(2)}) collective-permute-start(bf16[2,2,1024]{2,1,0:T(2,128)(2,1)S(1)} %get-tuple-element.18), channel_id=1, source_target_pairs={{0,64},{32,96},{64,0},{96,32},{1,65},{33,97},{65,1},{97,33},{2,66}... | collective-permute-start | bytes 24584 | tf_op jit(solution)/shard_map/ppermute | solution.py:274
  9.0 1.0 collective-permute-done.2
  10.2 0.3 broadcast_in_dim.2
  10.5 40.1 %all_to_all.10 = bf16[32,40,1024]{2,1,0:T(8,128)(2,1)S(1)} all-to-all(bf16[32,40,1024]{2,1,0:T(8,128)(2,1)S(1)} %broadcast_in_dim.2), channel_id=1, replica_groups=mesh['grp'=4,'seq'=32] {'seq'}, dimensions={0} | all-to-all | bytes 5242880 | tf_op jit(solution)/shard_map/all_to_all | solution.py:286
  50.6 1.1 copy.22
  51.7 3.6 %collective-permute-start.3 = (bf16[32,8,1024]{2,0,1:T(8,128)(2,1)}, bf16[32,8,1024]{2,0,1:T(8,128)(2,1)}, u32[]{:S(2)}, u32[]{:S(2)}) collective-permute-start(bf16[32,8,1024]{2,0,1:T(8,128)(2,1)} %copy.22), channel_id=1, source_target_pairs={{0,32},{32,0},{64,96},{96,64},{1,33},{33,1},{65,97},{97,65},{2,34}... | collective-permute-start | bytes 1572872 | tf_op jit(solution)/shard_map/ppermute | solution.py:274
  55.3 4.4 %collective-permute-start.1 = (bf16[2,128,1024]{2,1,0:T(8,128)(2,1)S(1)}, bf16[2,128,1024]{2,1,0:T(8,128)(2,1)}, u32[]{:S(2)}, u32[]{:S(2)}) collective-permute-start(bf16[2,128,1024]{2,1,0:T(8,128)(2,1)S(1)} %get-tuple-element.16), channel_id=1, source_target_pairs={{1,0},{2,1},{3,2},{4,3},{5,4},{6,5},{7,6},{8,7},{9,8},{10,9},{11,1... | collective-permute-start | bytes 1572872 | tf_op jit(solution)/shard_map/ppermute | solution.py:270
  59.7 1.9 collective-permute-start
  61.7 0.6 pad_maximum_fusion.3.live_ref
  62.3 1.6 slice.34
  63.9 0.0 collective-permute-done.3
  63.9 1.3 maximum_bitcast_fusion
  65.2 0.8 copy.17
  66.0 1.1 reshape.48.top_ref
  67.1 3.7 %collective-permute-done.1.after_ref = bf16[2,128,1024]{2,1,0:T(8,128)(2,1)} collective-permute-done((bf16[2,128,1024]{2,1,0:T(8,128)(2,1)S(1)}, bf16[2,128,1024]{2,1,0:T(8,128)(2,1)}, u32[]{:S(2)}, u32[]{:S(2)}) %collective-permute-start.1) | collective-permute-done | bytes 524320 | tf_op jit(solution)/shard_map/ppermute | solution.py:270
  70.8 9.1 %collective-permute-done.before_ref = bf16[2,128,1024]{2,1,0:T(8,128)(2,1)} collective-permute-done((bf16[2,128,1024]{2,1,0:T(8,128)(2,1)S(1)}, bf16[2,128,1024]{2,1,0:T(8,128)(2,1)}, u32[]{:S(2)}, u32[]{:S(2)}) %collective-permute-start) | collective-permute-done | bytes 524320 | tf_op jit(solution)/shard_map/ppermute | solution.py:270
  80.0 47.6 %attend.1 = (bf16[512,1024]{1,0:T(8,128)(2,1)}, bf16[512,1024]{1,0:T(8,128)(2,1)}, f32[2,512,1024]{2,1,0:T(8,128)}, bf16[2,128,1024]{2,1,0:T(8,128)(2,1)}, bf16[...) custom-call(f32[2]{0:T(128)} %pad_maximum_fusion.3.live_ref, ...), custom_call_target="tpu_custom_call" | custom-call | tf_op jit(solution)/shard_map/attend/pallas_call | solution.py:238
  127.6 1.5 reshape.50
  129.1 0.3 copy.26
  129.4 0.0 copy-start.2
  129.4 0.1 fusion.2
  129.5 0.3 collective-permute-start.6
  129.8 1.9 collective-permute-done.6
  131.7 0.2 fusion
  131.9 0.3 copy.19
  132.2 0.0 copy-done.2
  132.2 1.8 pad_maximum_fusion
  134.0 4.1 %all-to-all-start.1 = ((bf16[32,40,1024]{2,1,0:T(8,128)(2,1)}), bf16[32,40,1024]{2,1,0:T(8,128)(2,1)S(1)}, u32[]{:S(2)}, u32[]{:S(2)}) async-start(bf16[32,40,1024]{2,1,0:T(8,128)(2,1)} %pad_maximum_fusion), calls=%async_computation.1 | async-start | bytes 5242880 | tf_op jit(solution)/shard_map/all_to_all | solution.py:303
  138.0 3.0 %collective-permute-start.4 = (bf16[2,128,1024]{2,1,0:T(8,128)(2,1)}, bf16[2,128,1024]{2,1,0:T(8,128)(2,1)S(1)}, u32[]{:S(2)}, u32[]{:S(2)}) collective-permute-start(bf16[2,128,1024]{2,1,0:T(8,128)(2,1)} %get-tuple-element.22), channel_id=1, source_target_pairs={{0,1},{1,2},{2,3},{3,4},{4,5},{5,6},{6,7},{7,8},{8,9},{9,10},{10,1... | collective-permute-start | bytes 1572872 | tf_op jit(solution)/shard_map/ppermute | solution.py:270
  141.1 6.8 %collective-permute-start.5 = (bf16[2,128,1024]{2,1,0:T(8,128)(2,1)}, bf16[2,128,1024]{2,1,0:T(8,128)(2,1)}, u32[]{:S(2)}, u32[]{:S(2)}) collective-permute-start(bf16[2,128,1024]{2,1,0:T(8,128)(2,1)} %get-tuple-element.23), channel_id=1, source_target_pairs={{1,0},{2,1},{3,2},{4,3},{5,4},{6,5},{7,6},{8,7},{9,8},{10,9},{11,1... | collective-permute-start | bytes 1572872 | tf_op jit(solution)/shard_map/ppermute | solution.py:270
  147.8 26.4 %all-to-all-done.1 = bf16[32,40,1024]{2,1,0:T(8,128)(2,1)S(1)} async-done(((bf16[32,40,1024]{2,1,0:T(8,128)(2,1)}), bf16[32,40,1024]{2,1,0:T(8,128)(2,1)S(1)}, u32[]{:S(2)}, u32[]{:S(2)}) %all-to-all-start.1) | async-done | bytes 2621472 | tf_op jit(solution)/shard_map/all_to_all | solution.py:303
  174.3 0.5 convert_reduce_fusion
  174.8 1.4 collective-permute-start.7
  176.2 0.7 slice.38
  176.9 2.1 %collective-permute-done.7 = f32[2,2,1024]{2,1,0:T(2,128)S(1)} collective-permute-done((f32[2,2,1024]{2,1,0:T(2,128)S(1)}, f32[2,2,1024]{2,1,0:T(2,128)S(1)}, u32[]{:S(2)}, u32[]{:S(2)}) %collective-permute-start.7) | collective-permute-done | bytes 16416 | tf_op jit(solution)/shard_map/ppermute | solution.py:274
  179.0 0.6 fusion.1.top_ref
  179.6 6.7 %collective-permute-done.4.prev_ref = bf16[2,128,1024]{2,1,0:T(8,128)(2,1)S(1)} collective-permute-done((bf16[2,128,1024]{2,1,0:T(8,128)(2,1)}, bf16[2,128,1024]{2,1,0:T(8,128)(2,1)S(1)}, u32[]{:S(2)}, u32[]{:S(2)}) %collective-permute-start.4) | collective-permute-done | bytes 524320 | tf_op jit(solution)/shard_map/ppermute | solution.py:270
  186.2 0.0 copy-start.3
  186.2 0.0 collective-permute-done.5.next_ref
  186.2 0.8 copy-done.3
  187.0 9.9 %finish.1 = (bf16[512,1024]{1,0:T(8,128)(2,1)}, bf16[512,1024]{1,0:T(8,128)(2,1)}) custom-call(bf16[512,1024]{1,0:T(8,128)(2,1)} %k_ref.5, bf16[512,1024]{1,0:T(8,128)(2,1)} %v_ref.5, f32[2,512,1024]{2,1,0:T(8,128)} %get-tuple-element.21.diag_ref, bf16[2,128,1024]{2,1,0:T(8,128)(2,1)} %copy-done.3, bf16[2,128,1024]{2,1,0:T(8,128)(2,1)} %collective-permute-done.5.next_ref, ...), custom_call_target="tpu_custom_call" | custom-call | tf_op jit(solution)/shard_map/finish/pallas_call | solution.py:129
  (8 shorter events, 0.1 us)
Async XLA Ops:
  0.6 1.2 copy-start
  1.9 1.2 copy-start.1
  5.2 4.9 %collective-permute-start.2 = (bf16[2,2,1024]{2,1,0:T(2,128)(2,1)S(1)}, bf16[2,2,1024]{2,1,0:T(2,128)(2,1)S(1)}, u32[]{:S(2)}, u32[]{:S(2)}) collective-permute-start(bf16[2,2,1024]{2,1,0:T(2,128)(2,1)S(1)} %get-tuple-element.18), channel_id=1, source_target_pairs={{0,64},{32,96},{64,0},{96,32},{1,65},{33,97},{65,1},{97,33},{2,66}... | collective-permute-start | bytes 24584 | tf_op jit(solution)/shard_map/ppermute | solution.py:274
  51.7 12.2 %collective-permute-start.3 = (bf16[32,8,1024]{2,0,1:T(8,128)(2,1)}, bf16[32,8,1024]{2,0,1:T(8,128)(2,1)}, u32[]{:S(2)}, u32[]{:S(2)}) collective-permute-start(bf16[32,8,1024]{2,0,1:T(8,128)(2,1)} %copy.22), channel_id=1, source_target_pairs={{0,32},{32,0},{64,96},{96,64},{1,33},{33,1},{65,97},{97,65},{2,34}... | collective-permute-start | bytes 1572872 | tf_op jit(solution)/shard_map/ppermute | solution.py:274
  55.3 15.5 %collective-permute-start.1 = (bf16[2,128,1024]{2,1,0:T(8,128)(2,1)S(1)}, bf16[2,128,1024]{2,1,0:T(8,128)(2,1)}, u32[]{:S(2)}, u32[]{:S(2)}) collective-permute-start(bf16[2,128,1024]{2,1,0:T(8,128)(2,1)S(1)} %get-tuple-element.16), channel_id=1, source_target_pairs={{1,0},{2,1},{3,2},{4,3},{5,4},{6,5},{7,6},{8,7},{9,8},{10,9},{11,1... | collective-permute-start | bytes 1572872 | tf_op jit(solution)/shard_map/ppermute | solution.py:270
  59.7 20.3 %collective-permute-start = (bf16[2,128,1024]{2,1,0:T(8,128)(2,1)S(1)}, bf16[2,128,1024]{2,1,0:T(8,128)(2,1)}, u32[]{:S(2)}, u32[]{:S(2)}) collective-permute-start(bf16[2,128,1024]{2,1,0:T(8,128)(2,1)S(1)} %get-tuple-element.16), channel_id=1, source_target_pairs={{0,1},{1,2},{2,3},{3,4},{4,5},{5,6},{6,7},{7,8},{8,9},{9,10},{10,1... | collective-permute-start | bytes 1572872 | tf_op jit(solution)/shard_map/ppermute | solution.py:270
  129.4 2.8 %copy-start.2 = (bf16[32,2,16,1024]{3,2,1,0:T(8,128)(2,1)S(1)}, bf16[32,2,16,1024]{3,2,1,0:T(8,128)(2,1)}, u32[]{:S(2)}) copy-start(bf16[32,2,16,1024]{3,2,1,0:T(8,128)(2,1)} %get-tuple-element.24) | copy-start | bytes 6291460
  129.5 2.2 %collective-permute-start.6 = (bf16[32,8,1024]{2,0,1:T(8,128)(2,1)S(1)}, bf16[32,8,1024]{2,0,1:T(8,128)(2,1)S(1)}, u32[]{:S(2)}, u32[]{:S(2)}) collective-permute-start(bf16[32,8,1024]{2,0,1:T(8,128)(2,1)S(1)} %bitcast.35), channel_id=1, source_target_pairs={{0,32},{32,0},{64,96},{96,64},{1,33},{33,1},{65,97},{97,65},{2,34}... | collective-permute-start | bytes 1572872 | tf_op jit(solution)/shard_map/ppermute | solution.py:274
  134.0 40.3 %all-to-all-start.1 = ((bf16[32,40,1024]{2,1,0:T(8,128)(2,1)}), bf16[32,40,1024]{2,1,0:T(8,128)(2,1)S(1)}, u32[]{:S(2)}, u32[]{:S(2)}) async-start(bf16[32,40,1024]{2,1,0:T(8,128)(2,1)} %pad_maximum_fusion), calls=%async_computation.1 | async-start | bytes 5242880 | tf_op jit(solution)/shard_map/all_to_all | solution.py:303
  138.0 48.2 %collective-permute-start.4 = (bf16[2,128,1024]{2,1,0:T(8,128)(2,1)}, bf16[2,128,1024]{2,1,0:T(8,128)(2,1)S(1)}, u32[]{:S(2)}, u32[]{:S(2)}) collective-permute-start(bf16[2,128,1024]{2,1,0:T(8,128)(2,1)} %get-tuple-element.22), channel_id=1, source_target_pairs={{0,1},{1,2},{2,3},{3,4},{4,5},{5,6},{6,7},{7,8},{8,9},{9,10},{10,1... | collective-permute-start | bytes 1572872 | tf_op jit(solution)/shard_map/ppermute | solution.py:270
  141.1 45.2 %collective-permute-start.5 = (bf16[2,128,1024]{2,1,0:T(8,128)(2,1)}, bf16[2,128,1024]{2,1,0:T(8,128)(2,1)}, u32[]{:S(2)}, u32[]{:S(2)}) collective-permute-start(bf16[2,128,1024]{2,1,0:T(8,128)(2,1)} %get-tuple-element.23), channel_id=1, source_target_pairs={{1,0},{2,1},{3,2},{4,3},{5,4},{6,5},{7,6},{8,7},{9,8},{10,9},{11,1... | collective-permute-start | bytes 1572872 | tf_op jit(solution)/shard_map/ppermute | solution.py:270
  174.8 4.2 %collective-permute-start.7 = (f32[2,2,1024]{2,1,0:T(2,128)S(1)}, f32[2,2,1024]{2,1,0:T(2,128)S(1)}, u32[]{:S(2)}, u32[]{:S(2)}) collective-permute-start(f32[2,2,1024]{2,1,0:T(2,128)S(1)} %slice_bitcast_fusion), channel_id=1, source_target_pairs={{0,64},{32,96},{64,0},{96,32},{1,65},{33,97},{65,1},{97,33},{2,66}... | collective-permute-start | bytes 49160 | tf_op jit(solution)/shard_map/ppermute | solution.py:274
  186.2 0.8 copy-start.3

commit v2 on v1

v2 whole, which is shorter than its diff:
```python
import math

import jax
import jax.numpy as jnp
from jax import lax
from jax.experimental import pallas as pl
from jax.experimental.pallas import tpu as pltpu
from jax.sharding import PartitionSpec as P

D = 1024
H = 16
HD = 64
PAIR = 2 * HD
PAIRS = D // PAIR
BLOCK = 512
BOTH = 2 * BLOCK
P1 = 4
P2 = 32
RATIO = 8
NEAR = BLOCK // P1
OWN = BLOCK // P2
N_SEQ = 32
GROUP = OWN * N_SEQ
TOP = 256
SENT = 2 * OWN + 8
WIDE = GROUP + TOP + 2 * NEAR
CHUNK = 256
ROWS = 128
TILES = BLOCK // ROWS
UNROLL = 2
SOFT = 1.0 / math.sqrt(HD)

EPS = 1e-06
NEG = -1e30
LOG2E = math.log2(math.e)

F32 = jnp.float32
BF16 = jnp.bfloat16


def dot(a, b):
    return jnp.dot(a, b, preferred_element_type=F32)


def pieces(x, count):
    parts = []
    for _ in range(count):
        low = x.astype(BF16)
        parts.append(low)
        x = x - low.astype(F32)
    return parts


def pool_matrix(rows, cols, factor):
    row = lax.broadcasted_iota(jnp.int32, (rows, cols), 0)
    col = lax.broadcasted_iota(jnp.int32, (rows, cols), 1)
    return jnp.where(col // factor == row, 1.0, 0.0).astype(BF16)


def spread_matrix(rows, cols, factor):
    row = lax.broadcasted_iota(jnp.int32, (rows, cols), 0)
    col = lax.broadcasted_iota(jnp.int32, (rows, cols), 1)
    return jnp.where(row // factor == col, 1.0, 0.0).astype(BF16)


def head_means(*xs):
    width = 256
    row = lax.broadcasted_iota(jnp.int32, (width, width), 0)
    col = lax.broadcasted_iota(jnp.int32, (width, width), 1)
    same = jnp.where(row // HD == col // HD, 1.0 / HD, 0.0).astype(BF16)
    stack = [x[:, start : start + width] for x in xs for start in range(0, D, width)]
    stack = jnp.concatenate(stack, axis=0)
    count = stack.shape[0]
    found = dot(jnp.concatenate(pieces(stack, 3), axis=0), same)
    found = found[:count] + found[count : 2 * count] + found[2 * count :]
    means, at = [], 0
    for x in xs:
        rows = x.shape[0]
        tiles = [found[at + t * rows : at + t * rows + rows] for t in range(D // width)]
        means.append(jnp.concatenate(tiles, axis=1))
        at += rows * (D // width)
    return means


def normalize(*pooled):
    means = head_means(*[x * x for x in pooled])
    return [x * lax.rsqrt(mean + EPS) for x, mean in zip(pooled, means)]


def normalize_back(pooled, upstream):
    means = head_means(*[x * x for x in pooled], *[x * up for x, up in zip(pooled, upstream)])
    back = []
    for x, up, mean, inner in zip(pooled, upstream, means, means[len(pooled) :]):
        scale = lax.rsqrt(mean + EPS)
        back.append(scale * (up - x * (scale * scale * inner)))
    return back


def top_pool(rows):
    return jnp.mean(rows.astype(F32).reshape(rows.shape[0] // RATIO, RATIO, rows.shape[1]), axis=1)


def summaries_kernel(
    k_ref, v_ref, near_ref, near_pooled_ref, top_ref, pooled_ref, payload_ref, groups
):
    tile = pl.program_id(0)
    pooled = []
    for index, ref in enumerate((k_ref, v_ref)):
        rows = ref[...]
        pooled.append(dot(pool_matrix(ROWS // P1, ROWS, P1), rows) * (1.0 / P1))
        near_pooled_ref[index] = pooled[index]
        groups[index, tile] = dot(pool_matrix(8, ROWS, P2), rows) * (1.0 / P2)
    for index, near in enumerate(normalize(*pooled)):
        near_ref[index] = near.astype(BF16)

    @pl.when(tile == TILES - 1)
    def _():
        pooled = []
        for index in range(2):
            parts = [groups[index, t][: ROWS // P2] for t in range(TILES)]
            pooled.append(jnp.concatenate(parts, axis=0))
            pooled_ref[index] = pooled[index]
        low = [group.astype(BF16) for group in normalize(*pooled)]
        for index, group in enumerate(low):
            payload_ref[:, index * OWN : index * OWN + OWN] = jnp.broadcast_to(
                group[None], (N_SEQ, OWN, D)
            )
        for index, top in enumerate(normalize(*[top_pool(group) for group in low])):
            top_ref[index] = top.astype(BF16)


def collect_kernel(back_ref, up_ref, top_ref):
    up_ref[...] = jnp.sum(back_ref[:, : 2 * OWN].astype(F32), axis=0).reshape(2, OWN, D)
    top_ref[...] = jnp.sum(back_ref[:, 2 * OWN :].astype(F32), axis=0)


def finish_kernel(
    diag_ref, near_pooled_ref, prev_ref, next_ref, pooled_ref, up_ref, top_ref, swapped_ref,
    dk_ref, dv_ref, spread,
):
    tile = pl.program_id(0)

    @pl.when(tile == 0)
    def _():
        pooled = [pooled_ref[0], pooled_ref[1]]
        tops = [top_pool(group.astype(BF16)) for group in normalize(*pooled)]
        top_up = [
            top_ref[4 * index : 4 * index + 2] + swapped_ref[4 * index + 2 : 4 * index + 4]
            for index in range(2)
        ]
        ups = []
        for index, back in enumerate(normalize_back(tops, top_up)):
            back = jnp.broadcast_to(back[:, None, :] * (1.0 / RATIO), (OWN // RATIO, RATIO, D))
            ups.append(up_ref[index] + back.reshape(OWN, D))
        for index, back in enumerate(normalize_back(pooled, ups)):
            spread[index] = back * (1.0 / P2)

    count = ROWS // P1
    near_up = [prev_ref[index].astype(F32) + next_ref[index].astype(F32) for index in range(2)]
    near_back = normalize_back([near_pooled_ref[0], near_pooled_ref[1]], near_up)
    for index, out_ref in enumerate((dk_ref, dv_ref)):
        total = diag_ref[index]
        for part in pieces(near_back[index] * (1.0 / P1), 2):
            total = total + dot(spread_matrix(ROWS, count, P1), part)
        for place in range(ROWS // P2):
            cut = slice(place * P2, place * P2 + P2)
            row = spread[index, pl.ds(tile * (ROWS // P2) + place, 1)]
            out_ref[cut] = (total[cut] + row).astype(BF16)


def starts(count):
    return range(0, count, CHUNK)


def apart(x_t):
    zero = jnp.zeros((HD, BLOCK), x_t.dtype)
    first = jnp.concatenate([x_t[:HD], zero], axis=1)
    second = jnp.concatenate([zero, x_t[HD:]], axis=1)
    return jnp.concatenate([first, second], axis=0)


def together(x):
    return jnp.concatenate([x[:HD, :BLOCK], x[HD:PAIR, BLOCK:]], axis=0)


def by_head(row):
    return jnp.concatenate(
        [jnp.broadcast_to(row[:, :BLOCK], (HD, BLOCK)), jnp.broadcast_to(row[:, BLOCK:], (HD, BLOCK))],
        axis=0,
    )


def head_sums(x):
    return jnp.concatenate(
        [jnp.sum(x[:HD], axis=0, keepdims=True), jnp.sum(x[HD:], axis=0, keepdims=True)], axis=1
    )


def head_rows(x):
    lane = lax.broadcasted_iota(jnp.int32, x.shape, 1)
    zero = jnp.zeros((), BF16)
    return jnp.concatenate([jnp.where(lane < HD, x, zero), jnp.where(lane < HD, zero, x)], axis=0)


def forward(q_t, kcat, v_t, scores, weights, bias):
    count = kcat.shape[0]
    q_both = apart(q_t)
    largest = None
    for start in starts(count):
        part = dot(kcat[start : start + CHUNK], q_both)
        if start in bias:
            part = part + bias[start]
        scores[start : start + CHUNK] = part
        part = jnp.max(part.reshape(CHUNK // 8, 8, BOTH), axis=0)
        largest = part if largest is None else jnp.maximum(largest, part)
    largest = jnp.max(largest, axis=0, keepdims=True)
    for start in starts(count):
        part = (scores[start : start + CHUNK] - largest) * (LOG2E * SOFT)
        weights[start : start + CHUNK] = jnp.exp2(part).astype(BF16)
    found = dot(jnp.concatenate([v_t, jnp.ones((16, count), BF16)], axis=0), weights[...])
    return largest, found[PAIR : PAIR + 1], together(found)


def score_grads(scaled, delta, vones, weights, sgrad):
    row = lax.broadcasted_iota(jnp.int32, (16, BOTH), 0)
    extra = jnp.zeros((16, BOTH), F32)
    for place, piece in enumerate(pieces(-delta, 3)):
        extra = jnp.where(row == place, piece.astype(F32), extra)
    zero = jnp.zeros((PAIR - 16, BOTH), BF16)
    g_both = jnp.concatenate([apart(scaled), extra.astype(BF16), zero], axis=0)
    for start in starts(vones.shape[0]):
        cut = slice(start, start + CHUNK)
        part = dot(vones[cut], g_both)
        sgrad[cut] = (part * weights[cut].astype(F32)).astype(BF16)


def diag_kernel(q_ref, k_ref, v_ref, weights_ref, sum_ref, stats_ref, scores):
    largest, total, summed = forward(
        q_ref[...].T, k_ref, v_ref[...].T, scores, weights_ref.at[0], {}
    )
    stats_ref[0, 0:1] = largest
    stats_ref[0, 1:2] = total
    sum_ref[...] = summed


def low_rows(shape):
    return lax.broadcasted_iota(jnp.int32, shape, 1) < 4


def split_top(ref, lanes):
    both = ref[:, :, lanes].astype(F32).reshape(N_SEQ // 2, 2, 8, PAIR)
    first, second = both[:, 0], both[:, 1]
    low = low_rows(first.shape)
    k = jnp.where(low, first, pltpu.roll(second, 4, 1))
    v = jnp.where(low, pltpu.roll(first, 4, 1), second)
    return k.reshape(TOP // 2, PAIR).astype(BF16), v.reshape(TOP // 2, PAIR).astype(BF16)


def join_top(k, v):
    k = k.reshape(N_SEQ // 2, 8, PAIR)
    v = v.reshape(N_SEQ // 2, 8, PAIR)
    low = low_rows(k.shape)
    first = jnp.where(low, k, pltpu.roll(v, 4, 1))
    second = jnp.where(low, pltpu.roll(k, 4, 1), v)
    return jnp.stack([first, second], axis=1).reshape(N_SEQ, 8, PAIR).astype(BF16)


def wide_kernel(
    live_ref, q_ref, g_ref, before_ref, after_ref, sum_ref, stats_ref,
    group_ref, mine_ref, other_ref,
    out_ref, scaled_ref, delta_ref, kcat_ref, sgrad_ref,
    dgroup_ref, dmine_ref, dother_ref, dbefore_ref, dafter_ref,
    vones, scores, weights,
):
    near_row = lax.broadcasted_iota(jnp.int32, (CHUNK, 1), 0)
    bias = {GROUP + TOP: jnp.where(near_row < NEAR, live_ref[0], live_ref[1])}

    @pl.when(pl.program_id(0) == 0)
    def _():
        vones[:, :, PAIR:] = jnp.ones((UNROLL, WIDE, PAIR), BF16)

    for p in range(UNROLL):
        lanes = slice(p * PAIR, p * PAIR + PAIR)
        wide_pair(
            bias, q_ref.at[:, lanes], g_ref.at[:, lanes],
            before_ref.at[:, :, lanes], after_ref.at[:, :, lanes],
            sum_ref.at[lanes], stats_ref.at[p], group_ref.at[:, :, lanes],
            split_top(mine_ref, lanes), split_top(other_ref, lanes),
            out_ref.at[lanes], scaled_ref.at[lanes], delta_ref.at[p],
            kcat_ref.at[p], sgrad_ref.at[p],
            dgroup_ref.at[:, :, lanes], dmine_ref.at[:, :, lanes], dother_ref.at[:, :, lanes],
            dbefore_ref.at[:, :, lanes], dafter_ref.at[:, :, lanes],
            vones.at[p], scores.at[p], weights.at[p],
        )


def wide_pair(
    bias, q_ref, g_ref, before_ref, after_ref, sum_ref, stats_ref, group_ref, mine, other,
    out_ref, scaled_ref, delta_ref, kcat, sgrad,
    dgroup_ref, dmine_ref, dother_ref, dbefore_ref, dafter_ref,
    vones, scores, weights,
):
    kcat[0:GROUP] = group_ref[:, 0:OWN].reshape(GROUP, PAIR)
    vones[0:GROUP, :PAIR] = group_ref[:, OWN : 2 * OWN].reshape(GROUP, PAIR)
    for start, (k, v) in ((GROUP, mine), (GROUP + TOP // 2, other)):
        kcat[start : start + TOP // 2] = k
        vones[start : start + TOP // 2, :PAIR] = v
    for start, ref in ((GROUP + TOP, before_ref), (GROUP + TOP + NEAR, after_ref)):
        kcat[start : start + NEAR] = ref[0]
        vones[start : start + NEAR, :PAIR] = ref[1]
    queries = q_ref[...]
    largest, total, summed = forward(
        queries.T, kcat, vones[:, :PAIR].T, scores, weights, bias
    )
    local_largest, local_total = stats_ref[0:1], stats_ref[1:2]
    most = jnp.maximum(largest, local_largest)
    share = jnp.exp2((largest - most) * (LOG2E * SOFT))
    local_share = jnp.exp2((local_largest - most) * (LOG2E * SOFT))
    inverse = 1.0 / (share * total + local_share * local_total)
    share = by_head(share * inverse)
    local_share = by_head(local_share * inverse)
    attended = share * summed + local_share * sum_ref[...]
    out_ref[...] = attended.astype(BF16)
    grad = g_ref[...].T.astype(F32)
    local_scaled = (grad * local_share).astype(BF16)
    scaled_ref[...] = local_scaled
    delta_ref[0:1] = head_sums(local_scaled.astype(F32) * attended)
    scaled = (grad * share).astype(BF16)
    score_grads(scaled, head_sums(scaled.astype(F32) * attended), vones, weights, sgrad)
    q_rows = head_rows(queries)
    g_rows = head_rows(scaled.T)
    for start in starts(WIDE):
        cut = slice(start, start + CHUNK)
        dk = dot(sgrad[cut], q_rows) * SOFT
        dv = dot(weights[cut], g_rows)
        if start < GROUP:
            devices = slice(start // OWN, (start + CHUNK) // OWN)
            shape = (CHUNK // OWN, OWN, PAIR)
            dgroup_ref[devices, 0:OWN] = dk.astype(BF16).reshape(shape)
            dgroup_ref[devices, OWN : 2 * OWN] = dv.astype(BF16).reshape(shape)
        elif start < GROUP + TOP:
            half = TOP // 2
            dmine_ref[...] = join_top(dk[:half], dv[:half])
            dother_ref[...] = join_top(dk[half:], dv[half:])
        else:
            for index, value in enumerate((dk, dv)):
                dbefore_ref[index] = value[:NEAR].astype(BF16)
                dafter_ref[index] = value[NEAR:].astype(BF16)


def diag_back_kernel(
    q_ref, k_ref, v_ref, weights_ref, out_t_ref, scaled_ref, delta_ref, kcat_ref, wide_ref,
    out_ref, dq_ref, diag_ref, vones, sgrad,
):
    @pl.when(pl.program_id(0) == 0)
    def _():
        vones[:, PAIR:] = jnp.ones((BLOCK, PAIR), BF16)

    vones[:, :PAIR] = v_ref[...]
    out_ref[...] = out_t_ref[...].T
    weights = weights_ref.at[0]
    scaled = scaled_ref[...]
    score_grads(scaled, delta_ref[0, 0:1], vones, weights, sgrad)
    dq = dot(kcat_ref[0].T, wide_ref[0]) + dot(k_ref[...].T, sgrad[...])
    dq_ref[...] = (together(dq).T * SOFT).astype(BF16)
    q_rows = head_rows(q_ref[...])
    g_rows = head_rows(scaled.T)
    for start in starts(BLOCK):
        cut = slice(start, start + CHUNK)
        diag_ref[0, cut] = dot(sgrad[cut], q_rows) * SOFT
        diag_ref[1, cut] = dot(weights[cut], g_rows)


def shape_of(dtype, *shape):
    return jax.ShapeDtypeStruct(shape, dtype)


def on_lanes(*lead):
    return pl.BlockSpec(lead + (PAIR,), lambda p: (0,) * len(lead) + (p,))


def on_rows(*shape):
    return pl.BlockSpec(shape, lambda p: (p,) + (0,) * (len(shape) - 1))


def on_middle(*shape):
    return pl.BlockSpec(shape, lambda p: (0, p, 0))


def every(*shape):
    return pl.BlockSpec(shape, lambda p: (0,) * len(shape))


SMEM = pl.BlockSpec(memory_space=pltpu.SMEM)
SEQUENCE = on_lanes(BLOCK)
COLUMNS = on_rows(PAIR, BLOCK)
STATS = on_rows(1, 8, BOTH)
DIAG = on_rows(1, BLOCK, BOTH)
WIDE_KEYS = on_rows(1, WIDE, PAIR)
WIDE_GRADS = on_rows(1, WIDE, BOTH)


def call(kernel, name, steps, in_specs, out_specs, out_shape, scratch=()):
    return pl.pallas_call(
        kernel,
        grid=(steps,),
        in_specs=in_specs,
        out_specs=out_specs,
        out_shape=out_shape,
        scratch_shapes=scratch,
        compiler_params=pltpu.CompilerParams(vmem_limit_bytes=56 * 1024 * 1024),
        name=name,
    )


summaries = call(
    summaries_kernel,
    "summaries",
    TILES,
    [on_rows(ROWS, D)] * 2,
    [on_middle(2, ROWS // P1, D)] * 2
    + [every(2, OWN // RATIO, D), every(2, OWN, D), every(N_SEQ, 2 * OWN, D)],
    (
        shape_of(BF16, 2, NEAR, D),
        shape_of(F32, 2, NEAR, D),
        shape_of(BF16, 2, OWN // RATIO, D),
        shape_of(F32, 2, OWN, D),
        shape_of(BF16, N_SEQ, SENT, D),
    ),
    [pltpu.VMEM((2, TILES, 8, D), F32)],
)
diag_forward = call(
    diag_kernel,
    "diag_forward",
    PAIRS,
    [SEQUENCE] * 3,
    [DIAG, COLUMNS, STATS],
    (
        shape_of(BF16, PAIRS, BLOCK, BOTH),
        shape_of(F32, D, BLOCK),
        shape_of(F32, PAIRS, 8, BOTH),
    ),
    [pltpu.VMEM((BLOCK, BOTH), F32)],
)
def wide_lanes(*lead):
    return pl.BlockSpec(lead + (UNROLL * PAIR,), lambda p: (0,) * len(lead) + (p,))


wide_attend = call(
    wide_kernel,
    "wide_attend",
    PAIRS // UNROLL,
    [SMEM]
    + [wide_lanes(BLOCK)] * 2
    + [wide_lanes(2, NEAR)] * 2
    + [on_rows(UNROLL * PAIR, BLOCK), on_rows(UNROLL, 8, BOTH)]
    + [wide_lanes(N_SEQ, 2 * OWN)]
    + [wide_lanes(N_SEQ, 8)] * 2,
    [on_rows(UNROLL * PAIR, BLOCK)] * 2
    + [on_rows(UNROLL, 8, BOTH), on_rows(UNROLL, WIDE, PAIR), on_rows(UNROLL, WIDE, BOTH)]
    + [wide_lanes(N_SEQ, 2 * OWN)]
    + [wide_lanes(N_SEQ, 8)] * 2
    + [wide_lanes(2, NEAR)] * 2,
    (
        shape_of(BF16, D, BLOCK),
        shape_of(BF16, D, BLOCK),
        shape_of(F32, PAIRS, 8, BOTH),
        shape_of(BF16, PAIRS, WIDE, PAIR),
        shape_of(BF16, PAIRS, WIDE, BOTH),
        shape_of(BF16, N_SEQ, SENT, D),
        shape_of(BF16, N_SEQ, 8, D),
        shape_of(BF16, N_SEQ, 8, D),
        shape_of(BF16, 2, NEAR, D),
        shape_of(BF16, 2, NEAR, D),
    ),
    [
        pltpu.VMEM((UNROLL, WIDE, 2 * PAIR), BF16),
        pltpu.VMEM((UNROLL, WIDE, BOTH), F32),
        pltpu.VMEM((UNROLL, WIDE, BOTH), BF16),
    ],
)
diag_backward = call(
    diag_back_kernel,
    "diag_backward",
    PAIRS,
    [SEQUENCE] * 3 + [DIAG] + [COLUMNS] * 2 + [STATS, WIDE_KEYS, WIDE_GRADS],
    [SEQUENCE, SEQUENCE, on_lanes(2, BLOCK)],
    (shape_of(BF16, BLOCK, D), shape_of(BF16, BLOCK, D), shape_of(F32, 2, BLOCK, D)),
    [pltpu.VMEM((BLOCK, 2 * PAIR), BF16), pltpu.VMEM((BLOCK, BOTH), BF16)],
)
collect = pl.pallas_call(
    collect_kernel,
    out_shape=(shape_of(F32, 2, OWN, D), shape_of(F32, 8, D)),
    compiler_params=pltpu.CompilerParams(vmem_limit_bytes=16 * 1024 * 1024),
    name="collect",
)
finish = call(
    finish_kernel,
    "finish",
    TILES,
    [on_middle(2, ROWS, D)]
    + [on_middle(2, ROWS // P1, D)] * 3
    + [every(2, OWN, D)] * 2
    + [every(8, D)] * 2,
    [on_rows(ROWS, D)] * 2,
    (shape_of(BF16, BLOCK, D), shape_of(BF16, BLOCK, D)),
    [pltpu.VMEM((2, OWN, D), F32)],
)


def shifted(block, distance):
    count = lax.axis_size(("grp", "seq"))
    route = [(i, i + distance) for i in range(count) if 0 <= i + distance < count]
    return lax.ppermute(block, ("grp", "seq"), route)


def grp_swap(block, bit):
    return lax.ppermute(block, "grp", [(i, i ^ bit) for i in range(4)])


def per_device(queries, keys, values, out_grad):
    device = lax.axis_index("grp") * N_SEQ + lax.axis_index("seq")
    count = lax.axis_size(("grp", "seq"))
    live = jnp.stack(
        [jnp.where(device == 0, NEG, 0.0), jnp.where(device == count - 1, NEG, 0.0)]
    ).astype(F32)
    near, near_pooled, top, pooled, payload = summaries(keys, values)
    top_pair = jnp.stack([top, grp_swap(top, 2)], axis=1).reshape(8, D)
    tops = jnp.broadcast_to(top_pair[None], (N_SEQ, 8, D))
    payload = lax.dynamic_update_slice(payload, tops, (0, 2 * OWN, 0))
    everyone = lax.all_to_all(payload, "seq", 0, 0, tiled=True)
    before = shifted(near, 1)
    after = shifted(near, -1)
    diag_weights, diag_sum, diag_stats = diag_forward(queries, keys, values)
    everyone, diag_sum = lax.optimization_barrier((everyone, diag_sum))
    top_mine = everyone[:, 2 * OWN :]
    top_other = grp_swap(top_mine, 1)
    out_t, scaled, delta, kcat, sgrad, back, dmine, dother, dbefore, dafter = wide_attend(
        live, queries, out_grad, before, after, diag_sum, diag_stats,
        everyone, top_mine, top_other,
    )
    dmine = (dmine.astype(F32) + grp_swap(dother, 1).astype(F32)).astype(BF16)
    back = lax.dynamic_update_slice(back, dmine, (0, 2 * OWN, 0))
    back = lax.all_to_all(back, "seq", 0, 0, tiled=True)
    from_next = shifted(dbefore, -1)
    from_prev = shifted(dafter, 1)
    out, dq, diag = diag_backward(
        queries, keys, values, diag_weights, out_t, scaled, delta, kcat, sgrad
    )
    back, diag = lax.optimization_barrier((back, diag))
    group_up, top_up = collect(back)
    swapped = grp_swap(top_up, 2)
    dk, dv = finish(
        diag, near_pooled, from_prev, from_next, pooled, group_up, top_up, swapped
    )
    return out, dq, dk, dv


def solution(mesh):
    spec = P(("grp", "seq"), None)
    return jax.shard_map(
        per_device, mesh=mesh, in_specs=(spec,) * 4, out_specs=(spec,) * 4, check_vma=False
    )
```

time: 197 us -> 167 us (0.85); the launches traced: 197 us -> 164 us
  blocking collectives: 40.1 us -> 0 us
  starting transfers between devices: 29.3 us -> 51.8 us
  waiting for transfers between devices: 51 us -> 30.7 us
  Pallas kernels: 59.6 us -> 75.2 us
  local copies, waits for them, and re-layouts: 11.1 us -> 2.41 us
    all_to_all x1 -> x0, blocking collectives: 40.1 us -> none  [per_device(): everyone = lax.all_to_all(everyone, 'seq', 0, 0, tiled=True)]
    pallas_call x3 -> x6, Pallas kernels: 59.6 us -> 75.2 us  [the longest x1 31.4 us: per_device(): wide_attend(live, queries, out_grad, before, after, diag_sum, diag_stats,...]
    all_to_all x1 -> x2, waiting for transfers between devices: 26.4 us -> 12.5 us  [the longest x1 7.82 us: per_device(): everyone = lax.all_to_all(payload, 'seq', 0, 0, tiled=True)]
    all_to_all x1 -> x2, starting transfers between devices: 4.06 us -> 14.8 us  [the longest x1 8.95 us: per_device(): everyone = lax.all_to_all(payload, 'seq', 0, 0, tiled=True)]
    ppermute x4, starting transfers between devices: 9.13 us -> 15 us  [grp_swap(): return lax.ppermute(block, 'grp', [(i, i ^ bit) for i in range(4)])]
    ppermute x4, starting transfers between devices: 16.1 us -> 22 us  [shifted(): return lax.ppermute(block, ('grp', 'seq'), route)]
    ppermute x4, waiting for transfers between devices: 19.5 us -> 14.8 us  [shifted(): return lax.ppermute(block, ('grp', 'seq'), route)]
    reshape x5 -> x0, local copies, waits for them, and re-layouts: 2.92 us -> none  [the longest x2 1.78 us: per_device(): dtop.reshape(2, 2, N_SEQ, 4, D).transpose(1, 2, 0, 3, 4)]
  transfers between devices with their start and end apart: 9 -> 10, of which waited for: 7 -> 7; matrix products, arithmetic and copies ran while one was open for 4% -> 0% of each run, Pallas kernels for 0% -> 18%
where the time goes in v2:
time: 167 us; the launch traced here: 164 us
  Pallas kernels  75.2 us (45%)
  starting transfers between devices  51.8 us (31%)
  waiting for transfers between devices  30.7 us (18%)
  other arithmetic  3.4 us (2%)
  local copies, waits for them, and re-layouts  2.41 us (1%)
    pallas_call x1, Pallas kernels, per_device(): wide_attend(live, queries, out_grad, before, after, diag_sum, diag_stats,...  31.4 us
    ppermute x4, starting transfers between devices, shifted(): return lax.ppermute(block, ('grp', 'seq'), route)  22 us
    pallas_call x1, Pallas kernels, per_device(): diag_backward(queries, keys, values, diag_weights, out_t, scaled, delta,...  18.2 us
    ppermute x4, starting transfers between devices, grp_swap(): return lax.ppermute(block, 'grp', [(i, i ^ bit) for i in range(4)])  15 us
    ppermute x4, waiting for transfers between devices, shifted(): return lax.ppermute(block, ('grp', 'seq'), route)  14.8 us
    pallas_call x1, Pallas kernels, per_device(): diag_weights, diag_sum, diag_stats = diag_forward(queries, keys, values)  11.5 us
    all_to_all x1, starting transfers between devices, per_device(): everyone = lax.all_to_all(payload, 'seq', 0, 0, tiled=True)  8.95 us
    pallas_call x1, Pallas kernels, per_device(): finish(diag, near_pooled, from_prev, from_next, pooled, group_up, top_up,...  7.85 us
  transfers between devices with their start and end apart: 10, of which 7 were waited for; matrix products, arithmetic and copies ran while one was open for 0% of the time, Pallas kernels for 18%

profile of v2, /device:TPU:1, one launch (start us, length us, event | category | flops | bytes accessed | tf_op | source)
XLA Modules:
  0.0 164.3 jit_solution(1048564623793569965)
XLA Ops:
  0.6 5.9 %summaries.1 = (bf16[2,128,1024]{2,1,0:T(8,128)(2,1)}, f32[2,128,1024]{2,1,0:T(8,128)}, bf16[2,2,1024]{2,1,0:T(2,128)(2,1)}, f32[2,16,1024]{2,1,0:T(8,128)}, bf16[32,40,1024]{2,1,0:T(8,128)(2,1)}) custom-call(bf16[512,1024]{1,0:T(8,128)(2,1)} %k_ref.5, bf16[512,1024]{1,0:T(8,128)(2,1)} %v_ref.5), custom_call_target="tpu_custom_call" | custom-call | tf_op jit(solution)/shard_map/summaries/pallas_call | solution.py:527
  6.6 3.8 %collective-permute-start.2 = (bf16[2,2,1024]{2,1,0:T(2,128)(2,1)}, bf16[2,2,1024]{2,1,0:T(2,128)(2,1)S(1)}, u32[]{:S(2)}, u32[]{:S(2)}) collective-permute-start(bf16[2,2,1024]{2,1,0:T(2,128)(2,1)} %get-tuple-element.36), channel_id=1, source_target_pairs={{0,64},{32,96},{64,0},{96,32},{1,65},{33,97},{65,1},{97,33},{2,66}... | collective-permute-start | bytes 24584 | tf_op jit(solution)/shard_map/ppermute | solution.py:518
  10.4 1.3 collective-permute-done.2
  11.6 0.7 pad_maximum_fusion
  12.4 0.9 broadcast_dynamic-update-slice_fusion
  13.3 8.9 %all-to-all-start = ((bf16[32,40,1024]{2,1,0:T(8,128)(2,1)}), bf16[32,40,1024]{2,1,0:T(8,128)(2,1)S(1)}, u32[]{:S(2)}, u32[]{:S(2)}) async-start(bf16[32,40,1024]{2,1,0:T(8,128)(2,1)} %broadcast_dynamic-update-slice_fusion), calls=%async_computation | async-start | bytes 5242880 | tf_op jit(solution)/shard_map/all_to_all | solution.py:531
  22.2 9.7 %collective-permute-start.1 = (bf16[2,128,1024]{2,1,0:T(8,128)(2,1)}, bf16[2,128,1024]{2,1,0:T(8,128)(2,1)}, u32[]{:S(2)}, u32[]{:S(2)}) collective-permute-start(bf16[2,128,1024]{2,1,0:T(8,128)(2,1)} %get-tuple-element.34), channel_id=1, source_target_pairs={{1,0},{2,1},{3,2},{4,3},{5,4},{6,5},{7,6},{8,7},{9,8},{10,9},{11,1... | collective-permute-start | bytes 1572872 | tf_op jit(solution)/shard_map/ppermute | solution.py:514
  32.0 1.9 %collective-permute-start = (bf16[2,128,1024]{2,1,0:T(8,128)(2,1)}, bf16[2,128,1024]{2,1,0:T(8,128)(2,1)}, u32[]{:S(2)}, u32[]{:S(2)}) collective-permute-start(bf16[2,128,1024]{2,1,0:T(8,128)(2,1)} %get-tuple-element.34), channel_id=1, source_target_pairs={{0,1},{1,2},{2,3},{3,4},{4,5},{5,6},{6,7},{7,8},{8,9},{9,10},{10,1... | collective-permute-start | bytes 1572872 | tf_op jit(solution)/shard_map/ppermute | solution.py:514
  33.9 11.5 %diag_forward.1 = (bf16[8,512,1024]{2,1,0:T(8,128)(2,1)}, f32[1024,512]{1,0:T(8,128)}, f32[8,8,1024]{2,1,0:T(8,128)}) custom-call(bf16[512,1024]{1,0:T(8,128)(2,1)} %q_ref.5, bf16[512,1024]{1,0:T(8,128)(2,1)} %k_ref.5, bf16[512,1024]{1,0:T(8,128)(2,1)} %v_ref.5), custom_call_target="tpu_custom_call" | custom-call | tf_op jit(solution)/shard_map/diag_forward/pallas_call | solution.py:534
  45.4 7.8 %all-to-all-done.group_ref = bf16[32,40,1024]{2,1,0:T(8,128)(2,1)S(1)} async-done(((bf16[32,40,1024]{2,1,0:T(8,128)(2,1)}), bf16[32,40,1024]{2,1,0:T(8,128)(2,1)S(1)}, u32[]{:S(2)}, u32[]{:S(2)}) %all-to-all-start) | async-done | bytes 2621472 | tf_op jit(solution)/shard_map/all_to_all | solution.py:531
  53.2 0.0 copy-start.2
  53.3 0.0 copy-start.3
  53.3 5.0 %collective-permute-start.3 = (bf16[32,8,1024]{2,1,0:T(8,128)(2,1)S(1)}, bf16[32,8,1024]{2,1,0:T(8,128)(2,1)}, u32[]{:S(2)}, u32[]{:S(2)}) collective-permute-start(bf16[32,8,1024]{2,1,0:T(8,128)(2,1)S(1)} %slice.3.mine_ref), channel_id=1, source_target_pairs={{0,32},{32,0},{64,96},{96,64},{1,33},{33,1},{65,97},{97,65},{2,34}... | collective-permute-start | bytes 1572872 | tf_op jit(solution)/shard_map/ppermute | solution.py:518
  58.2 0.6 pad_maximum_fusion.1.live_ref
  58.8 5.6 %collective-permute-done.1.after_ref = bf16[2,128,1024]{2,1,0:T(8,128)(2,1)} collective-permute-done((bf16[2,128,1024]{2,1,0:T(8,128)(2,1)}, bf16[2,128,1024]{2,1,0:T(8,128)(2,1)}, u32[]{:S(2)}, u32[]{:S(2)}) %collective-permute-start.1) | collective-permute-done | bytes 524320 | tf_op jit(solution)/shard_map/ppermute | solution.py:514
  64.4 3.8 %collective-permute-done.before_ref = bf16[2,128,1024]{2,1,0:T(8,128)(2,1)} collective-permute-done((bf16[2,128,1024]{2,1,0:T(8,128)(2,1)}, bf16[2,128,1024]{2,1,0:T(8,128)(2,1)}, u32[]{:S(2)}, u32[]{:S(2)}) %collective-permute-start) | collective-permute-done | bytes 524320 | tf_op jit(solution)/shard_map/ppermute | solution.py:514
  68.3 0.0 collective-permute-done.3.other_ref
  68.3 0.0 copy-done.2
  68.3 0.0 copy-done.3
  68.3 31.4 %wide_attend.1 = (bf16[1024,512]{1,0:T(8,128)(2,1)}, bf16[1024,512]{1,0:T(8,128)(2,1)}, f32[8,8,1024]{2,1,0:T(8,128)}, bf16[8,1024,128]{2,1,0:T(8,128)(2,1)}, bf...) custom-call(f32[2]{0:T(128)} %pad_maximum_fusion.1.live_ref, ...), custom_call_target="tpu_custom_call" | custom-call | tf_op jit(solution)/shard_map/wide_attend/pallas_call | solution.py:538
  99.6 0.1 collective-permute-start.4
  99.7 2.1 %collective-permute-done.4 = bf16[32,8,1024]{2,1,0:T(8,128)(2,1)S(1)} collective-permute-done((bf16[32,8,1024]{2,1,0:T(8,128)(2,1)}, bf16[32,8,1024]{2,1,0:T(8,128)(2,1)S(1)}, u32[]{:S(2)}, u32[]{:S(2)}) %collective-permute-start.4) | collective-permute-done | bytes 524320 | tf_op jit(solution)/shard_map/ppermute | solution.py:518
  101.8 2.1 %fusion = bf16[32,40,1024]{2,1,0:T(8,128)(2,1)} fusion(bf16[32,40,1024]{2,1,0:T(8,128)(2,1)} %get-tuple-element.48, bf16[32,8,1024]{2,1,0:T(8,128)(2,1)S(1)} %collective-permute-done.4, bf16[32,8,1024]{2,1,0:T(8,128)(2,1)} %get-tuple-element.49), kind=kLoop, calls=%fused_computation.1 | loop fusion | flops 1048576 | bytes 1572864 | tf_op jit(solution)/shard_map/dynamic_update_slice | solution.py:543
  103.9 5.8 %all-to-all-start.1 = ((bf16[32,40,1024]{2,1,0:T(8,128)(2,1)}), bf16[32,40,1024]{2,1,0:T(8,128)(2,1)S(1)}, u32[]{:S(2)}, u32[]{:S(2)}) async-start(bf16[32,40,1024]{2,1,0:T(8,128)(2,1)} %fusion), calls=%async_computation.1 | async-start | bytes 5242880 | tf_op jit(solution)/shard_map/all_to_all | solution.py:544
  109.8 3.1 %collective-permute-start.5 = (bf16[2,128,1024]{2,1,0:T(8,128)(2,1)}, bf16[2,128,1024]{2,1,0:T(8,128)(2,1)S(1)}, u32[]{:S(2)}, u32[]{:S(2)}) collective-permute-start(bf16[2,128,1024]{2,1,0:T(8,128)(2,1)} %get-tuple-element.54), channel_id=1, source_target_pairs={{0,1},{1,2},{2,3},{3,4},{4,5},{5,6},{6,7},{7,8},{8,9},{9,10},{10,1... | collective-permute-start | bytes 1572872 | tf_op jit(solution)/shard_map/ppermute | solution.py:514
  112.9 7.2 %collective-permute-start.6 = (bf16[2,128,1024]{2,1,0:T(8,128)(2,1)}, bf16[2,128,1024]{2,1,0:T(8,128)(2,1)}, u32[]{:S(2)}, u32[]{:S(2)}) collective-permute-start(bf16[2,128,1024]{2,1,0:T(8,128)(2,1)} %get-tuple-element.55), channel_id=1, source_target_pairs={{1,0},{2,1},{3,2},{4,3},{5,4},{6,5},{7,6},{8,7},{9,8},{10,9},{11,1... | collective-permute-start | bytes 1572872 | tf_op jit(solution)/shard_map/ppermute | solution.py:514
  120.1 18.2 %diag_backward.1 = (bf16[512,1024]{1,0:T(8,128)(2,1)}, bf16[512,1024]{1,0:T(8,128)(2,1)}, f32[2,512,1024]{2,1,0:T(8,128)}) custom-call(bf16[512,1024]{1,0:T(8,128)(2,1)} %q_ref.5, bf16[512,1024]{1,0:T(8,128)(2,1)} %k_ref.5, bf16[512,1024]{1,0:T(8,128)(2,1)} %v_ref.5, bf16[8,512,1024]{2,1,0:T(8,128)(2,1)} %get-tuple-element.33.weights_ref, ...), custom_call_target="tpu_custom_call" | custom-call | tf_op jit(solution)/shard_map/diag_backward/pallas_call | solution.py:547
  138.4 4.7 %all-to-all-done.1.back_ref = bf16[32,40,1024]{2,1,0:T(8,128)(2,1)S(1)} async-done(((bf16[32,40,1024]{2,1,0:T(8,128)(2,1)}), bf16[32,40,1024]{2,1,0:T(8,128)(2,1)S(1)}, u32[]{:S(2)}, u32[]{:S(2)}) %all-to-all-start.1) | async-done | bytes 2621472 | tf_op jit(solution)/shard_map/all_to_all | solution.py:544
  143.1 0.4 collect.1
  143.5 0.0 copy-start
  143.5 0.6 copy-done
  144.1 0.0 copy-start.1
  144.1 6.2 %collective-permute-start.7 = (f32[8,1024]{1,0:T(8,128)S(1)}, f32[8,1024]{1,0:T(8,128)S(1)}, u32[]{:S(2)}, u32[]{:S(2)}) collective-permute-start(f32[8,1024]{1,0:T(8,128)S(1)} %get-tuple-element.59.top_ref), channel_id=1, source_target_pairs={{0,64},{32,96},{64,0},{96,32},{1,65},{33,97},{65,1},{97,33},{2,66}... | collective-permute-start | bytes 98312 | tf_op jit(solution)/shard_map/ppermute | solution.py:518
  150.3 5.3 %collective-permute-done.5.prev_ref = bf16[2,128,1024]{2,1,0:T(8,128)(2,1)S(1)} collective-permute-done((bf16[2,128,1024]{2,1,0:T(8,128)(2,1)}, bf16[2,128,1024]{2,1,0:T(8,128)(2,1)S(1)}, u32[]{:S(2)}, u32[]{:S(2)}) %collective-permute-start.5) | collective-permute-done | bytes 524320 | tf_op jit(solution)/shard_map/ppermute | solution.py:514
  155.7 0.0 copy-start.4
  155.7 0.0 collective-permute-done.6.next_ref
  155.7 0.0 collective-permute-done.7.swapped_ref
  155.7 0.0 copy-start.5
  155.7 0.0 copy-done.1
  155.7 0.8 copy-done.4
  156.5 0.0 copy-done.5
  156.5 7.8 %finish.1 = (bf16[512,1024]{1,0:T(8,128)(2,1)}, bf16[512,1024]{1,0:T(8,128)(2,1)}) custom-call(f32[2,512,1024]{2,1,0:T(8,128)} %get-tuple-element.52.diag_ref, f32[2,128,1024]{2,1,0:T(8,128)} %get-tuple-element.53.near_pooled_ref, bf16[2,128,1024]{2,1,0:T(8,128)(2,1)} %copy-done.4, bf16[2,128,1024]{2,1,0:T(8,128)(2,1)} %collective-permute-done.6.next_ref, ...), custom_call_target="tpu_custom_call" | custom-call | tf_op jit(solution)/shard_map/finish/pallas_call | solution.py:553
  (3 shorter events, 0.1 us)
Async XLA Ops:
  6.6 5.1 %collective-permute-start.2 = (bf16[2,2,1024]{2,1,0:T(2,128)(2,1)}, bf16[2,2,1024]{2,1,0:T(2,128)(2,1)S(1)}, u32[]{:S(2)}, u32[]{:S(2)}) collective-permute-start(bf16[2,2,1024]{2,1,0:T(2,128)(2,1)} %get-tuple-element.36), channel_id=1, source_target_pairs={{0,64},{32,96},{64,0},{96,32},{1,65},{33,97},{65,1},{97,33},{2,66}... | collective-permute-start | bytes 24584 | tf_op jit(solution)/shard_map/ppermute | solution.py:518
  13.3 39.9 %all-to-all-start = ((bf16[32,40,1024]{2,1,0:T(8,128)(2,1)}), bf16[32,40,1024]{2,1,0:T(8,128)(2,1)S(1)}, u32[]{:S(2)}, u32[]{:S(2)}) async-start(bf16[32,40,1024]{2,1,0:T(8,128)(2,1)} %broadcast_dynamic-update-slice_fusion), calls=%async_computation | async-start | bytes 5242880 | tf_op jit(solution)/shard_map/all_to_all | solution.py:531
  22.2 42.2 %collective-permute-start.1 = (bf16[2,128,1024]{2,1,0:T(8,128)(2,1)}, bf16[2,128,1024]{2,1,0:T(8,128)(2,1)}, u32[]{:S(2)}, u32[]{:S(2)}) collective-permute-start(bf16[2,128,1024]{2,1,0:T(8,128)(2,1)} %get-tuple-element.34), channel_id=1, source_target_pairs={{1,0},{2,1},{3,2},{4,3},{5,4},{6,5},{7,6},{8,7},{9,8},{10,9},{11,1... | collective-permute-start | bytes 1572872 | tf_op jit(solution)/shard_map/ppermute | solution.py:514
  32.0 36.3 %collective-permute-start = (bf16[2,128,1024]{2,1,0:T(8,128)(2,1)}, bf16[2,128,1024]{2,1,0:T(8,128)(2,1)}, u32[]{:S(2)}, u32[]{:S(2)}) collective-permute-start(bf16[2,128,1024]{2,1,0:T(8,128)(2,1)} %get-tuple-element.34), channel_id=1, source_target_pairs={{0,1},{1,2},{2,3},{3,4},{4,5},{5,6},{6,7},{7,8},{8,9},{9,10},{10,1... | collective-permute-start | bytes 1572872 | tf_op jit(solution)/shard_map/ppermute | solution.py:514
  53.2 15.0 %copy-start.2 = (bf16[32,40,1024]{2,1,0:T(8,128)(2,1)}, bf16[32,40,1024]{2,1,0:T(8,128)(2,1)S(1)}, u32[]{:S(2)}) copy-start(bf16[32,40,1024]{2,1,0:T(8,128)(2,1)S(1)} %all-to-all-done.group_ref) | copy-start | bytes 7864324
  53.3 15.0 %copy-start.3 = (bf16[32,8,1024]{2,1,0:T(8,128)(2,1)}, bf16[32,8,1024]{2,1,0:T(8,128)(2,1)S(1)}, u32[]{:S(2)}) copy-start(bf16[32,8,1024]{2,1,0:T(8,128)(2,1)S(1)} %slice.3.mine_ref) | copy-start | bytes 1572868
  53.3 15.0 %collective-permute-start.3 = (bf16[32,8,1024]{2,1,0:T(8,128)(2,1)S(1)}, bf16[32,8,1024]{2,1,0:T(8,128)(2,1)}, u32[]{:S(2)}, u32[]{:S(2)}) collective-permute-start(bf16[32,8,1024]{2,1,0:T(8,128)(2,1)S(1)} %slice.3.mine_ref), channel_id=1, source_target_pairs={{0,32},{32,0},{64,96},{96,64},{1,33},{33,1},{65,97},{97,65},{2,34}... | collective-permute-start | bytes 1572872 | tf_op jit(solution)/shard_map/ppermute | solution.py:518
  99.6 2.2 %collective-permute-start.4 = (bf16[32,8,1024]{2,1,0:T(8,128)(2,1)}, bf16[32,8,1024]{2,1,0:T(8,128)(2,1)S(1)}, u32[]{:S(2)}, u32[]{:S(2)}) collective-permute-start(bf16[32,8,1024]{2,1,0:T(8,128)(2,1)} %get-tuple-element.50), channel_id=1, source_target_pairs={{0,32},{32,0},{64,96},{96,64},{1,33},{33,1},{65,97},{97,65},{2,34}... | collective-permute-start | bytes 1572872 | tf_op jit(solution)/shard_map/ppermute | solution.py:518
  103.9 39.2 %all-to-all-start.1 = ((bf16[32,40,1024]{2,1,0:T(8,128)(2,1)}), bf16[32,40,1024]{2,1,0:T(8,128)(2,1)S(1)}, u32[]{:S(2)}, u32[]{:S(2)}) async-start(bf16[32,40,1024]{2,1,0:T(8,128)(2,1)} %fusion), calls=%async_computation.1 | async-start | bytes 5242880 | tf_op jit(solution)/shard_map/all_to_all | solution.py:544
  109.8 45.9 %collective-permute-start.5 = (bf16[2,128,1024]{2,1,0:T(8,128)(2,1)}, bf16[2,128,1024]{2,1,0:T(8,128)(2,1)S(1)}, u32[]{:S(2)}, u32[]{:S(2)}) collective-permute-start(bf16[2,128,1024]{2,1,0:T(8,128)(2,1)} %get-tuple-element.54), channel_id=1, source_target_pairs={{0,1},{1,2},{2,3},{3,4},{4,5},{5,6},{6,7},{7,8},{8,9},{9,10},{10,1... | collective-permute-start | bytes 1572872 | tf_op jit(solution)/shard_map/ppermute | solution.py:514
  112.9 42.8 %collective-permute-start.6 = (bf16[2,128,1024]{2,1,0:T(8,128)(2,1)}, bf16[2,128,1024]{2,1,0:T(8,128)(2,1)}, u32[]{:S(2)}, u32[]{:S(2)}) collective-permute-start(bf16[2,128,1024]{2,1,0:T(8,128)(2,1)} %get-tuple-element.55), channel_id=1, source_target_pairs={{1,0},{2,1},{3,2},{4,3},{5,4},{6,5},{7,6},{8,7},{9,8},{10,9},{11,1... | collective-permute-start | bytes 1572872 | tf_op jit(solution)/shard_map/ppermute | solution.py:514
  143.5 0.7 copy-start
  144.1 11.6 %copy-start.1 = (f32[8,1024]{1,0:T(8,128)}, f32[8,1024]{1,0:T(8,128)S(1)}, u32[]{:S(2)}) copy-start(f32[8,1024]{1,0:T(8,128)S(1)} %get-tuple-element.59.top_ref) | copy-start | bytes 98308
  144.1 11.5 %collective-permute-start.7 = (f32[8,1024]{1,0:T(8,128)S(1)}, f32[8,1024]{1,0:T(8,128)S(1)}, u32[]{:S(2)}, u32[]{:S(2)}) collective-permute-start(f32[8,1024]{1,0:T(8,128)S(1)} %get-tuple-element.59.top_ref), channel_id=1, source_target_pairs={{0,64},{32,96},{64,0},{96,32},{1,65},{33,97},{65,1},{97,33},{2,66}... | collective-permute-start | bytes 98312 | tf_op jit(solution)/shard_map/ppermute | solution.py:518
  155.7 0.8 copy-start.4
  155.7 0.8 copy-start.5

commit v3 on v2

--- a/solution.py
+++ b/solution.py
@@ -28,6 +28,7 @@
 ROWS = 128
 TILES = BLOCK // ROWS
 UNROLL = 2
+LAG = 8
 SOFT = 1.0 / math.sqrt(HD)
 
 EPS = 1e-06
@@ -40,6 +41,10 @@
 
 def dot(a, b):
     return jnp.dot(a, b, preferred_element_type=F32)
+
+
+def dot_rows(a, b):
+    return lax.dot_general(a, b, (((1,), (1,)), ((), ())), preferred_element_type=F32)
 
 
 def pieces(x, count):
@@ -63,7 +68,7 @@
     return jnp.where(row // factor == col, 1.0, 0.0).astype(BF16)
 
 
-def head_means(*xs):
+def head_means(count_pieces, *xs):
     width = 256
     row = lax.broadcasted_iota(jnp.int32, (width, width), 0)
     col = lax.broadcasted_iota(jnp.int32, (width, width), 1)
@@ -71,8 +76,8 @@
     stack = [x[:, start : start + width] for x in xs for start in range(0, D, width)]
     stack = jnp.concatenate(stack, axis=0)
     count = stack.shape[0]
-    found = dot(jnp.concatenate(pieces(stack, 3), axis=0), same)
-    found = found[:count] + found[count : 2 * count] + found[2 * count :]
+    found = dot(jnp.concatenate(pieces(stack, count_pieces), axis=0), same)
+    found = sum(found[at : at + count] for at in range(0, count_pieces * count, count))
     means, at = [], 0
     for x in xs:
         rows = x.shape[0]
@@ -83,12 +88,12 @@
 
 
 def normalize(*pooled):
-    means = head_means(*[x * x for x in pooled])
+    means = head_means(3, *[x * x for x in pooled])
     return [x * lax.rsqrt(mean + EPS) for x, mean in zip(pooled, means)]
 
 
 def normalize_back(pooled, upstream):
-    means = head_means(*[x * x for x in pooled], *[x * up for x, up in zip(pooled, upstream)])
+    means = head_means(2, *[x * x for x in pooled], *[x * up for x, up in zip(pooled, upstream)])
     back = []
     for x, up, mean, inner in zip(pooled, upstream, means, means[len(pooled) :]):
         scale = lax.rsqrt(mean + EPS)
@@ -100,18 +105,10 @@
     return jnp.mean(rows.astype(F32).reshape(rows.shape[0] // RATIO, RATIO, rows.shape[1]), axis=1)
 
 
-def summaries_kernel(
-    k_ref, v_ref, near_ref, near_pooled_ref, top_ref, pooled_ref, payload_ref, groups
-):
+def group_kernel(k_ref, v_ref, payload_ref, top_ref, pooled_ref, groups):
     tile = pl.program_id(0)
-    pooled = []
     for index, ref in enumerate((k_ref, v_ref)):
-        rows = ref[...]
-        pooled.append(dot(pool_matrix(ROWS // P1, ROWS, P1), rows) * (1.0 / P1))
-        near_pooled_ref[index] = pooled[index]
-        groups[index, tile] = dot(pool_matrix(8, ROWS, P2), rows) * (1.0 / P2)
-    for index, near in enumerate(normalize(*pooled)):
-        near_ref[index] = near.astype(BF16)
+        groups[index, tile] = dot(pool_matrix(8, ROWS, P2), ref[...]) * (1.0 / P2)
 
     @pl.when(tile == TILES - 1)
     def _():
@@ -129,6 +126,15 @@
             top_ref[index] = top.astype(BF16)
 
 
+def near_kernel(k_ref, v_ref, near_ref, near_pooled_ref):
+    pooled = []
+    for index, ref in enumerate((k_ref, v_ref)):
+        pooled.append(dot(pool_matrix(ROWS // P1, ROWS, P1), ref[...]) * (1.0 / P1))
+        near_pooled_ref[index] = pooled[index]
+    for index, near in enumerate(normalize(*pooled)):
+        near_ref[index] = near.astype(BF16)
+
+
 def collect_kernel(back_ref, up_ref, top_ref):
     up_ref[...] = jnp.sum(back_ref[:, : 2 * OWN].astype(F32), axis=0).reshape(2, OWN, D)
     top_ref[...] = jnp.sum(back_ref[:, 2 * OWN :].astype(F32), axis=0)
@@ -157,11 +163,12 @@
 
     count = ROWS // P1
     near_up = [prev_ref[index].astype(F32) + next_ref[index].astype(F32) for index in range(2)]
+    over = spread_matrix(ROWS, count, P1)
+    over = jnp.concatenate([over, over], axis=1)
     near_back = normalize_back([near_pooled_ref[0], near_pooled_ref[1]], near_up)
     for index, out_ref in enumerate((dk_ref, dv_ref)):
-        total = diag_ref[index]
-        for part in pieces(near_back[index] * (1.0 / P1), 2):
-            total = total + dot(spread_matrix(ROWS, count, P1), part)
+        both = jnp.concatenate(pieces(near_back[index] * (1.0 / P1), 2), axis=0)
+        total = diag_ref[index] + dot(over, both)
         for place in range(ROWS // P2):
             cut = slice(place * P2, place * P2 + P2)
             row = spread[index, pl.ds(tile * (ROWS // P2) + place, 1)]
@@ -202,42 +209,50 @@
     return jnp.concatenate([jnp.where(lane < HD, x, zero), jnp.where(lane < HD, zero, x)], axis=0)
 
 
-def forward(q_t, kcat, v_t, scores, weights, bias):
-    count = kcat.shape[0]
-    q_both = apart(q_t)
-    largest = None
-    for start in starts(count):
-        part = dot(kcat[start : start + CHUNK], q_both)
-        if start in bias:
-            part = part + bias[start]
-        scores[start : start + CHUNK] = part
-        part = jnp.max(part.reshape(CHUNK // 8, 8, BOTH), axis=0)
-        largest = part if largest is None else jnp.maximum(largest, part)
-    largest = jnp.max(largest, axis=0, keepdims=True)
-    for start in starts(count):
-        part = (scores[start : start + CHUNK] - largest) * (LOG2E * SOFT)
-        weights[start : start + CHUNK] = jnp.exp2(part).astype(BF16)
-    found = dot(jnp.concatenate([v_t, jnp.ones((16, count), BF16)], axis=0), weights[...])
-    return largest, found[PAIR : PAIR + 1], together(found)
-
-
-def score_grads(scaled, delta, vones, weights, sgrad):
+def score_step(start, q_rows, kcat, scores, bias, largest):
+    part = dot_rows(kcat[start : start + CHUNK], q_rows)
+    if start in bias:
+        part = part + bias[start]
+    scores[start : start + CHUNK] = part
+    part = jnp.max(part.reshape(CHUNK // 8, 8, BOTH), axis=0)
+    return part if largest is None else jnp.maximum(largest, part)
+
+
+def weight_step(start, scores, weights, largest):
+    part = (scores[start : start + CHUNK] - largest) * (LOG2E * SOFT)
+    weights[start : start + CHUNK] = jnp.exp2(part).astype(BF16)
+
+
+def value_step(v_t, weights):
+    found = dot(jnp.concatenate([v_t, jnp.ones((16, v_t.shape[1]), BF16)], axis=0), weights[...])
+    return found[PAIR : PAIR + 1], together(found)
+
+
+def grads_and_delta(scaled, delta):
     row = lax.broadcasted_iota(jnp.int32, (16, BOTH), 0)
     extra = jnp.zeros((16, BOTH), F32)
     for place, piece in enumerate(pieces(-delta, 3)):
         extra = jnp.where(row == place, piece.astype(F32), extra)
     zero = jnp.zeros((PAIR - 16, BOTH), BF16)
-    g_both = jnp.concatenate([apart(scaled), extra.astype(BF16), zero], axis=0)
-    for start in starts(vones.shape[0]):
-        cut = slice(start, start + CHUNK)
-        part = dot(vones[cut], g_both)
-        sgrad[cut] = (part * weights[cut].astype(F32)).astype(BF16)
-
-
-def diag_kernel(q_ref, k_ref, v_ref, weights_ref, sum_ref, stats_ref, scores):
-    largest, total, summed = forward(
-        q_ref[...].T, k_ref, v_ref[...].T, scores, weights_ref.at[0], {}
-    )
+    return jnp.concatenate([apart(scaled), extra.astype(BF16), zero], axis=0)
+
+
+def grad_step(start, g_both, vones, weights, sgrad):
+    cut = slice(start, start + CHUNK)
+    part = dot(vones[cut], g_both)
+    sgrad[cut] = (part * weights[cut].astype(F32)).astype(BF16)
+
+
+def diag_kernel(q_ref, k_ref, v_ref, g_ref, weights_ref, sum_ref, stats_ref, g_t_ref, scores):
+    g_t_ref[...] = g_ref[...].T
+    q_rows = head_rows(q_ref[...])
+    largest = None
+    for start in starts(BLOCK):
+        largest = score_step(start, q_rows, k_ref, scores, {}, largest)
+    largest = jnp.max(largest, axis=0, keepdims=True)
+    for start in starts(BLOCK):
+        weight_step(start, scores, weights_ref.at[0], largest)
+    total, summed = value_step(v_ref[...].T, weights_ref.at[0])
     stats_ref[0, 0:1] = largest
     stats_ref[0, 1:2] = total
     sum_ref[...] = summed
@@ -279,10 +294,11 @@
     def _():
         vones[:, :, PAIR:] = jnp.ones((UNROLL, WIDE, PAIR), BF16)
 
+    running = []
     for p in range(UNROLL):
         lanes = slice(p * PAIR, p * PAIR + PAIR)
-        wide_pair(
-            bias, q_ref.at[:, lanes], g_ref.at[:, lanes],
+        running.append(wide_pair(
+            bias, q_ref.at[:, lanes], g_ref.at[lanes],
             before_ref.at[:, :, lanes], after_ref.at[:, :, lanes],
             sum_ref.at[lanes], stats_ref.at[p], group_ref.at[:, :, lanes],
             split_top(mine_ref, lanes), split_top(other_ref, lanes),
@@ -291,7 +307,18 @@
             dgroup_ref.at[:, :, lanes], dmine_ref.at[:, :, lanes], dother_ref.at[:, :, lanes],
             dbefore_ref.at[:, :, lanes], dafter_ref.at[:, :, lanes],
             vones.at[p], scores.at[p], weights.at[p],
-        )
+        ))
+    staggered(running, LAG)
+
+
+def staggered(running, lag):
+    tick, left = 0, list(enumerate(running))
+    while left:
+        for item in list(left):
+            index, steps = item
+            if tick >= index * lag and next(steps, None) is None:
+                left.remove(item)
+        tick += 1
 
 
 def wide_pair(
@@ -308,10 +335,17 @@
     for start, ref in ((GROUP + TOP, before_ref), (GROUP + TOP + NEAR, after_ref)):
         kcat[start : start + NEAR] = ref[0]
         vones[start : start + NEAR, :PAIR] = ref[1]
-    queries = q_ref[...]
-    largest, total, summed = forward(
-        queries.T, kcat, vones[:, :PAIR].T, scores, weights, bias
-    )
+    q_rows = head_rows(q_ref[...])
+    largest = None
+    for start in starts(WIDE):
+        largest = score_step(start, q_rows, kcat, scores, bias, largest)
+        yield True
+    largest = jnp.max(largest, axis=0, keepdims=True)
+    for start in starts(WIDE):
+        weight_step(start, scores, weights, largest)
+        yield True
+    total, summed = value_step(vones[:, :PAIR].T, weights)
+    yield True
     local_largest, local_total = stats_ref[0:1], stats_ref[1:2]
     most = jnp.maximum(largest, local_largest)
     share = jnp.exp2((largest - most) * (LOG2E * SOFT))
@@ -321,13 +355,16 @@
     local_share = by_head(local_share * inverse)
     attended = share * summed + local_share * sum_ref[...]
     out_ref[...] = attended.astype(BF16)
-    grad = g_ref[...].T.astype(F32)
+    grad = g_ref[...].astype(F32)
     local_scaled = (grad * local_share).astype(BF16)
     scaled_ref[...] = local_scaled
     delta_ref[0:1] = head_sums(local_scaled.astype(F32) * attended)
     scaled = (grad * share).astype(BF16)
-    score_grads(scaled, head_sums(scaled.astype(F32) * attended), vones, weights, sgrad)
-    q_rows = head_rows(queries)
+    g_both = grads_and_delta(scaled, head_sums(scaled.astype(F32) * attended))
+    yield True
+    for start in starts(WIDE):
+        grad_step(start, g_both, vones, weights, sgrad)
+        yield True
     g_rows = head_rows(scaled.T)
     for start in starts(WIDE):
         cut = slice(start, start + CHUNK)
@@ -346,6 +383,7 @@
             for index, value in enumerate((dk, dv)):
                 dbefore_ref[index] = value[:NEAR].astype(BF16)
                 dafter_ref[index] = value[NEAR:].astype(BF16)
+        yield True
 
 
 def diag_back_kernel(
@@ -360,7 +398,9 @@
     out_ref[...] = out_t_ref[...].T
     weights = weights_ref.at[0]
     scaled = scaled_ref[...]
-    score_grads(scaled, delta_ref[0, 0:1], vones, weights, sgrad)
+    g_both = grads_and_delta(scaled, delta_ref[0, 0:1])
+    for start in starts(BLOCK):
+        grad_step(start, g_both, vones, weights, sgrad)
     dq = dot(kcat_ref[0].T, wide_ref[0]) + dot(k_ref[...].T, sgrad[...])
     dq_ref[...] = (together(dq).T * SOFT).astype(BF16)
     q_rows = head_rows(q_ref[...])
@@ -413,32 +453,38 @@
     )
 
 
-summaries = call(
-    summaries_kernel,
-    "summaries",
+group_summaries = call(
+    group_kernel,
+    "group_summaries",
     TILES,
     [on_rows(ROWS, D)] * 2,
-    [on_middle(2, ROWS // P1, D)] * 2
-    + [every(2, OWN // RATIO, D), every(2, OWN, D), every(N_SEQ, 2 * OWN, D)],
+    [every(N_SEQ, 2 * OWN, D), every(2, OWN // RATIO, D), every(2, OWN, D)],
     (
-        shape_of(BF16, 2, NEAR, D),
-        shape_of(F32, 2, NEAR, D),
+        shape_of(BF16, N_SEQ, SENT, D),
         shape_of(BF16, 2, OWN // RATIO, D),
         shape_of(F32, 2, OWN, D),
-        shape_of(BF16, N_SEQ, SENT, D),
     ),
     [pltpu.VMEM((2, TILES, 8, D), F32)],
+)
+near_summaries = call(
+    near_kernel,
+    "near_summaries",
+    TILES,
+    [on_rows(ROWS, D)] * 2,
+    [on_middle(2, ROWS // P1, D)] * 2,
+    (shape_of(BF16, 2, NEAR, D), shape_of(F32, 2, NEAR, D)),
 )
 diag_forward = call(
     diag_kernel,
     "diag_forward",
     PAIRS,
-    [SEQUENCE] * 3,
-    [DIAG, COLUMNS, STATS],
+    [SEQUENCE] * 4,
+    [DIAG, COLUMNS, STATS, COLUMNS],
     (
         shape_of(BF16, PAIRS, BLOCK, BOTH),
         shape_of(F32, D, BLOCK),
         shape_of(F32, PAIRS, 8, BOTH),
+        shape_of(BF16, D, BLOCK),
     ),
     [pltpu.VMEM((BLOCK, BOTH), F32)],
 )
@@ -451,7 +497,7 @@
     "wide_attend",
     PAIRS // UNROLL,
     [SMEM]
-    + [wide_lanes(BLOCK)] * 2
+    + [wide_lanes(BLOCK), on_rows(UNROLL * PAIR, BLOCK)]
     + [wide_lanes(2, NEAR)] * 2
     + [on_rows(UNROLL * PAIR, BLOCK), on_rows(UNROLL, 8, BOTH)]
     + [wide_lanes(N_SEQ, 2 * OWN)]
@@ -470,9 +516,8 @@
         shape_of(BF16, N_SEQ, SENT, D),
         shape_of(BF16, N_SEQ, 8, D),
         shape_of(BF16, N_SEQ, 8, D),
-        shape_of(BF16, 2, NEAR, D),
-        shape_of(BF16, 2, NEAR, D),
-    ),
+    )
+    + (shape_of(BF16, 2, NEAR, D),) * 2,
     [
         pltpu.VMEM((UNROLL, WIDE, 2 * PAIR), BF16),
         pltpu.VMEM((UNROLL, WIDE, BOTH), F32),
@@ -524,19 +569,22 @@
     live = jnp.stack(
         [jnp.where(device == 0, NEG, 0.0), jnp.where(device == count - 1, NEG, 0.0)]
     ).astype(F32)
-    near, near_pooled, top, pooled, payload = summaries(keys, values)
-    top_pair = jnp.stack([top, grp_swap(top, 2)], axis=1).reshape(8, D)
+    payload, top, pooled = group_summaries(keys, values)
+    swapped = grp_swap(top, 2)
+    near, near_pooled = near_summaries(keys, values)
+    near, live = lax.optimization_barrier((near, live))
+    top_pair = jnp.stack([top, swapped], axis=1).reshape(8, D)
     tops = jnp.broadcast_to(top_pair[None], (N_SEQ, 8, D))
     payload = lax.dynamic_update_slice(payload, tops, (0, 2 * OWN, 0))
     everyone = lax.all_to_all(payload, "seq", 0, 0, tiled=True)
     before = shifted(near, 1)
     after = shifted(near, -1)
-    diag_weights, diag_sum, diag_stats = diag_forward(queries, keys, values)
+    diag_weights, diag_sum, diag_stats, grad_t = diag_forward(queries, keys, values, out_grad)
     everyone, diag_sum = lax.optimization_barrier((everyone, diag_sum))
     top_mine = everyone[:, 2 * OWN :]
     top_other = grp_swap(top_mine, 1)
     out_t, scaled, delta, kcat, sgrad, back, dmine, dother, dbefore, dafter = wide_attend(
-        live, queries, out_grad, before, after, diag_sum, diag_stats,
+        live, queries, grad_t, before, after, diag_sum, diag_stats,
         everyone, top_mine, top_other,
     )
     dmine = (dmine.astype(F32) + grp_swap(dother, 1).astype(F32)).astype(BF16)

time: 167 us -> 161 us (0.964)
  waiting for transfers between devices: 30.7 us -> 26 us
    all_to_all x1, waiting for transfers between devices: 7.82 us -> 2.63 us  [per_device(): everyone = lax.all_to_all(payload, 'seq', 0, 0, tiled=True)]
    pallas_call x3 -> x4, Pallas kernels: 48.8 us -> 48.7 us  [the longest x1 28 us: per_device(): wide_attend(live, queries, grad_t, before, after, diag_sum, diag_stats, e...]
  transfers between devices with their start and end apart: 10 -> 10, of which waited for: 7 -> 7; matrix products, arithmetic and copies ran while one was open for 0% -> 0% of each run, Pallas kernels for 18% -> 22%
where the time goes in v3:
time: 161 us; the launch traced here: 159 us
  Pallas kernels  74 us (46%)
  starting transfers between devices  51.6 us (32%)
  waiting for transfers between devices  26 us (16%)
  other arithmetic  3.42 us (2%)
  local copies, waits for them, and re-layouts  3.13 us (2%)
    pallas_call x1, Pallas kernels, per_device(): wide_attend(live, queries, grad_t, before, after, diag_sum, diag_stats, e...  28 us
    ppermute x4, starting transfers between devices, shifted(): return lax.ppermute(block, ('grp', 'seq'), route)  22 us
    pallas_call x1, Pallas kernels, per_device(): diag_backward(queries, keys, values, diag_weights, out_t, scaled, delta,...  18.2 us
    ppermute x4, waiting for transfers between devices, shifted(): return lax.ppermute(block, ('grp', 'seq'), route)  15.3 us
    ppermute x4, starting transfers between devices, grp_swap(): return lax.ppermute(block, 'grp', [(i, i ^ bit) for i in range(4)])  15.1 us
    pallas_call x1, Pallas kernels, per_device(): diag_forward(queries, keys, values, out_grad)  11.5 us
    all_to_all x1, starting transfers between devices, per_device(): everyone = lax.all_to_all(payload, 'seq', 0, 0, tiled=True)  8.95 us
    pallas_call x1, Pallas kernels, per_device(): finish(diag, near_pooled, from_prev, from_next, pooled, group_up, top_up,...  6.78 us
  transfers between devices with their start and end apart: 10, of which 7 were waited for; matrix products, arithmetic and copies ran while one was open for 0% of the time, Pallas kernels for 22%

profile of v3, /device:TPU:1, one launch (start us, length us, event | category | flops | bytes accessed | tf_op | source)
XLA Modules:
  0.0 159.0 jit_solution(5923253090459310348)
XLA Ops:
  0.6 4.6 %group_summaries.1 = (bf16[32,40,1024]{2,1,0:T(8,128)(2,1)}, bf16[2,2,1024]{2,1,0:T(2,128)(2,1)}, f32[2,16,1024]{2,1,0:T(8,128)}) custom-call(bf16[512,1024]{1,0:T(8,128)(2,1)} %k_ref.7, bf16[512,1024]{1,0:T(8,128)(2,1)} %v_ref.7), custom_call_target="tpu_custom_call" | custom-call | tf_op jit(solution)/shard_map/group_summaries/pallas_call | solution.py:572
  5.3 3.7 %collective-permute-start.2 = (bf16[2,2,1024]{2,1,0:T(2,128)(2,1)}, bf16[2,2,1024]{2,1,0:T(2,128)(2,1)S(1)}, u32[]{:S(2)}, u32[]{:S(2)}) collective-permute-start(bf16[2,2,1024]{2,1,0:T(2,128)(2,1)} %get-tuple-element.42), channel_id=1, source_target_pairs={{0,64},{32,96},{64,0},{96,32},{1,65},{33,97},{65,1},{97,33},{2,66}... | collective-permute-start | bytes 24584 | tf_op jit(solution)/shard_map/ppermute | solution.py:563
  9.0 1.2 collective-permute-done.2
  10.3 0.7 pad_maximum_fusion
  11.0 0.9 broadcast_dynamic-update-slice_fusion
  11.9 8.9 %all-to-all-start = ((bf16[32,40,1024]{2,1,0:T(8,128)(2,1)}), bf16[32,40,1024]{2,1,0:T(8,128)(2,1)S(1)}, u32[]{:S(2)}, u32[]{:S(2)}) async-start(bf16[32,40,1024]{2,1,0:T(8,128)(2,1)} %broadcast_dynamic-update-slice_fusion), calls=%async_computation | async-start | bytes 5242880 | tf_op jit(solution)/shard_map/all_to_all | solution.py:579
  20.8 4.5 %near_summaries.1 = (bf16[2,128,1024]{2,1,0:T(8,128)(2,1)}, f32[2,128,1024]{2,1,0:T(8,128)}) custom-call(bf16[512,1024]{1,0:T(8,128)(2,1)} %k_ref.7, bf16[512,1024]{1,0:T(8,128)(2,1)} %v_ref.7), custom_call_target="tpu_custom_call" | custom-call | tf_op jit(solution)/shard_map/near_summaries/pallas_call | solution.py:574
  25.3 0.7 pad_maximum_fusion.1.live_ref
  26.0 9.7 %collective-permute-start.1 = (bf16[2,128,1024]{2,1,0:T(8,128)(2,1)}, bf16[2,128,1024]{2,1,0:T(8,128)(2,1)S(1)}, u32[]{:S(2)}, u32[]{:S(2)}) collective-permute-start(bf16[2,128,1024]{2,1,0:T(8,128)(2,1)} %get-tuple-element.40), channel_id=1, source_target_pairs={{1,0},{2,1},{3,2},{4,3},{5,4},{6,5},{7,6},{8,7},{9,8},{10,9},{11,1... | collective-permute-start | bytes 1572872 | tf_op jit(solution)/shard_map/ppermute | solution.py:559
  35.7 1.9 %collective-permute-start = (bf16[2,128,1024]{2,1,0:T(8,128)(2,1)}, bf16[2,128,1024]{2,1,0:T(8,128)(2,1)}, u32[]{:S(2)}, u32[]{:S(2)}) collective-permute-start(bf16[2,128,1024]{2,1,0:T(8,128)(2,1)} %get-tuple-element.40), channel_id=1, source_target_pairs={{0,1},{1,2},{2,3},{3,4},{4,5},{5,6},{6,7},{7,8},{8,9},{9,10},{10,1... | collective-permute-start | bytes 1572872 | tf_op jit(solution)/shard_map/ppermute | solution.py:559
  37.6 11.5 %diag_forward.1 = (bf16[8,512,1024]{2,1,0:T(8,128)(2,1)}, f32[1024,512]{1,0:T(8,128)}, f32[8,8,1024]{2,1,0:T(8,128)}, bf16[1024,512]{1,0:T(8,128)(2,1)}) custom-call(bf16[512,1024]{1,0:T(8,128)(2,1)} %q_ref.5, bf16[512,1024]{1,0:T(8,128)(2,1)} %k_ref.7, bf16[512,1024]{1,0:T(8,128)(2,1)} %v_ref.7, bf16[512,1024]{1,0:T(8,128)(2,1)} %g_ref.1), custom_call_target="tpu_custom_call" | custom-call | tf_op jit(solution)/shard_map/diag_forward/pallas_call | solution.py:582
  49.1 2.6 %all-to-all-done.group_ref = bf16[32,40,1024]{2,1,0:T(8,128)(2,1)S(1)} async-done(((bf16[32,40,1024]{2,1,0:T(8,128)(2,1)}), bf16[32,40,1024]{2,1,0:T(8,128)(2,1)S(1)}, u32[]{:S(2)}, u32[]{:S(2)}) %all-to-all-start) | async-done | bytes 2621472 | tf_op jit(solution)/shard_map/all_to_all | solution.py:579
  51.8 0.0 copy-start.2
  51.8 0.0 copy-start.3
  51.8 5.0 %collective-permute-start.3 = (bf16[32,8,1024]{2,1,0:T(8,128)(2,1)S(1)}, bf16[32,8,1024]{2,1,0:T(8,128)(2,1)S(1)}, u32[]{:S(2)}, u32[]{:S(2)}) collective-permute-start(bf16[32,8,1024]{2,1,0:T(8,128)(2,1)S(1)} %slice.3.mine_ref), channel_id=1, source_target_pairs={{0,32},{32,0},{64,96},{96,64},{1,33},{33,1},{65,97},{97,65},{2,34}... | collective-permute-start | bytes 1572872 | tf_op jit(solution)/shard_map/ppermute | solution.py:563
  56.8 6.2 %collective-permute-done.1.after_ref = bf16[2,128,1024]{2,1,0:T(8,128)(2,1)S(1)} collective-permute-done((bf16[2,128,1024]{2,1,0:T(8,128)(2,1)}, bf16[2,128,1024]{2,1,0:T(8,128)(2,1)S(1)}, u32[]{:S(2)}, u32[]{:S(2)}) %collective-permute-start.1) | collective-permute-done | bytes 524320 | tf_op jit(solution)/shard_map/ppermute | solution.py:559
  63.0 0.0 copy-start.5
  63.0 3.8 %collective-permute-done.before_ref = bf16[2,128,1024]{2,1,0:T(8,128)(2,1)} collective-permute-done((bf16[2,128,1024]{2,1,0:T(8,128)(2,1)}, bf16[2,128,1024]{2,1,0:T(8,128)(2,1)}, u32[]{:S(2)}, u32[]{:S(2)}) %collective-permute-start) | collective-permute-done | bytes 524320 | tf_op jit(solution)/shard_map/ppermute | solution.py:559
  66.9 0.0 collective-permute-done.3.other_ref
  66.9 0.0 copy-start.6
  66.9 0.0 copy-done.2
  66.9 0.0 copy-done.3
  66.9 0.0 copy-done.5
  66.9 0.8 copy-done.6
  67.7 28.0 %wide_attend.1 = (bf16[1024,512]{1,0:T(8,128)(2,1)}, bf16[1024,512]{1,0:T(8,128)(2,1)}, f32[8,8,1024]{2,1,0:T(8,128)}, bf16[8,1024,128]{2,1,0:T(8,128)(2,1)}, bf...) custom-call(f32[2]{0:T(128)} %pad_maximum_fusion.1.live_ref, ...), custom_call_target="tpu_custom_call" | custom-call | tf_op jit(solution)/shard_map/wide_attend/pallas_call | solution.py:586
  95.7 0.1 collective-permute-start.4
  95.8 2.1 %collective-permute-done.4 = bf16[32,8,1024]{2,1,0:T(8,128)(2,1)S(1)} collective-permute-done((bf16[32,8,1024]{2,1,0:T(8,128)(2,1)}, bf16[32,8,1024]{2,1,0:T(8,128)(2,1)S(1)}, u32[]{:S(2)}, u32[]{:S(2)}) %collective-permute-start.4) | collective-permute-done | bytes 524320 | tf_op jit(solution)/shard_map/ppermute | solution.py:563
  97.9 2.0 %fusion = bf16[32,40,1024]{2,1,0:T(8,128)(2,1)} fusion(bf16[32,40,1024]{2,1,0:T(8,128)(2,1)} %get-tuple-element.54, bf16[32,8,1024]{2,1,0:T(8,128)(2,1)S(1)} %collective-permute-done.4, bf16[32,8,1024]{2,1,0:T(8,128)(2,1)} %get-tuple-element.55), kind=kLoop, calls=%fused_computation.1 | loop fusion | flops 1048576 | bytes 1572864 | tf_op jit(solution)/shard_map/dynamic_update_slice | solution.py:591
  99.9 5.6 %all-to-all-start.1 = ((bf16[32,40,1024]{2,1,0:T(8,128)(2,1)}), bf16[32,40,1024]{2,1,0:T(8,128)(2,1)S(1)}, u32[]{:S(2)}, u32[]{:S(2)}) async-start(bf16[32,40,1024]{2,1,0:T(8,128)(2,1)} %fusion), calls=%async_computation.1 | async-start | bytes 5242880 | tf_op jit(solution)/shard_map/all_to_all | solution.py:592
  105.5 3.1 %collective-permute-start.5 = (bf16[2,128,1024]{2,1,0:T(8,128)(2,1)}, bf16[2,128,1024]{2,1,0:T(8,128)(2,1)S(1)}, u32[]{:S(2)}, u32[]{:S(2)}) collective-permute-start(bf16[2,128,1024]{2,1,0:T(8,128)(2,1)} %get-tuple-element.60), channel_id=1, source_target_pairs={{0,1},{1,2},{2,3},{3,4},{4,5},{5,6},{6,7},{7,8},{8,9},{9,10},{10,1... | collective-permute-start | bytes 1572872 | tf_op jit(solution)/shard_map/ppermute | solution.py:559
  108.6 7.2 %collective-permute-start.6 = (bf16[2,128,1024]{2,1,0:T(8,128)(2,1)}, bf16[2,128,1024]{2,1,0:T(8,128)(2,1)}, u32[]{:S(2)}, u32[]{:S(2)}) collective-permute-start(bf16[2,128,1024]{2,1,0:T(8,128)(2,1)} %get-tuple-element.61), channel_id=1, source_target_pairs={{1,0},{2,1},{3,2},{4,3},{5,4},{6,5},{7,6},{8,7},{9,8},{10,9},{11,1... | collective-permute-start | bytes 1572872 | tf_op jit(solution)/shard_map/ppermute | solution.py:559
  115.9 18.2 %diag_backward.1 = (bf16[512,1024]{1,0:T(8,128)(2,1)}, bf16[512,1024]{1,0:T(8,128)(2,1)}, f32[2,512,1024]{2,1,0:T(8,128)}) custom-call(bf16[512,1024]{1,0:T(8,128)(2,1)} %q_ref.5, bf16[512,1024]{1,0:T(8,128)(2,1)} %k_ref.7, bf16[512,1024]{1,0:T(8,128)(2,1)} %v_ref.7, bf16[8,512,1024]{2,1,0:T(8,128)(2,1)} %get-tuple-element.36.weights_ref, ...), custom_call_target="tpu_custom_call" | custom-call | tf_op jit(solution)/shard_map/diag_backward/pallas_call | solution.py:595
  134.1 4.8 %all-to-all-done.1.back_ref = bf16[32,40,1024]{2,1,0:T(8,128)(2,1)S(1)} async-done(((bf16[32,40,1024]{2,1,0:T(8,128)(2,1)}), bf16[32,40,1024]{2,1,0:T(8,128)(2,1)S(1)}, u32[]{:S(2)}, u32[]{:S(2)}) %all-to-all-start.1) | async-done | bytes 2621472 | tf_op jit(solution)/shard_map/all_to_all | solution.py:592
  138.9 0.4 collect.1
  139.2 0.0 copy-start
  139.2 0.6 copy-done
  139.9 0.0 copy-start.1
  139.9 6.3 %collective-permute-start.7 = (f32[8,1024]{1,0:T(8,128)S(1)}, f32[8,1024]{1,0:T(8,128)S(1)}, u32[]{:S(2)}, u32[]{:S(2)}) collective-permute-start(f32[8,1024]{1,0:T(8,128)S(1)} %get-tuple-element.65.top_ref), channel_id=1, source_target_pairs={{0,64},{32,96},{64,0},{96,32},{1,65},{33,97},{65,1},{97,33},{2,66}... | collective-permute-start | bytes 98312 | tf_op jit(solution)/shard_map/ppermute | solution.py:563
  146.2 5.2 %collective-permute-done.5.prev_ref = bf16[2,128,1024]{2,1,0:T(8,128)(2,1)S(1)} collective-permute-done((bf16[2,128,1024]{2,1,0:T(8,128)(2,1)}, bf16[2,128,1024]{2,1,0:T(8,128)(2,1)S(1)}, u32[]{:S(2)}, u32[]{:S(2)}) %collective-permute-start.5) | collective-permute-done | bytes 524320 | tf_op jit(solution)/shard_map/ppermute | solution.py:559
  151.4 0.0 copy-start.4
  151.4 0.0 collective-permute-done.6.next_ref
  151.4 0.0 collective-permute-done.7.swapped_ref
  151.4 0.0 copy-start.7
  151.4 0.0 copy-done.1
  151.4 0.8 copy-done.4
  152.2 0.0 copy-done.7
  152.2 6.8 %finish.1 = (bf16[512,1024]{1,0:T(8,128)(2,1)}, bf16[512,1024]{1,0:T(8,128)(2,1)}) custom-call(f32[2,512,1024]{2,1,0:T(8,128)} %get-tuple-element.58.diag_ref, f32[2,128,1024]{2,1,0:T(8,128)} %get-tuple-element.59.near_pooled_ref, bf16[2,128,1024]{2,1,0:T(8,128)(2,1)} %copy-done.4, bf16[2,128,1024]{2,1,0:T(8,128)(2,1)} %collective-permute-done.6.next_ref, ...), custom_call_target="tpu_custom_call" | custom-call | tf_op jit(solution)/shard_map/finish/pallas_call | solution.py:601
  (3 shorter events, 0.1 us)
Async XLA Ops:
  5.3 5.0 %collective-permute-start.2 = (bf16[2,2,1024]{2,1,0:T(2,128)(2,1)}, bf16[2,2,1024]{2,1,0:T(2,128)(2,1)S(1)}, u32[]{:S(2)}, u32[]{:S(2)}) collective-permute-start(bf16[2,2,1024]{2,1,0:T(2,128)(2,1)} %get-tuple-element.42), channel_id=1, source_target_pairs={{0,64},{32,96},{64,0},{96,32},{1,65},{33,97},{65,1},{97,33},{2,66}... | collective-permute-start | bytes 24584 | tf_op jit(solution)/shard_map/ppermute | solution.py:563
  11.9 39.9 %all-to-all-start = ((bf16[32,40,1024]{2,1,0:T(8,128)(2,1)}), bf16[32,40,1024]{2,1,0:T(8,128)(2,1)S(1)}, u32[]{:S(2)}, u32[]{:S(2)}) async-start(bf16[32,40,1024]{2,1,0:T(8,128)(2,1)} %broadcast_dynamic-update-slice_fusion), calls=%async_computation | async-start | bytes 5242880 | tf_op jit(solution)/shard_map/all_to_all | solution.py:579
  26.0 37.1 %collective-permute-start.1 = (bf16[2,128,1024]{2,1,0:T(8,128)(2,1)}, bf16[2,128,1024]{2,1,0:T(8,128)(2,1)S(1)}, u32[]{:S(2)}, u32[]{:S(2)}) collective-permute-start(bf16[2,128,1024]{2,1,0:T(8,128)(2,1)} %get-tuple-element.40), channel_id=1, source_target_pairs={{1,0},{2,1},{3,2},{4,3},{5,4},{6,5},{7,6},{8,7},{9,8},{10,9},{11,1... | collective-permute-start | bytes 1572872 | tf_op jit(solution)/shard_map/ppermute | solution.py:559
  35.7 31.2 %collective-permute-start = (bf16[2,128,1024]{2,1,0:T(8,128)(2,1)}, bf16[2,128,1024]{2,1,0:T(8,128)(2,1)}, u32[]{:S(2)}, u32[]{:S(2)}) collective-permute-start(bf16[2,128,1024]{2,1,0:T(8,128)(2,1)} %get-tuple-element.40), channel_id=1, source_target_pairs={{0,1},{1,2},{2,3},{3,4},{4,5},{5,6},{6,7},{7,8},{8,9},{9,10},{10,1... | collective-permute-start | bytes 1572872 | tf_op jit(solution)/shard_map/ppermute | solution.py:559
  51.8 15.1 %copy-start.2 = (bf16[32,40,1024]{2,1,0:T(8,128)(2,1)}, bf16[32,40,1024]{2,1,0:T(8,128)(2,1)S(1)}, u32[]{:S(2)}) copy-start(bf16[32,40,1024]{2,1,0:T(8,128)(2,1)S(1)} %all-to-all-done.group_ref) | copy-start | bytes 7864324
  51.8 15.1 %copy-start.3 = (bf16[32,8,1024]{2,1,0:T(8,128)(2,1)}, bf16[32,8,1024]{2,1,0:T(8,128)(2,1)S(1)}, u32[]{:S(2)}) copy-start(bf16[32,8,1024]{2,1,0:T(8,128)(2,1)S(1)} %slice.3.mine_ref) | copy-start | bytes 1572868
  51.8 15.0 %collective-permute-start.3 = (bf16[32,8,1024]{2,1,0:T(8,128)(2,1)S(1)}, bf16[32,8,1024]{2,1,0:T(8,128)(2,1)S(1)}, u32[]{:S(2)}, u32[]{:S(2)}) collective-permute-start(bf16[32,8,1024]{2,1,0:T(8,128)(2,1)S(1)} %slice.3.mine_ref), channel_id=1, source_target_pairs={{0,32},{32,0},{64,96},{96,64},{1,33},{33,1},{65,97},{97,65},{2,34}... | collective-permute-start | bytes 1572872 | tf_op jit(solution)/shard_map/ppermute | solution.py:563
  63.0 3.8 %copy-start.5 = (bf16[2,128,1024]{2,1,0:T(8,128)(2,1)}, bf16[2,128,1024]{2,1,0:T(8,128)(2,1)S(1)}, u32[]{:S(2)}) copy-start(bf16[2,128,1024]{2,1,0:T(8,128)(2,1)S(1)} %collective-permute-done.1.after_ref) | copy-start | bytes 1572868
  66.9 0.8 copy-start.6
  95.7 2.2 %collective-permute-start.4 = (bf16[32,8,1024]{2,1,0:T(8,128)(2,1)}, bf16[32,8,1024]{2,1,0:T(8,128)(2,1)S(1)}, u32[]{:S(2)}, u32[]{:S(2)}) collective-permute-start(bf16[32,8,1024]{2,1,0:T(8,128)(2,1)} %get-tuple-element.56), channel_id=1, source_target_pairs={{0,32},{32,0},{64,96},{96,64},{1,33},{33,1},{65,97},{97,65},{2,34}... | collective-permute-start | bytes 1572872 | tf_op jit(solution)/shard_map/ppermute | solution.py:563
  99.9 38.9 %all-to-all-start.1 = ((bf16[32,40,1024]{2,1,0:T(8,128)(2,1)}), bf16[32,40,1024]{2,1,0:T(8,128)(2,1)S(1)}, u32[]{:S(2)}, u32[]{:S(2)}) async-start(bf16[32,40,1024]{2,1,0:T(8,128)(2,1)} %fusion), calls=%async_computation.1 | async-start | bytes 5242880 | tf_op jit(solution)/shard_map/all_to_all | solution.py:592
  105.5 45.9 %collective-permute-start.5 = (bf16[2,128,1024]{2,1,0:T(8,128)(2,1)}, bf16[2,128,1024]{2,1,0:T(8,128)(2,1)S(1)}, u32[]{:S(2)}, u32[]{:S(2)}) collective-permute-start(bf16[2,128,1024]{2,1,0:T(8,128)(2,1)} %get-tuple-element.60), channel_id=1, source_target_pairs={{0,1},{1,2},{2,3},{3,4},{4,5},{5,6},{6,7},{7,8},{8,9},{9,10},{10,1... | collective-permute-start | bytes 1572872 | tf_op jit(solution)/shard_map/ppermute | solution.py:559
  108.6 42.8 %collective-permute-start.6 = (bf16[2,128,1024]{2,1,0:T(8,128)(2,1)}, bf16[2,128,1024]{2,1,0:T(8,128)(2,1)}, u32[]{:S(2)}, u32[]{:S(2)}) collective-permute-start(bf16[2,128,1024]{2,1,0:T(8,128)(2,1)} %get-tuple-element.61), channel_id=1, source_target_pairs={{1,0},{2,1},{3,2},{4,3},{5,4},{6,5},{7,6},{8,7},{9,8},{10,9},{11,1... | collective-permute-start | bytes 1572872 | tf_op jit(solution)/shard_map/ppermute | solution.py:559
  139.2 0.6 copy-start
  139.9 11.6 %copy-start.1 = (f32[8,1024]{1,0:T(8,128)}, f32[8,1024]{1,0:T(8,128)S(1)}, u32[]{:S(2)}) copy-start(f32[8,1024]{1,0:T(8,128)S(1)} %get-tuple-element.65.top_ref) | copy-start | bytes 98308
  139.9 11.6 %collective-permute-start.7 = (f32[8,1024]{1,0:T(8,128)S(1)}, f32[8,1024]{1,0:T(8,128)S(1)}, u32[]{:S(2)}, u32[]{:S(2)}) collective-permute-start(f32[8,1024]{1,0:T(8,128)S(1)} %get-tuple-element.65.top_ref), channel_id=1, source_target_pairs={{0,64},{32,96},{64,0},{96,32},{1,65},{33,97},{65,1},{97,33},{2,66}... | collective-permute-start | bytes 98312 | tf_op jit(solution)/shard_map/ppermute | solution.py:563
  151.4 0.8 copy-start.4
  151.4 0.8 copy-start.7

commit v4 on v3

--- a/solution.py
+++ b/solution.py
@@ -1,3 +1,4 @@
+import functools
 import math
 
 import jax
@@ -28,6 +29,9 @@
 ROWS = 128
 TILES = BLOCK // ROWS
 UNROLL = 2
+PARTS = 2
+LANES = D // PARTS
+PART_STEPS = PAIRS // PARTS // UNROLL
 LAG = 8
 SOFT = 1.0 / math.sqrt(HD)
 
@@ -105,7 +109,8 @@
     return jnp.mean(rows.astype(F32).reshape(rows.shape[0] // RATIO, RATIO, rows.shape[1]), axis=1)
 
 
-def group_kernel(k_ref, v_ref, payload_ref, top_ref, pooled_ref, groups):
+def group_kernel(k_ref, v_ref, top_ref, pooled_ref, *rest):
+    payloads, groups = rest[:PARTS], rest[PARTS]
     tile = pl.program_id(0)
     for index, ref in enumerate((k_ref, v_ref)):
         groups[index, tile] = dot(pool_matrix(8, ROWS, P2), ref[...]) * (1.0 / P2)
@@ -119,9 +124,11 @@
             pooled_ref[index] = pooled[index]
         low = [group.astype(BF16) for group in normalize(*pooled)]
         for index, group in enumerate(low):
-            payload_ref[:, index * OWN : index * OWN + OWN] = jnp.broadcast_to(
-                group[None], (N_SEQ, OWN, D)
-            )
+            for part, payload_ref in enumerate(payloads):
+                lanes = slice(part * LANES, part * LANES + LANES)
+                payload_ref[:, index * OWN : index * OWN + OWN] = jnp.broadcast_to(
+                    group[None, :, lanes], (N_SEQ, OWN, LANES)
+                )
         for index, top in enumerate(normalize(*[top_pool(group) for group in low])):
             top_ref[index] = top.astype(BF16)
 
@@ -135,9 +142,13 @@
         near_ref[index] = near.astype(BF16)
 
 
-def collect_kernel(back_ref, up_ref, top_ref):
-    up_ref[...] = jnp.sum(back_ref[:, : 2 * OWN].astype(F32), axis=0).reshape(2, OWN, D)
-    top_ref[...] = jnp.sum(back_ref[:, 2 * OWN :].astype(F32), axis=0)
+def collect_kernel(*refs):
+    backs, (up_ref, top_ref) = refs[:PARTS], refs[PARTS:]
+    for part, back_ref in enumerate(backs):
+        lanes = slice(part * LANES, part * LANES + LANES)
+        total = jnp.sum(back_ref[:, : 2 * OWN].astype(F32), axis=0)
+        up_ref[:, :, lanes] = total.reshape(2, OWN, LANES)
+        top_ref[:, lanes] = jnp.sum(back_ref[:, 2 * OWN :].astype(F32), axis=0)
 
 
 def finish_kernel(
@@ -243,19 +254,37 @@
     sgrad[cut] = (part * weights[cut].astype(F32)).astype(BF16)
 
 
+def pair_lanes():
+    return [(p, slice(p * PAIR, p * PAIR + PAIR)) for p in range(UNROLL)]
+
+
 def diag_kernel(q_ref, k_ref, v_ref, g_ref, weights_ref, sum_ref, stats_ref, g_t_ref, scores):
+    running = [
+        diag_pair(
+            q_ref.at[:, lanes], k_ref.at[:, lanes], v_ref.at[:, lanes], g_ref.at[:, lanes],
+            weights_ref.at[p], sum_ref.at[lanes], stats_ref.at[p], g_t_ref.at[lanes], scores.at[p],
+        )
+        for p, lanes in pair_lanes()
+    ]
+    staggered(running, BLOCK // CHUNK)
+
+
+def diag_pair(q_ref, k_ref, v_ref, g_ref, weights, sum_ref, stats_ref, g_t_ref, scores):
     g_t_ref[...] = g_ref[...].T
     q_rows = head_rows(q_ref[...])
     largest = None
     for start in starts(BLOCK):
         largest = score_step(start, q_rows, k_ref, scores, {}, largest)
+        yield True
     largest = jnp.max(largest, axis=0, keepdims=True)
     for start in starts(BLOCK):
-        weight_step(start, scores, weights_ref.at[0], largest)
-    total, summed = value_step(v_ref[...].T, weights_ref.at[0])
-    stats_ref[0, 0:1] = largest
-    stats_ref[0, 1:2] = total
+        weight_step(start, scores, weights, largest)
+        yield True
+    total, summed = value_step(v_ref[...].T, weights)
+    stats_ref[0:1] = largest
+    stats_ref[1:2] = total
     sum_ref[...] = summed
+    yield True
 
 
 def low_rows(shape):
@@ -282,11 +311,12 @@
 
 def wide_kernel(
     live_ref, q_ref, g_ref, before_ref, after_ref, sum_ref, stats_ref,
-    group_ref, mine_ref, other_ref,
-    out_ref, scaled_ref, delta_ref, kcat_ref, sgrad_ref,
-    dgroup_ref, dmine_ref, dother_ref, dbefore_ref, dafter_ref,
-    vones, scores, weights,
+    group_ref, mine_ref, other_ref, *rest,
 ):
+    (
+        out_ref, scaled_ref, delta_ref, kcat_ref, sgrad_ref, dbefore_ref, dafter_ref,
+        dgroup_ref, dmine_ref, dother_ref, vones, scores, weights,
+    ) = rest[-13:]
     near_row = lax.broadcasted_iota(jnp.int32, (CHUNK, 1), 0)
     bias = {GROUP + TOP: jnp.where(near_row < NEAR, live_ref[0], live_ref[1])}
 
@@ -392,23 +422,41 @@
 ):
     @pl.when(pl.program_id(0) == 0)
     def _():
-        vones[:, PAIR:] = jnp.ones((BLOCK, PAIR), BF16)
-
+        vones[:, :, PAIR:] = jnp.ones((UNROLL, BLOCK, PAIR), BF16)
+
+    running = [
+        diag_back_pair(
+            q_ref.at[:, lanes], k_ref.at[:, lanes], v_ref.at[:, lanes], weights_ref.at[p],
+            out_t_ref.at[lanes], scaled_ref.at[lanes], delta_ref.at[p], kcat_ref.at[p],
+            wide_ref.at[p], out_ref.at[:, lanes], dq_ref.at[:, lanes], diag_ref.at[:, :, lanes],
+            vones.at[p], sgrad.at[p],
+        )
+        for p, lanes in pair_lanes()
+    ]
+    staggered(running, BLOCK // CHUNK)
+
+
+def diag_back_pair(
+    q_ref, k_ref, v_ref, weights, out_t_ref, scaled_ref, delta_ref, kcat, wide,
+    out_ref, dq_ref, diag_ref, vones, sgrad,
+):
     vones[:, :PAIR] = v_ref[...]
     out_ref[...] = out_t_ref[...].T
-    weights = weights_ref.at[0]
     scaled = scaled_ref[...]
-    g_both = grads_and_delta(scaled, delta_ref[0, 0:1])
+    g_both = grads_and_delta(scaled, delta_ref[0:1])
     for start in starts(BLOCK):
         grad_step(start, g_both, vones, weights, sgrad)
-    dq = dot(kcat_ref[0].T, wide_ref[0]) + dot(k_ref[...].T, sgrad[...])
+        yield True
+    dq = dot(kcat[...].T, wide[...]) + dot(k_ref[...].T, sgrad[...])
     dq_ref[...] = (together(dq).T * SOFT).astype(BF16)
+    yield True
     q_rows = head_rows(q_ref[...])
     g_rows = head_rows(scaled.T)
     for start in starts(BLOCK):
         cut = slice(start, start + CHUNK)
         diag_ref[0, cut] = dot(sgrad[cut], q_rows) * SOFT
         diag_ref[1, cut] = dot(weights[cut], g_rows)
+        yield True
 
 
 def shape_of(dtype, *shape):
@@ -416,7 +464,7 @@
 
 
 def on_lanes(*lead):
-    return pl.BlockSpec(lead + (PAIR,), lambda p: (0,) * len(lead) + (p,))
+    return pl.BlockSpec(lead + (UNROLL * PAIR,), lambda p: (0,) * len(lead) + (p,))
 
 
 def on_rows(*shape):
@@ -433,11 +481,11 @@
 
 SMEM = pl.BlockSpec(memory_space=pltpu.SMEM)
 SEQUENCE = on_lanes(BLOCK)
-COLUMNS = on_rows(PAIR, BLOCK)
-STATS = on_rows(1, 8, BOTH)
-DIAG = on_rows(1, BLOCK, BOTH)
-WIDE_KEYS = on_rows(1, WIDE, PAIR)
-WIDE_GRADS = on_rows(1, WIDE, BOTH)
+COLUMNS = on_rows(UNROLL * PAIR, BLOCK)
+STATS = on_rows(UNROLL, 8, BOTH)
+DIAG = on_rows(UNROLL, BLOCK, BOTH)
+WIDE_KEYS = on_rows(UNROLL, WIDE, PAIR)
+WIDE_GRADS = on_rows(UNROLL, WIDE, BOTH)
 
 
 def call(kernel, name, steps, in_specs, out_specs, out_shape, scratch=()):
@@ -458,12 +506,9 @@
     "group_summaries",
     TILES,
     [on_rows(ROWS, D)] * 2,
-    [every(N_SEQ, 2 * OWN, D), every(2, OWN // RATIO, D), every(2, OWN, D)],
-    (
-        shape_of(BF16, N_SEQ, SENT, D),
-        shape_of(BF16, 2, OWN // RATIO, D),
-        shape_of(F32, 2, OWN, D),
-    ),
+    [every(2, OWN // RATIO, D), every(2, OWN, D)] + [every(N_SEQ, 2 * OWN, LANES)] * PARTS,
+    (shape_of(BF16, 2, OWN // RATIO, D), shape_of(F32, 2, OWN, D))
+    + (shape_of(BF16, N_SEQ, SENT, LANES),) * PARTS,
     [pltpu.VMEM((2, TILES, 8, D), F32)],
 )
 near_summaries = call(
@@ -477,7 +522,7 @@
 diag_forward = call(
     diag_kernel,
     "diag_forward",
-    PAIRS,
+    PAIRS // UNROLL,
     [SEQUENCE] * 4,
     [DIAG, COLUMNS, STATS, COLUMNS],
     (
@@ -486,52 +531,75 @@
         shape_of(F32, PAIRS, 8, BOTH),
         shape_of(BF16, D, BLOCK),
     ),
-    [pltpu.VMEM((BLOCK, BOTH), F32)],
+    [pltpu.VMEM((UNROLL, BLOCK, BOTH), F32)],
 )
-def wide_lanes(*lead):
-    return pl.BlockSpec(lead + (UNROLL * PAIR,), lambda p: (0,) * len(lead) + (p,))
-
-
-wide_attend = call(
-    wide_kernel,
-    "wide_attend",
-    PAIRS // UNROLL,
-    [SMEM]
-    + [wide_lanes(BLOCK), on_rows(UNROLL * PAIR, BLOCK)]
-    + [wide_lanes(2, NEAR)] * 2
-    + [on_rows(UNROLL * PAIR, BLOCK), on_rows(UNROLL, 8, BOTH)]
-    + [wide_lanes(N_SEQ, 2 * OWN)]
-    + [wide_lanes(N_SEQ, 8)] * 2,
-    [on_rows(UNROLL * PAIR, BLOCK)] * 2
-    + [on_rows(UNROLL, 8, BOTH), on_rows(UNROLL, WIDE, PAIR), on_rows(UNROLL, WIDE, BOTH)]
-    + [wide_lanes(N_SEQ, 2 * OWN)]
-    + [wide_lanes(N_SEQ, 8)] * 2
-    + [wide_lanes(2, NEAR)] * 2,
-    (
-        shape_of(BF16, D, BLOCK),
-        shape_of(BF16, D, BLOCK),
-        shape_of(F32, PAIRS, 8, BOTH),
-        shape_of(BF16, PAIRS, WIDE, PAIR),
-        shape_of(BF16, PAIRS, WIDE, BOTH),
-        shape_of(BF16, N_SEQ, SENT, D),
-        shape_of(BF16, N_SEQ, 8, D),
-        shape_of(BF16, N_SEQ, 8, D),
+def wide_attend(part, *args):
+    offset = part * PART_STEPS
+
+    def part_lanes(*lead):
+        return pl.BlockSpec(lead + (UNROLL * PAIR,), lambda p: (0,) * len(lead) + (p,))
+
+    def wide_lanes(*lead):
+        return pl.BlockSpec(
+            lead + (UNROLL * PAIR,), lambda p: (0,) * len(lead) + (p + offset,)
+        )
+
+    def wide_rows(*shape):
+        return pl.BlockSpec(shape, lambda p: (p + offset,) + (0,) * (len(shape) - 1))
+
+    in_specs = (
+        [SMEM, wide_lanes(BLOCK), wide_rows(UNROLL * PAIR, BLOCK)]
+        + [wide_lanes(2, NEAR)] * 2
+        + [wide_rows(UNROLL * PAIR, BLOCK), wide_rows(UNROLL, 8, BOTH)]
+        + [part_lanes(N_SEQ, 2 * OWN)]
+        + [part_lanes(N_SEQ, 8)] * 2
     )
-    + (shape_of(BF16, 2, NEAR, D),) * 2,
-    [
-        pltpu.VMEM((UNROLL, WIDE, 2 * PAIR), BF16),
-        pltpu.VMEM((UNROLL, WIDE, BOTH), F32),
-        pltpu.VMEM((UNROLL, WIDE, BOTH), BF16),
-    ],
-)
+    shared = len(args) - len(in_specs)
+    aliases = {len(in_specs) + index: index for index in range(shared)}
+    return pl.pallas_call(
+        wide_kernel,
+        grid=(PART_STEPS,),
+        in_specs=in_specs + [pl.BlockSpec(memory_space=pl.ANY)] * shared,
+        out_specs=[wide_rows(UNROLL * PAIR, BLOCK)] * 2
+        + [wide_rows(UNROLL, 8, BOTH), wide_rows(UNROLL, WIDE, PAIR)]
+        + [wide_rows(UNROLL, WIDE, BOTH)]
+        + [wide_lanes(2, NEAR)] * 2
+        + [part_lanes(N_SEQ, 2 * OWN)]
+        + [part_lanes(N_SEQ, 8)] * 2,
+        out_shape=(
+            shape_of(BF16, D, BLOCK),
+            shape_of(BF16, D, BLOCK),
+            shape_of(F32, PAIRS, 8, BOTH),
+            shape_of(BF16, PAIRS, WIDE, PAIR),
+            shape_of(BF16, PAIRS, WIDE, BOTH),
+            shape_of(BF16, 2, NEAR, D),
+            shape_of(BF16, 2, NEAR, D),
+            shape_of(BF16, N_SEQ, SENT, LANES),
+            shape_of(BF16, N_SEQ, 8, LANES),
+            shape_of(BF16, N_SEQ, 8, LANES),
+        ),
+        scratch_shapes=[
+            pltpu.VMEM((UNROLL, WIDE, 2 * PAIR), BF16),
+            pltpu.VMEM((UNROLL, WIDE, BOTH), F32),
+            pltpu.VMEM((UNROLL, WIDE, BOTH), BF16),
+        ],
+        input_output_aliases=aliases,
+        compiler_params=pltpu.CompilerParams(vmem_limit_bytes=56 * 1024 * 1024),
+        name="wide_attend%d" % part,
+    )(*args)
+
+
 diag_backward = call(
     diag_back_kernel,
     "diag_backward",
-    PAIRS,
+    PAIRS // UNROLL,
     [SEQUENCE] * 3 + [DIAG] + [COLUMNS] * 2 + [STATS, WIDE_KEYS, WIDE_GRADS],
     [SEQUENCE, SEQUENCE, on_lanes(2, BLOCK)],
     (shape_of(BF16, BLOCK, D), shape_of(BF16, BLOCK, D), shape_of(F32, 2, BLOCK, D)),
-    [pltpu.VMEM((BLOCK, 2 * PAIR), BF16), pltpu.VMEM((BLOCK, BOTH), BF16)],
+    [
+        pltpu.VMEM((UNROLL, BLOCK, 2 * PAIR), BF16),
+        pltpu.VMEM((UNROLL, BLOCK, BOTH), BF16),
+    ],
 )
 collect = pl.pallas_call(
     collect_kernel,
@@ -563,40 +631,65 @@
     return lax.ppermute(block, "grp", [(i, i ^ bit) for i in range(4)])
 
 
+def exchanged(payload):
+    return lax.all_to_all(payload, "seq", 0, 0, tiled=True)
+
+
 def per_device(queries, keys, values, out_grad):
     device = lax.axis_index("grp") * N_SEQ + lax.axis_index("seq")
     count = lax.axis_size(("grp", "seq"))
     live = jnp.stack(
         [jnp.where(device == 0, NEG, 0.0), jnp.where(device == count - 1, NEG, 0.0)]
     ).astype(F32)
-    payload, top, pooled = group_summaries(keys, values)
+    top, pooled, *payloads = group_summaries(keys, values)
     swapped = grp_swap(top, 2)
     near, near_pooled = near_summaries(keys, values)
     near, live = lax.optimization_barrier((near, live))
+    payloads[0], near_pooled = lax.optimization_barrier((payloads[0], near_pooled))
     top_pair = jnp.stack([top, swapped], axis=1).reshape(8, D)
-    tops = jnp.broadcast_to(top_pair[None], (N_SEQ, 8, D))
-    payload = lax.dynamic_update_slice(payload, tops, (0, 2 * OWN, 0))
-    everyone = lax.all_to_all(payload, "seq", 0, 0, tiled=True)
+    for part in range(PARTS):
+        tops = top_pair[:, part * LANES : part * LANES + LANES]
+        payloads[part] = lax.dynamic_update_slice(
+            payloads[part], jnp.broadcast_to(tops[None], (N_SEQ, 8, LANES)), (0, 2 * OWN, 0)
+        )
+    everyone = [exchanged(payloads[0])]
     before = shifted(near, 1)
     after = shifted(near, -1)
     diag_weights, diag_sum, diag_stats, grad_t = diag_forward(queries, keys, values, out_grad)
-    everyone, diag_sum = lax.optimization_barrier((everyone, diag_sum))
-    top_mine = everyone[:, 2 * OWN :]
-    top_other = grp_swap(top_mine, 1)
-    out_t, scaled, delta, kcat, sgrad, back, dmine, dother, dbefore, dafter = wide_attend(
-        live, queries, grad_t, before, after, diag_sum, diag_stats,
-        everyone, top_mine, top_other,
+    payloads[1], everyone[0], diag_sum, before, after = lax.optimization_barrier(
+        (payloads[1], everyone[0], diag_sum, before, after)
     )
-    dmine = (dmine.astype(F32) + grp_swap(dother, 1).astype(F32)).astype(BF16)
-    back = lax.dynamic_update_slice(back, dmine, (0, 2 * OWN, 0))
-    back = lax.all_to_all(back, "seq", 0, 0, tiled=True)
+    everyone.append(exchanged(payloads[1]))
+    kept, returned = (), []
+    for part in range(PARTS):
+        if part:
+            top_mine = everyone[part][:, 2 * OWN :]
+            top_other, returned[-1] = lax.optimization_barrier(
+                (grp_swap(top_mine, 1), returned[-1])
+            )
+            returned[-1] = exchanged(returned[-1])
+        else:
+            top_mine = everyone[part][:, 2 * OWN :]
+            top_other = grp_swap(top_mine, 1)
+        *kept, back, dmine, dother = wide_attend(
+            part, live, queries, grad_t, before, after, diag_sum, diag_stats,
+            everyone[part], top_mine, top_other, *kept,
+        )
+        if part:
+            back, dmine, dother, returned[0] = lax.optimization_barrier(
+                (back, dmine, dother, returned[0])
+            )
+        dmine = (dmine.astype(F32) + grp_swap(dother, 1).astype(F32)).astype(BF16)
+        returned.append(lax.dynamic_update_slice(back, dmine, (0, 2 * OWN, 0)))
+    returned[-1] = exchanged(returned[-1])
+    out_t, scaled, delta, kcat, sgrad, dbefore, dafter = kept
     from_next = shifted(dbefore, -1)
     from_prev = shifted(dafter, 1)
     out, dq, diag = diag_backward(
         queries, keys, values, diag_weights, out_t, scaled, delta, kcat, sgrad
     )
-    back, diag = lax.optimization_barrier((back, diag))
-    group_up, top_up = collect(back)
+    returned[-1], diag = lax.optimization_barrier((returned[-1], diag))
+    group_up, top_up = collect(*returned)
     swapped = grp_swap(top_up, 2)
     dk, dv = finish(
         diag, near_pooled, from_prev, from_next, pooled, group_up, top_up, swapped

time: 161 us -> 159 us (0.988)
  waiting for transfers between devices: 26 us -> 18.7 us
  starting transfers between devices: 51.6 us -> 54.7 us
  local copies, waits for them, and re-layouts: 3.13 us -> 5.02 us
    all_to_all x2 -> x4, starting transfers between devices: 14.5 us -> 24.1 us  [exchanged(): return lax.all_to_all(payload, 'seq', 0, 0, tiled=True)]
    ppermute x4 -> x6, starting transfers between devices: 15.1 us -> 9.62 us  [grp_swap(): return lax.ppermute(block, 'grp', [(i, i ^ bit) for i in range(4)])]
    all_to_all x2 -> x4, waiting for transfers between devices: 7.38 us -> 3.38 us  [exchanged(): return lax.all_to_all(payload, 'seq', 0, 0, tiled=True)]
    pallas_call x3 -> x4, Pallas kernels: 33 us -> 36.8 us  [the longest x2 31.7 us: wide_attend(): pl.pallas_call(wide_kernel, grid=(PART_STEPS,), in_specs=in_specs + [pl.B...]
    ppermute x4, waiting for transfers between devices: 15.3 us -> 12.1 us  [shifted(): return lax.ppermute(block, ('grp', 'seq'), route)]
    pallas_call x1, Pallas kernels: 11.5 us -> 9.69 us  [per_device(): diag_forward(queries, keys, values, out_grad)]
    dynamic_update_slice x1 -> x2, other arithmetic: 2.05 us -> 3.53 us  [per_device(): returned.append(lax.dynamic_update_slice(back, dmine, (0, 2 * OWN, 0)))]
    unnamed x16 -> x28, local copies, waits for them, and re-layouts: 2.22 us -> 3.47 us
  transfers between devices with their start and end apart: 10 -> 14, of which waited for: 7 -> 8; matrix products, arithmetic and copies ran while one was open for 0% -> 2% of each run, Pallas kernels for 22% -> 40%
where the time goes in v4:
time: 159 us; the launch traced here: 158 us
  Pallas kernels  74.7 us (47%)
  starting transfers between devices  54.7 us (34%)
  waiting for transfers between devices  18.7 us (12%)
  local copies, waits for them, and re-layouts  5.02 us (3%)
  other arithmetic  4.2 us (3%)
    pallas_call x2, Pallas kernels, wide_attend(): pl.pallas_call(wide_kernel, grid=(PART_STEPS,), in_specs=in_specs + [pl.B...  31.7 us
    all_to_all x4, starting transfers between devices, exchanged(): return lax.all_to_all(payload, 'seq', 0, 0, tiled=True)  24.1 us
    ppermute x4, starting transfers between devices, shifted(): return lax.ppermute(block, ('grp', 'seq'), route)  20.9 us
    pallas_call x1, Pallas kernels, per_device(): diag_backward(queries, keys, values, diag_weights, out_t, scaled, delta,...  17 us
    ppermute x4, waiting for transfers between devices, shifted(): return lax.ppermute(block, ('grp', 'seq'), route)  12.1 us
    pallas_call x1, Pallas kernels, per_device(): diag_forward(queries, keys, values, out_grad)  9.69 us
    ppermute x6, starting transfers between devices, grp_swap(): return lax.ppermute(block, 'grp', [(i, i ^ bit) for i in range(4)])  9.62 us
    pallas_call x1, Pallas kernels, per_device(): finish(diag, near_pooled, from_prev, from_next, pooled, group_up, top_up,...  6.76 us
  transfers between devices with their start and end apart: 14, of which 8 were waited for; matrix products, arithmetic and copies ran while one was open for 2% of the time, Pallas kernels for 40%

profile of v4, /device:TPU:1, one launch (start us, length us, event | category | flops | bytes accessed | tf_op | source)
XLA Modules:
  0.0 158.1 jit_solution(576430160359180428)
XLA Ops:
  0.6 4.7 %group_summaries.1 = (bf16[2,2,1024]{2,1,0:T(2,128)(2,1)}, f32[2,16,1024]{2,1,0:T(8,128)}, bf16[32,40,512]{2,1,0:T(8,128)(2,1)}, bf16[32,40,512]{2,1,0:T(8,128)(2,1)}) custom-call(bf16[512,1024]{1,0:T(8,128)(2,1)} %k_ref.7, bf16[512,1024]{1,0:T(8,128)(2,1)} %v_ref.7), custom_call_target="tpu_custom_call" | custom-call | tf_op jit(solution)/shard_map/group_summaries/pallas_call | solution.py:644
  5.3 3.7 %collective-permute-start = (bf16[2,2,1024]{2,1,0:T(2,128)(2,1)}, bf16[2,2,1024]{2,1,0:T(2,128)(2,1)S(1)}, u32[]{:S(2)}, u32[]{:S(2)}) collective-permute-start(bf16[2,2,1024]{2,1,0:T(2,128)(2,1)} %get-tuple-element.63), channel_id=1, source_target_pairs={{0,64},{32,96},{64,0},{96,32},{1,65},{33,97},{65,1},{97,33},{2,66}... | collective-permute-start | bytes 24584 | tf_op jit(solution)/shard_map/ppermute | solution.py:631
  9.0 4.4 %near_summaries.1 = (bf16[2,128,1024]{2,1,0:T(8,128)(2,1)}, f32[2,128,1024]{2,1,0:T(8,128)}) custom-call(bf16[512,1024]{1,0:T(8,128)(2,1)} %k_ref.7, bf16[512,1024]{1,0:T(8,128)(2,1)} %v_ref.7), custom_call_target="tpu_custom_call" | custom-call | tf_op jit(solution)/shard_map/near_summaries/pallas_call | solution.py:646
  13.5 0.0 collective-permute-done
  13.5 0.0 copy-done.12
  13.6 0.7 broadcast_dynamic-update-slice_fusion
  14.3 8.1 %all-to-all-start = ((bf16[32,40,512]{2,1,0:T(8,128)(2,1)}), bf16[32,40,512]{2,1,0:T(8,128)(2,1)S(1)}, u32[]{:S(2)}, u32[]{:S(2)}) async-start(bf16[32,40,512]{2,1,0:T(8,128)(2,1)} %broadcast_dynamic-update-slice_fusion), calls=%async_computation | async-start | bytes 2621440 | tf_op jit(solution)/shard_map/all_to_all | solution.py:635
  22.5 0.6 pad_maximum_fusion.1.live_ref
  23.1 0.0 copy-done.13
  23.1 8.8 %collective-permute-start.2 = (bf16[2,128,1024]{2,1,0:T(8,128)(2,1)S(1)}, bf16[2,128,1024]{2,1,0:T(8,128)(2,1)S(1)}, u32[]{:S(2)}, u32[]{:S(2)}) collective-permute-start(bf16[2,128,1024]{2,1,0:T(8,128)(2,1)S(1)} %copy-done.13), channel_id=1, source_target_pairs={{1,0},{2,1},{3,2},{4,3},{5,4},{6,5},{7,6},{8,7},{9,8},{10,9},{11,1... | collective-permute-start | bytes 1572872 | tf_op jit(solution)/shard_map/ppermute | solution.py:627
  31.9 1.9 %collective-permute-start.1 = (bf16[2,128,1024]{2,1,0:T(8,128)(2,1)S(1)}, bf16[2,128,1024]{2,1,0:T(8,128)(2,1)S(1)}, u32[]{:S(2)}, u32[]{:S(2)}) collective-permute-start(bf16[2,128,1024]{2,1,0:T(8,128)(2,1)S(1)} %copy-done.13), channel_id=1, source_target_pairs={{0,1},{1,2},{2,3},{3,4},{4,5},{5,6},{6,7},{7,8},{8,9},{9,10},{10,1... | collective-permute-start | bytes 1572872 | tf_op jit(solution)/shard_map/ppermute | solution.py:627
  33.9 9.7 %diag_forward.1 = (bf16[8,512,1024]{2,1,0:T(8,128)(2,1)}, f32[1024,512]{1,0:T(8,128)}, f32[8,8,1024]{2,1,0:T(8,128)}, bf16[1024,512]{1,0:T(8,128)(2,1)}) custom-call(bf16[512,1024]{1,0:T(8,128)(2,1)} %q_ref.7, bf16[512,1024]{1,0:T(8,128)(2,1)} %k_ref.7, bf16[512,1024]{1,0:T(8,128)(2,1)} %v_ref.7, bf16[512,1024]{1,0:T(8,128)(2,1)} %g_ref.1), custom_call_target="tpu_custom_call" | custom-call | tf_op jit(solution)/shard_map/diag_forward/pallas_call | solution.py:658
  43.6 0.8 broadcast_dynamic-update-slice_fusion.1
  44.3 5.7 %collective-permute-done.2.after_ref = bf16[2,128,1024]{2,1,0:T(8,128)(2,1)S(1)} collective-permute-done((bf16[2,128,1024]{2,1,0:T(8,128)(2,1)S(1)}, bf16[2,128,1024]{2,1,0:T(8,128)(2,1)S(1)}, u32[]{:S(2)}, u32[]{:S(2)}) %collective-permute-start.2) | collective-permute-done | bytes 524320 | tf_op jit(solution)/shard_map/ppermute | solution.py:627
  50.0 4.3 %collective-permute-done.1.before_ref = bf16[2,128,1024]{2,1,0:T(8,128)(2,1)S(1)} collective-permute-done((bf16[2,128,1024]{2,1,0:T(8,128)(2,1)S(1)}, bf16[2,128,1024]{2,1,0:T(8,128)(2,1)S(1)}, u32[]{:S(2)}, u32[]{:S(2)}) %collective-permute-start.1) | collective-permute-done | bytes 524320 | tf_op jit(solution)/shard_map/ppermute | solution.py:627
  54.3 0.0 all-to-all-done.group_ref
  54.3 0.8 copy-done.5
  55.1 4.0 %all-to-all-start.1 = ((bf16[32,40,512]{2,1,0:T(8,128)(2,1)}), bf16[32,40,512]{2,1,0:T(8,128)(2,1)S(1)}, u32[]{:S(2)}, u32[]{:S(2)}) async-start(bf16[32,40,512]{2,1,0:T(8,128)(2,1)} %broadcast_dynamic-update-slice_fusion.1), calls=%async_computation.1 | async-start | bytes 2621440 | tf_op jit(solution)/shard_map/all_to_all | solution.py:635
  59.1 0.4 collective-permute-start.4
  59.5 1.2 collective-permute-done.4.other_ref
  60.7 0.7 copy-done.10
  61.4 16.3 %wide_attend0.1 = (bf16[1024,512]{1,0:T(8,128)(2,1)}, bf16[1024,512]{1,0:T(8,128)(2,1)}, f32[8,8,1024]{2,1,0:T(8,128)}, bf16[8,1024,128]{2,1,0:T(8,128)(2,1)}, b...) custom-call(f32[2]{0:T(128)} %pad_maximum_fusion.1.live_ref, ...), custom_call_target="tpu_custom_call" | custom-call | tf_op jit(solution)/shard_map/wide_attend0/pallas_call | solution.py:559
  77.7 0.4 collective-permute-start.5
  78.1 0.3 all-to-all-done.1.group_ref
  78.5 1.4 collective-permute-start.3
  79.9 0.0 collective-permute-done.5
  79.9 1.8 %fusion = bf16[32,40,512]{2,1,0:T(8,128)(2,1)} fusion(bf16[32,40,512]{2,1,0:T(8,128)(2,1)} %get-tuple-element.75, bf16[32,8,512]{2,1,0:T(8,128)(2,1)S(1)} %collective-permute-done.5, bf16[32,8,512]{2,1,0:T(8,128)(2,1)} %get-tuple-element.76), kind=kLoop, calls=%fused_computation.2 | loop fusion | flops 524288 | bytes 786432 | tf_op jit(solution)/shard_map/dynamic_update_slice | solution.py:683
  81.7 0.0 collective-permute-done.3.other_ref
  81.7 0.7 copy-done.9
  82.4 7.8 %all-to-all-start.2 = ((bf16[32,40,512]{2,1,0:T(8,128)(2,1)}), bf16[32,40,512]{2,1,0:T(8,128)(2,1)S(1)}, u32[]{:S(2)}, u32[]{:S(2)}) async-start(bf16[32,40,512]{2,1,0:T(8,128)(2,1)} %fusion), calls=%async_computation.2 | async-start | bytes 2621440 | tf_op jit(solution)/shard_map/all_to_all | solution.py:635
  90.2 15.4 %wide_attend1.1 = (bf16[1024,512]{1,0:T(8,128)(2,1)}, bf16[1024,512]{1,0:T(8,128)(2,1)}, f32[8,8,1024]{2,1,0:T(8,128)}, bf16[8,1024,128]{2,1,0:T(8,128)(2,1)}, b...) custom-call(f32[2]{0:T(128)} %pad_maximum_fusion.1.live_ref, ...), custom_call_target="tpu_custom_call", output_to_operand_aliasing={{0}: (10, {}), {1}: (11, {}), {2}: (12, {}), {3}: (13, {}),... | custom-call | tf_op jit(solution)/shard_map/wide_attend1/pallas_call | solution.py:559
  105.6 3.1 %all-to-all-done.2.refs_0_ = bf16[32,40,512]{2,1,0:T(8,128)(2,1)S(1)} async-done(((bf16[32,40,512]{2,1,0:T(8,128)(2,1)}), bf16[32,40,512]{2,1,0:T(8,128)(2,1)S(1)}, u32[]{:S(2)}, u32[]{:S(2)}) %all-to-all-start.2) | async-done | bytes 1310752 | tf_op jit(solution)/shard_map/all_to_all | solution.py:635
  108.7 2.1 %collective-permute-start.6 = (bf16[32,8,512]{2,1,0:T(8,128)(2,1)}, bf16[32,8,512]{2,1,0:T(8,128)(2,1)S(1)}, u32[]{:S(2)}, u32[]{:S(2)}) collective-permute-start(bf16[32,8,512]{2,1,0:T(8,128)(2,1)} %get-tuple-element.99), channel_id=1, source_target_pairs={{0,32},{32,0},{64,96},{96,64},{1,33},{33,1},{65,97},{97,65},{2,34}... | collective-permute-start | bytes 786440 | tf_op jit(solution)/shard_map/ppermute | solution.py:631
  110.8 1.4 collective-permute-done.6
  112.2 1.8 %fusion.1 = bf16[32,40,512]{2,1,0:T(8,128)(2,1)} fusion(bf16[32,40,512]{2,1,0:T(8,128)(2,1)} %get-tuple-element.97, bf16[32,8,512]{2,1,0:T(8,128)(2,1)S(1)} %collective-permute-done.6, bf16[32,8,512]{2,1,0:T(8,128)(2,1)} %get-tuple-element.98), kind=kLoop, calls=%fused_computation.3 | loop fusion | flops 524288 | bytes 786432 | tf_op jit(solution)/shard_map/dynamic_update_slice | solution.py:683
  114.0 4.2 %all-to-all-start.3 = ((bf16[32,40,512]{2,1,0:T(8,128)(2,1)}), bf16[32,40,512]{2,1,0:T(8,128)(2,1)S(1)}, u32[]{:S(2)}, u32[]{:S(2)}) async-start(bf16[32,40,512]{2,1,0:T(8,128)(2,1)} %fusion.1), calls=%async_computation.3 | async-start | bytes 2621440 | tf_op jit(solution)/shard_map/all_to_all | solution.py:635
  118.2 3.1 %collective-permute-start.7 = (bf16[2,128,1024]{2,1,0:T(8,128)(2,1)}, bf16[2,128,1024]{2,1,0:T(8,128)(2,1)}, u32[]{:S(2)}, u32[]{:S(2)}) collective-permute-start(bf16[2,128,1024]{2,1,0:T(8,128)(2,1)} %get-tuple-element.103), channel_id=1, source_target_pairs={{0,1},{1,2},{2,3},{3,4},{4,5},{5,6},{6,7},{7,8},{8,9},{9,10},{10,1... | collective-permute-start | bytes 1572872 | tf_op jit(solution)/shard_map/ppermute | solution.py:627
  121.3 7.1 %collective-permute-start.8 = (bf16[2,128,1024]{2,1,0:T(8,128)(2,1)S(1)}, bf16[2,128,1024]{2,1,0:T(8,128)(2,1)}, u32[]{:S(2)}, u32[]{:S(2)}) collective-permute-start(bf16[2,128,1024]{2,1,0:T(8,128)(2,1)S(1)} %copy-done.8), channel_id=1, source_target_pairs={{1,0},{2,1},{3,2},{4,3},{5,4},{6,5},{7,6},{8,7},{9,8},{10,9},{11,1... | collective-permute-start | bytes 1572872 | tf_op jit(solution)/shard_map/ppermute | solution.py:627
  128.4 17.0 %diag_backward.1 = (bf16[512,1024]{1,0:T(8,128)(2,1)}, bf16[512,1024]{1,0:T(8,128)(2,1)}, f32[2,512,1024]{2,1,0:T(8,128)}) custom-call(bf16[512,1024]{1,0:T(8,128)(2,1)} %q_ref.7, bf16[512,1024]{1,0:T(8,128)(2,1)} %k_ref.7, bf16[512,1024]{1,0:T(8,128)(2,1)} %v_ref.7, bf16[8,512,1024]{2,1,0:T(8,128)(2,1)} %get-tuple-element.58.weights_ref, ...), custom_call_target="tpu_custom_call" | custom-call | tf_op jit(solution)/shard_map/diag_backward/pallas_call | solution.py:688
  145.4 0.0 all-to-all-done.3.refs_1_
  145.4 0.4 collect.1
  145.8 0.6 copy-done
  146.5 1.6 collective-permute-start.9
  148.0 2.1 %collective-permute-done.7.prev_ref = bf16[2,128,1024]{2,1,0:T(8,128)(2,1)} collective-permute-done((bf16[2,128,1024]{2,1,0:T(8,128)(2,1)}, bf16[2,128,1024]{2,1,0:T(8,128)(2,1)}, u32[]{:S(2)}, u32[]{:S(2)}) %collective-permute-start.7) | collective-permute-done | bytes 524320 | tf_op jit(solution)/shard_map/ppermute | solution.py:627
  150.1 0.0 collective-permute-done.8.next_ref
  150.1 0.6 collective-permute-done.9.swapped_ref
  150.7 0.6 copy-done.11
  151.3 6.8 %finish.1 = (bf16[512,1024]{1,0:T(8,128)(2,1)}, bf16[512,1024]{1,0:T(8,128)(2,1)}) custom-call(f32[2,512,1024]{2,1,0:T(8,128)} %get-tuple-element.101.diag_ref, f32[2,128,1024]{2,1,0:T(8,128)} %get-tuple-element.102.near_pooled_ref, bf16[2,128,1024]{2,1,0:T(8,128)(2,1)} %collective-permute-done.7.prev_ref, ...), custom_call_target="tpu_custom_call" | custom-call | tf_op jit(solution)/shard_map/finish/pallas_call | solution.py:694
  (27 shorter events, 0.1 us)
Async XLA Ops:
  5.3 8.2 %copy-start.12 = (bf16[2,2,1024]{2,1,0:T(2,128)(2,1)S(1)}, bf16[2,2,1024]{2,1,0:T(2,128)(2,1)}, u32[]{:S(2)}) copy-start(bf16[2,2,1024]{2,1,0:T(2,128)(2,1)} %get-tuple-element.63) | copy-start | bytes 24580
  5.3 8.2 %collective-permute-start = (bf16[2,2,1024]{2,1,0:T(2,128)(2,1)}, bf16[2,2,1024]{2,1,0:T(2,128)(2,1)S(1)}, u32[]{:S(2)}, u32[]{:S(2)}) collective-permute-start(bf16[2,2,1024]{2,1,0:T(2,128)(2,1)} %get-tuple-element.63), channel_id=1, source_target_pairs={{0,64},{32,96},{64,0},{96,32},{1,65},{33,97},{65,1},{97,33},{2,66}... | collective-permute-start | bytes 24584 | tf_op jit(solution)/shard_map/ppermute | solution.py:631
  14.3 8.8 %copy-start.13 = (bf16[2,128,1024]{2,1,0:T(8,128)(2,1)S(1)}, bf16[2,128,1024]{2,1,0:T(8,128)(2,1)}, u32[]{:S(2)}) copy-start(bf16[2,128,1024]{2,1,0:T(8,128)(2,1)} %get-tuple-element.68) | copy-start | bytes 1572868
  14.3 40.0 %all-to-all-start = ((bf16[32,40,512]{2,1,0:T(8,128)(2,1)}), bf16[32,40,512]{2,1,0:T(8,128)(2,1)S(1)}, u32[]{:S(2)}, u32[]{:S(2)}) async-start(bf16[32,40,512]{2,1,0:T(8,128)(2,1)} %broadcast_dynamic-update-slice_fusion), calls=%async_computation | async-start | bytes 2621440 | tf_op jit(solution)/shard_map/all_to_all | solution.py:635
  23.1 26.9 %collective-permute-start.2 = (bf16[2,128,1024]{2,1,0:T(8,128)(2,1)S(1)}, bf16[2,128,1024]{2,1,0:T(8,128)(2,1)S(1)}, u32[]{:S(2)}, u32[]{:S(2)}) collective-permute-start(bf16[2,128,1024]{2,1,0:T(8,128)(2,1)S(1)} %copy-done.13), channel_id=1, source_target_pairs={{1,0},{2,1},{3,2},{4,3},{5,4},{6,5},{7,6},{8,7},{9,8},{10,9},{11,1... | collective-permute-start | bytes 1572872 | tf_op jit(solution)/shard_map/ppermute | solution.py:627
  31.9 22.4 %collective-permute-start.1 = (bf16[2,128,1024]{2,1,0:T(8,128)(2,1)S(1)}, bf16[2,128,1024]{2,1,0:T(8,128)(2,1)S(1)}, u32[]{:S(2)}, u32[]{:S(2)}) collective-permute-start(bf16[2,128,1024]{2,1,0:T(8,128)(2,1)S(1)} %copy-done.13), channel_id=1, source_target_pairs={{0,1},{1,2},{2,3},{3,4},{4,5},{5,6},{6,7},{7,8},{8,9},{9,10},{10,1... | collective-permute-start | bytes 1572872 | tf_op jit(solution)/shard_map/ppermute | solution.py:627
  50.0 5.1 %copy-start.4 = (bf16[2,128,1024]{2,1,0:T(8,128)(2,1)}, bf16[2,128,1024]{2,1,0:T(8,128)(2,1)S(1)}, u32[]{:S(2)}) copy-start(bf16[2,128,1024]{2,1,0:T(8,128)(2,1)S(1)} %collective-permute-done.2.after_ref) | copy-start | bytes 1572868
  54.3 0.8 copy-start.5
  54.3 4.8 %copy-start.3 = (bf16[32,40,512]{2,1,0:T(8,128)(2,1)}, bf16[32,40,512]{2,1,0:T(8,128)(2,1)S(1)}, u32[]{:S(2)}) copy-start(bf16[32,40,512]{2,1,0:T(8,128)(2,1)S(1)} %all-to-all-done.group_ref) | copy-start | bytes 3932164
  55.1 23.3 %all-to-all-start.1 = ((bf16[32,40,512]{2,1,0:T(8,128)(2,1)}), bf16[32,40,512]{2,1,0:T(8,128)(2,1)S(1)}, u32[]{:S(2)}, u32[]{:S(2)}) async-start(bf16[32,40,512]{2,1,0:T(8,128)(2,1)} %broadcast_dynamic-update-slice_fusion.1), calls=%async_computation.1 | async-start | bytes 2621440 | tf_op jit(solution)/shard_map/all_to_all | solution.py:635
  59.1 1.6 %copy-start.7 = (bf16[32,8,512]{2,1,0:T(8,128)(2,1)}, bf16[32,8,512]{2,1,0:T(8,128)(2,1)S(1)}, u32[]{:S(2)}) copy-start(bf16[32,8,512]{2,1,0:T(8,128)(2,1)S(1)} %slice.15.mine_ref) | copy-start | bytes 786436
  59.1 1.6 %collective-permute-start.4 = (bf16[32,8,512]{2,1,0:T(8,128)(2,1)S(1)}, bf16[32,8,512]{2,1,0:T(8,128)(2,1)S(1)}, u32[]{:S(2)}, u32[]{:S(2)}) collective-permute-start(bf16[32,8,512]{2,1,0:T(8,128)(2,1)S(1)} %slice.15.mine_ref), channel_id=1, source_target_pairs={{0,32},{32,0},{64,96},{96,64},{1,33},{33,1},{65,97},{97,65},{2,34}... | collective-permute-start | bytes 786440 | tf_op jit(solution)/shard_map/ppermute | solution.py:631
  60.7 0.7 copy-start.10
  77.7 2.2 %collective-permute-start.5 = (bf16[32,8,512]{2,1,0:T(8,128)(2,1)}, bf16[32,8,512]{2,1,0:T(8,128)(2,1)S(1)}, u32[]{:S(2)}, u32[]{:S(2)}) collective-permute-start(bf16[32,8,512]{2,1,0:T(8,128)(2,1)} %get-tuple-element.77), channel_id=1, source_target_pairs={{0,32},{32,0},{64,96},{96,64},{1,33},{33,1},{65,97},{97,65},{2,34}... | collective-permute-start | bytes 786440 | tf_op jit(solution)/shard_map/ppermute | solution.py:631
  78.4 3.2 %copy-start.2 = (bf16[32,40,512]{2,1,0:T(8,128)(2,1)}, bf16[32,40,512]{2,1,0:T(8,128)(2,1)S(1)}, u32[]{:S(2)}) copy-start(bf16[32,40,512]{2,1,0:T(8,128)(2,1)S(1)} %all-to-all-done.1.group_ref) | copy-start | bytes 3932164
  78.5 3.2 %copy-start.6 = (bf16[32,8,512]{2,1,0:T(8,128)(2,1)}, bf16[32,8,512]{2,1,0:T(8,128)(2,1)S(1)}, u32[]{:S(2)}) copy-start(bf16[32,8,512]{2,1,0:T(8,128)(2,1)S(1)} %slice.18.mine_ref) | copy-start | bytes 786436
  78.5 3.2 %collective-permute-start.3 = (bf16[32,8,512]{2,1,0:T(8,128)(2,1)S(1)}, bf16[32,8,512]{2,1,0:T(8,128)(2,1)S(1)}, u32[]{:S(2)}, u32[]{:S(2)}) collective-permute-start(bf16[32,8,512]{2,1,0:T(8,128)(2,1)S(1)} %slice.18.mine_ref), channel_id=1, source_target_pairs={{0,32},{32,0},{64,96},{96,64},{1,33},{33,1},{65,97},{97,65},{2,34}... | collective-permute-start | bytes 786440 | tf_op jit(solution)/shard_map/ppermute | solution.py:631
  81.7 0.7 copy-start.9
  82.4 26.3 %all-to-all-start.2 = ((bf16[32,40,512]{2,1,0:T(8,128)(2,1)}), bf16[32,40,512]{2,1,0:T(8,128)(2,1)S(1)}, u32[]{:S(2)}, u32[]{:S(2)}) async-start(bf16[32,40,512]{2,1,0:T(8,128)(2,1)} %fusion), calls=%async_computation.2 | async-start | bytes 2621440 | tf_op jit(solution)/shard_map/all_to_all | solution.py:635
  108.7 3.5 %collective-permute-start.6 = (bf16[32,8,512]{2,1,0:T(8,128)(2,1)}, bf16[32,8,512]{2,1,0:T(8,128)(2,1)S(1)}, u32[]{:S(2)}, u32[]{:S(2)}) collective-permute-start(bf16[32,8,512]{2,1,0:T(8,128)(2,1)} %get-tuple-element.99), channel_id=1, source_target_pairs={{0,32},{32,0},{64,96},{96,64},{1,33},{33,1},{65,97},{97,65},{2,34}... | collective-permute-start | bytes 786440 | tf_op jit(solution)/shard_map/ppermute | solution.py:631
  114.0 7.3 %copy-start.8 = (bf16[2,128,1024]{2,1,0:T(8,128)(2,1)S(1)}, bf16[2,128,1024]{2,1,0:T(8,128)(2,1)}, u32[]{:S(2)}) copy-start(bf16[2,128,1024]{2,1,0:T(8,128)(2,1)} %get-tuple-element.104) | copy-start | bytes 1572868
  114.0 31.4 %all-to-all-start.3 = ((bf16[32,40,512]{2,1,0:T(8,128)(2,1)}), bf16[32,40,512]{2,1,0:T(8,128)(2,1)S(1)}, u32[]{:S(2)}, u32[]{:S(2)}) async-start(bf16[32,40,512]{2,1,0:T(8,128)(2,1)} %fusion.1), calls=%async_computation.3 | async-start | bytes 2621440 | tf_op jit(solution)/shard_map/all_to_all | solution.py:635
  118.2 32.0 %collective-permute-start.7 = (bf16[2,128,1024]{2,1,0:T(8,128)(2,1)}, bf16[2,128,1024]{2,1,0:T(8,128)(2,1)}, u32[]{:S(2)}, u32[]{:S(2)}) collective-permute-start(bf16[2,128,1024]{2,1,0:T(8,128)(2,1)} %get-tuple-element.103), channel_id=1, source_target_pairs={{0,1},{1,2},{2,3},{3,4},{4,5},{5,6},{6,7},{7,8},{8,9},{9,10},{10,1... | collective-permute-start | bytes 1572872 | tf_op jit(solution)/shard_map/ppermute | solution.py:627
  121.3 28.8 %collective-permute-start.8 = (bf16[2,128,1024]{2,1,0:T(8,128)(2,1)S(1)}, bf16[2,128,1024]{2,1,0:T(8,128)(2,1)}, u32[]{:S(2)}, u32[]{:S(2)}) collective-permute-start(bf16[2,128,1024]{2,1,0:T(8,128)(2,1)S(1)} %copy-done.8), channel_id=1, source_target_pairs={{1,0},{2,1},{3,2},{4,3},{5,4},{6,5},{7,6},{8,7},{9,8},{10,9},{11,1... | collective-permute-start | bytes 1572872 | tf_op jit(solution)/shard_map/ppermute | solution.py:627
  145.8 0.7 copy-start
  146.4 4.3 %copy-start.1 = (f32[8,1024]{1,0:T(8,128)}, f32[8,1024]{1,0:T(8,128)S(1)}, u32[]{:S(2)}) copy-start(f32[8,1024]{1,0:T(8,128)S(1)} %get-tuple-element.109.top_ref) | copy-start | bytes 98308
  146.5 4.3 %collective-permute-start.9 = (f32[8,1024]{1,0:T(8,128)S(1)}, f32[8,1024]{1,0:T(8,128)S(1)}, u32[]{:S(2)}, u32[]{:S(2)}) collective-permute-start(f32[8,1024]{1,0:T(8,128)S(1)} %get-tuple-element.109.top_ref), channel_id=1, source_target_pairs={{0,64},{32,96},{64,0},{96,32},{1,65},{33,97},{65,1},{97,33},{2,66}... | collective-permute-start | bytes 98312 | tf_op jit(solution)/shard_map/ppermute | solution.py:631
  150.7 0.6 copy-start.11

commit v5 on v4

--- a/solution.py
+++ b/solution.py
@@ -314,9 +314,9 @@
     group_ref, mine_ref, other_ref, *rest,
 ):
     (
-        out_ref, scaled_ref, delta_ref, kcat_ref, sgrad_ref, dbefore_ref, dafter_ref,
-        dgroup_ref, dmine_ref, dother_ref, vones, scores, weights,
-    ) = rest[-13:]
+        out_ref, scaled_ref, delta_ref, dq_ref, dbefore_ref, dafter_ref,
+        dgroup_ref, dmine_ref, dother_ref, kcats, vones, scores, weights, sgrads,
+    ) = rest[-14:]
     near_row = lax.broadcasted_iota(jnp.int32, (CHUNK, 1), 0)
     bias = {GROUP + TOP: jnp.where(near_row < NEAR, live_ref[0], live_ref[1])}
 
@@ -333,7 +333,7 @@
             sum_ref.at[lanes], stats_ref.at[p], group_ref.at[:, :, lanes],
             split_top(mine_ref, lanes), split_top(other_ref, lanes),
             out_ref.at[lanes], scaled_ref.at[lanes], delta_ref.at[p],
-            kcat_ref.at[p], sgrad_ref.at[p],
+            dq_ref.at[lanes], kcats.at[p], sgrads.at[p],
             dgroup_ref.at[:, :, lanes], dmine_ref.at[:, :, lanes], dother_ref.at[:, :, lanes],
             dbefore_ref.at[:, :, lanes], dafter_ref.at[:, :, lanes],
             vones.at[p], scores.at[p], weights.at[p],
@@ -353,7 +353,7 @@
 
 def wide_pair(
     bias, q_ref, g_ref, before_ref, after_ref, sum_ref, stats_ref, group_ref, mine, other,
-    out_ref, scaled_ref, delta_ref, kcat, sgrad,
+    out_ref, scaled_ref, delta_ref, dq_ref, kcat, sgrad,
     dgroup_ref, dmine_ref, dother_ref, dbefore_ref, dafter_ref,
     vones, scores, weights,
 ):
@@ -395,6 +395,8 @@
     for start in starts(WIDE):
         grad_step(start, g_both, vones, weights, sgrad)
         yield True
+    dq_ref[...] = together(dot(kcat[...].T, sgrad[...]))
+    yield True
     g_rows = head_rows(scaled.T)
     for start in starts(WIDE):
         cut = slice(start, start + CHUNK)
@@ -417,7 +419,7 @@
 
 
 def diag_back_kernel(
-    q_ref, k_ref, v_ref, weights_ref, out_t_ref, scaled_ref, delta_ref, kcat_ref, wide_ref,
+    q_ref, k_ref, v_ref, weights_ref, out_t_ref, scaled_ref, delta_ref, wide_ref,
     out_ref, dq_ref, diag_ref, vones, sgrad,
 ):
     @pl.when(pl.program_id(0) == 0)
@@ -427,8 +429,8 @@
     running = [
         diag_back_pair(
             q_ref.at[:, lanes], k_ref.at[:, lanes], v_ref.at[:, lanes], weights_ref.at[p],
-            out_t_ref.at[lanes], scaled_ref.at[lanes], delta_ref.at[p], kcat_ref.at[p],
-            wide_ref.at[p], out_ref.at[:, lanes], dq_ref.at[:, lanes], diag_ref.at[:, :, lanes],
+            out_t_ref.at[lanes], scaled_ref.at[lanes], delta_ref.at[p],
+            wide_ref.at[lanes], out_ref.at[:, lanes], dq_ref.at[:, lanes], diag_ref.at[:, :, lanes],
             vones.at[p], sgrad.at[p],
         )
         for p, lanes in pair_lanes()
@@ -437,7 +439,7 @@
 
 
 def diag_back_pair(
-    q_ref, k_ref, v_ref, weights, out_t_ref, scaled_ref, delta_ref, kcat, wide,
+    q_ref, k_ref, v_ref, weights, out_t_ref, scaled_ref, delta_ref, wide_ref,
     out_ref, dq_ref, diag_ref, vones, sgrad,
 ):
     vones[:, :PAIR] = v_ref[...]
@@ -447,8 +449,8 @@
     for start in starts(BLOCK):
         grad_step(start, g_both, vones, weights, sgrad)
         yield True
-    dq = dot(kcat[...].T, wide[...]) + dot(k_ref[...].T, sgrad[...])
-    dq_ref[...] = (together(dq).T * SOFT).astype(BF16)
+    dq = wide_ref[...] + together(dot(k_ref[...].T, sgrad[...]))
+    dq_ref[...] = (dq.T * SOFT).astype(BF16)
     yield True
     q_rows = head_rows(q_ref[...])
     g_rows = head_rows(scaled.T)
@@ -484,8 +486,6 @@
 COLUMNS = on_rows(UNROLL * PAIR, BLOCK)
 STATS = on_rows(UNROLL, 8, BOTH)
 DIAG = on_rows(UNROLL, BLOCK, BOTH)
-WIDE_KEYS = on_rows(UNROLL, WIDE, PAIR)
-WIDE_GRADS = on_rows(UNROLL, WIDE, BOTH)
 
 
 def call(kernel, name, steps, in_specs, out_specs, out_shape, scratch=()):
@@ -561,8 +561,7 @@
         grid=(PART_STEPS,),
         in_specs=in_specs + [pl.BlockSpec(memory_space=pl.ANY)] * shared,
         out_specs=[wide_rows(UNROLL * PAIR, BLOCK)] * 2
-        + [wide_rows(UNROLL, 8, BOTH), wide_rows(UNROLL, WIDE, PAIR)]
-        + [wide_rows(UNROLL, WIDE, BOTH)]
+        + [wide_rows(UNROLL, 8, BOTH), wide_rows(UNROLL * PAIR, BLOCK)]
         + [wide_lanes(2, NEAR)] * 2
         + [part_lanes(N_SEQ, 2 * OWN)]
         + [part_lanes(N_SEQ, 8)] * 2,
@@ -570,8 +569,7 @@
             shape_of(BF16, D, BLOCK),
             shape_of(BF16, D, BLOCK),
             shape_of(F32, PAIRS, 8, BOTH),
-            shape_of(BF16, PAIRS, WIDE, PAIR),
-            shape_of(BF16, PAIRS, WIDE, BOTH),
+            shape_of(F32, D, BLOCK),
             shape_of(BF16, 2, NEAR, D),
             shape_of(BF16, 2, NEAR, D),
             shape_of(BF16, N_SEQ, SENT, LANES),
@@ -579,8 +577,10 @@
             shape_of(BF16, N_SEQ, 8, LANES),
         ),
         scratch_shapes=[
+            pltpu.VMEM((UNROLL, WIDE, PAIR), BF16),
             pltpu.VMEM((UNROLL, WIDE, 2 * PAIR), BF16),
             pltpu.VMEM((UNROLL, WIDE, BOTH), F32),
+            pltpu.VMEM((UNROLL, WIDE, BOTH), BF16),
             pltpu.VMEM((UNROLL, WIDE, BOTH), BF16),
         ],
         input_output_aliases=aliases,
@@ -593,7 +593,7 @@
     diag_back_kernel,
     "diag_backward",
     PAIRS // UNROLL,
-    [SEQUENCE] * 3 + [DIAG] + [COLUMNS] * 2 + [STATS, WIDE_KEYS, WIDE_GRADS],
+    [SEQUENCE] * 3 + [DIAG] + [COLUMNS] * 2 + [STATS, COLUMNS],
     [SEQUENCE, SEQUENCE, on_lanes(2, BLOCK)],
     (shape_of(BF16, BLOCK, D), shape_of(BF16, BLOCK, D), shape_of(F32, 2, BLOCK, D)),
     [
@@ -682,11 +682,11 @@
         dmine = (dmine.astype(F32) + grp_swap(dother, 1).astype(F32)).astype(BF16)
         returned.append(lax.dynamic_update_slice(back, dmine, (0, 2 * OWN, 0)))
     returned[-1] = exchanged(returned[-1])
-    out_t, scaled, delta, kcat, sgrad, dbefore, dafter = kept
+    out_t, scaled, delta, dq_t, dbefore, dafter = kept
     from_next = shifted(dbefore, -1)
     from_prev = shifted(dafter, 1)
     out, dq, diag = diag_backward(
-        queries, keys, values, diag_weights, out_t, scaled, delta, kcat, sgrad
+        queries, keys, values, diag_weights, out_t, scaled, delta, dq_t
     )
     returned[-1], diag = lax.optimization_barrier((returned[-1], diag))
     group_up, top_up = collect(*returned)

time: 159 us -> 159 us (level)
  Pallas kernels: 74.7 us -> 71.3 us
  waiting for transfers between devices: 18.7 us -> 21.7 us
    ppermute x4, waiting for transfers between devices: 12.1 us -> 16.9 us  [shifted(): return lax.ppermute(block, ('grp', 'seq'), route)]
    pallas_call x1, Pallas kernels: 17 us -> 12.3 us  [per_device(): diag_backward(queries, keys, values, diag_weights, out_t, scaled, delta,...]
  transfers between devices with their start and end apart: 14 -> 14, of which waited for: 8 -> 7; matrix products, arithmetic and copies ran while one was open for 2% -> 2% of each run, Pallas kernels for 40% -> 38%
where the time goes in v5:
time: 159 us; the launch traced here: 158 us
  Pallas kernels  71.3 us (45%)
  starting transfers between devices  55.2 us (35%)
  waiting for transfers between devices  21.7 us (14%)
  local copies, waits for them, and re-layouts  5.12 us (3%)
  other arithmetic  4.08 us (3%)
    pallas_call x2, Pallas kernels, wide_attend(): pl.pallas_call(wide_kernel, grid=(PART_STEPS,), in_specs=in_specs + [pl.B...  33.1 us
    all_to_all x4, starting transfers between devices, exchanged(): return lax.all_to_all(payload, 'seq', 0, 0, tiled=True)  24.5 us
    ppermute x4, starting transfers between devices, shifted(): return lax.ppermute(block, ('grp', 'seq'), route)  21 us
    ppermute x4, waiting for transfers between devices, shifted(): return lax.ppermute(block, ('grp', 'seq'), route)  16.9 us
    pallas_call x1, Pallas kernels, per_device(): diag_backward(queries, keys, values, diag_weights, out_t, scaled, delta,...  12.3 us
    ppermute x6, starting transfers between devices, grp_swap(): return lax.ppermute(block, 'grp', [(i, i ^ bit) for i in range(4)])  9.78 us
    pallas_call x1, Pallas kernels, per_device(): diag_forward(queries, keys, values, out_grad)  9.68 us
    pallas_call x1, Pallas kernels, per_device(): finish(diag, near_pooled, from_prev, from_next, pooled, group_up, top_up,...  6.76 us
  transfers between devices with their start and end apart: 14, of which 7 were waited for; matrix products, arithmetic and copies ran while one was open for 2% of the time, Pallas kernels for 38%

profile of v5, /device:TPU:1, one launch (start us, length us, event | category | flops | bytes accessed | tf_op | source)
XLA Modules:
  0.0 158.3 jit_solution(6117282280629942977)
XLA Ops:
  0.6 4.7 %group_summaries.1 = (bf16[2,2,1024]{2,1,0:T(2,128)(2,1)}, f32[2,16,1024]{2,1,0:T(8,128)}, bf16[32,40,512]{2,1,0:T(8,128)(2,1)}, bf16[32,40,512]{2,1,0:T(8,128)(2,1)}) custom-call(bf16[512,1024]{1,0:T(8,128)(2,1)} %k_ref.7, bf16[512,1024]{1,0:T(8,128)(2,1)} %v_ref.7), custom_call_target="tpu_custom_call" | custom-call | tf_op jit(solution)/shard_map/group_summaries/pallas_call | solution.py:644
  5.3 3.7 %collective-permute-start = (bf16[2,2,1024]{2,1,0:T(2,128)(2,1)}, bf16[2,2,1024]{2,1,0:T(2,128)(2,1)S(1)}, u32[]{:S(2)}, u32[]{:S(2)}) collective-permute-start(bf16[2,2,1024]{2,1,0:T(2,128)(2,1)} %get-tuple-element.61), channel_id=1, source_target_pairs={{0,64},{32,96},{64,0},{96,32},{1,65},{33,97},{65,1},{97,33},{2,66}... | collective-permute-start | bytes 24584 | tf_op jit(solution)/shard_map/ppermute | solution.py:631
  9.1 4.4 %near_summaries.1 = (bf16[2,128,1024]{2,1,0:T(8,128)(2,1)}, f32[2,128,1024]{2,1,0:T(8,128)}) custom-call(bf16[512,1024]{1,0:T(8,128)(2,1)} %k_ref.7, bf16[512,1024]{1,0:T(8,128)(2,1)} %v_ref.7), custom_call_target="tpu_custom_call" | custom-call | tf_op jit(solution)/shard_map/near_summaries/pallas_call | solution.py:646
  13.5 0.0 collective-permute-done
  13.6 0.8 broadcast_dynamic-update-slice_fusion
  14.4 8.1 %all-to-all-start = ((bf16[32,40,512]{2,1,0:T(8,128)(2,1)}), bf16[32,40,512]{2,1,0:T(8,128)(2,1)S(1)}, u32[]{:S(2)}, u32[]{:S(2)}) async-start(bf16[32,40,512]{2,1,0:T(8,128)(2,1)} %broadcast_dynamic-update-slice_fusion), calls=%async_computation | async-start | bytes 2621440 | tf_op jit(solution)/shard_map/all_to_all | solution.py:635
  22.5 0.6 pad_maximum_fusion.1.live_ref
  23.1 8.8 %collective-permute-start.2 = (bf16[2,128,1024]{2,1,0:T(8,128)(2,1)S(1)}, bf16[2,128,1024]{2,1,0:T(8,128)(2,1)S(1)}, u32[]{:S(2)}, u32[]{:S(2)}) collective-permute-start(bf16[2,128,1024]{2,1,0:T(8,128)(2,1)S(1)} %copy-done.13), channel_id=1, source_target_pairs={{1,0},{2,1},{3,2},{4,3},{5,4},{6,5},{7,6},{8,7},{9,8},{10,9},{11,1... | collective-permute-start | bytes 1572872 | tf_op jit(solution)/shard_map/ppermute | solution.py:627
  32.0 1.9 %collective-permute-start.1 = (bf16[2,128,1024]{2,1,0:T(8,128)(2,1)S(1)}, bf16[2,128,1024]{2,1,0:T(8,128)(2,1)S(1)}, u32[]{:S(2)}, u32[]{:S(2)}) collective-permute-start(bf16[2,128,1024]{2,1,0:T(8,128)(2,1)S(1)} %copy-done.13), channel_id=1, source_target_pairs={{0,1},{1,2},{2,3},{3,4},{4,5},{5,6},{6,7},{7,8},{8,9},{9,10},{10,1... | collective-permute-start | bytes 1572872 | tf_op jit(solution)/shard_map/ppermute | solution.py:627
  33.9 9.7 %diag_forward.1 = (bf16[8,512,1024]{2,1,0:T(8,128)(2,1)}, f32[1024,512]{1,0:T(8,128)}, f32[8,8,1024]{2,1,0:T(8,128)}, bf16[1024,512]{1,0:T(8,128)(2,1)}) custom-call(bf16[512,1024]{1,0:T(8,128)(2,1)} %q_ref.7, bf16[512,1024]{1,0:T(8,128)(2,1)} %k_ref.7, bf16[512,1024]{1,0:T(8,128)(2,1)} %v_ref.7, bf16[512,1024]{1,0:T(8,128)(2,1)} %g_ref.1), custom_call_target="tpu_custom_call" | custom-call | tf_op jit(solution)/shard_map/diag_forward/pallas_call | solution.py:658
  43.6 0.7 broadcast_dynamic-update-slice_fusion.1
  44.4 5.7 %collective-permute-done.2.after_ref = bf16[2,128,1024]{2,1,0:T(8,128)(2,1)S(1)} collective-permute-done((bf16[2,128,1024]{2,1,0:T(8,128)(2,1)S(1)}, bf16[2,128,1024]{2,1,0:T(8,128)(2,1)S(1)}, u32[]{:S(2)}, u32[]{:S(2)}) %collective-permute-start.2) | collective-permute-done | bytes 524320 | tf_op jit(solution)/shard_map/ppermute | solution.py:627
  50.1 4.3 %collective-permute-done.1.before_ref = bf16[2,128,1024]{2,1,0:T(8,128)(2,1)S(1)} collective-permute-done((bf16[2,128,1024]{2,1,0:T(8,128)(2,1)S(1)}, bf16[2,128,1024]{2,1,0:T(8,128)(2,1)S(1)}, u32[]{:S(2)}, u32[]{:S(2)}) %collective-permute-start.1) | collective-permute-done | bytes 524320 | tf_op jit(solution)/shard_map/ppermute | solution.py:627
  54.4 0.0 all-to-all-done.group_ref
  54.4 0.8 copy-done.5
  55.2 4.0 %all-to-all-start.1 = ((bf16[32,40,512]{2,1,0:T(8,128)(2,1)}), bf16[32,40,512]{2,1,0:T(8,128)(2,1)S(1)}, u32[]{:S(2)}, u32[]{:S(2)}) async-start(bf16[32,40,512]{2,1,0:T(8,128)(2,1)} %broadcast_dynamic-update-slice_fusion.1), calls=%async_computation.1 | async-start | bytes 2621440 | tf_op jit(solution)/shard_map/all_to_all | solution.py:635
  59.1 0.0 copy-done.3
  59.2 0.4 collective-permute-start.4
  59.6 1.2 collective-permute-done.4.other_ref
  60.8 0.0 copy-done.7
  60.8 0.7 copy-done.10
  61.5 16.5 %wide_attend0.1 = (bf16[1024,512]{1,0:T(8,128)(2,1)}, bf16[1024,512]{1,0:T(8,128)(2,1)}, f32[8,8,1024]{2,1,0:T(8,128)}, f32[1024,512]{1,0:T(8,128)}, bf16[2,128,...) custom-call(f32[2]{0:T(128)} %pad_maximum_fusion.1.live_ref, ...), custom_call_target="tpu_custom_call" | custom-call | tf_op jit(solution)/shard_map/wide_attend0/pallas_call | solution.py:559
  78.1 0.4 collective-permute-start.5
  78.4 0.1 all-to-all-done.1.group_ref
  78.5 1.6 %collective-permute-start.3 = (bf16[32,8,512]{2,1,0:T(8,128)(2,1)S(1)}, bf16[32,8,512]{2,1,0:T(8,128)(2,1)S(1)}, u32[]{:S(2)}, u32[]{:S(2)}) collective-permute-start(bf16[32,8,512]{2,1,0:T(8,128)(2,1)S(1)} %slice.18.mine_ref), channel_id=1, source_target_pairs={{0,32},{32,0},{64,96},{96,64},{1,33},{33,1},{65,97},{97,65},{2,34}... | collective-permute-start | bytes 786440 | tf_op jit(solution)/shard_map/ppermute | solution.py:631
  80.1 0.0 collective-permute-done.5
  80.1 1.7 %fusion = bf16[32,40,512]{2,1,0:T(8,128)(2,1)} fusion(bf16[32,40,512]{2,1,0:T(8,128)(2,1)} %get-tuple-element.73, bf16[32,8,512]{2,1,0:T(8,128)(2,1)S(1)} %collective-permute-done.5, bf16[32,8,512]{2,1,0:T(8,128)(2,1)} %get-tuple-element.74), kind=kLoop, calls=%fused_computation.2 | loop fusion | flops 524288 | bytes 786432 | tf_op jit(solution)/shard_map/dynamic_update_slice | solution.py:683
  81.9 0.0 collective-permute-done.3.other_ref
  81.9 0.7 copy-done.9
  82.6 7.7 %all-to-all-start.2 = ((bf16[32,40,512]{2,1,0:T(8,128)(2,1)}), bf16[32,40,512]{2,1,0:T(8,128)(2,1)S(1)}, u32[]{:S(2)}, u32[]{:S(2)}) async-start(bf16[32,40,512]{2,1,0:T(8,128)(2,1)} %fusion), calls=%async_computation.2 | async-start | bytes 2621440 | tf_op jit(solution)/shard_map/all_to_all | solution.py:635
  90.3 16.6 %wide_attend1.1 = (bf16[1024,512]{1,0:T(8,128)(2,1)}, bf16[1024,512]{1,0:T(8,128)(2,1)}, f32[8,8,1024]{2,1,0:T(8,128)}, f32[1024,512]{1,0:T(8,128)}, bf16[2,128,...) custom-call(f32[2]{0:T(128)} %pad_maximum_fusion.1.live_ref, ...), custom_call_target="tpu_custom_call", output_to_operand_aliasing={{0}: (10, {}), {1}: (11, {}), {2}: (12, {}), {3}: (13, {}),... | custom-call | tf_op jit(solution)/shard_map/wide_attend1/pallas_call | solution.py:559
  106.9 2.1 %all-to-all-done.2.refs_0_ = bf16[32,40,512]{2,1,0:T(8,128)(2,1)S(1)} async-done(((bf16[32,40,512]{2,1,0:T(8,128)(2,1)}), bf16[32,40,512]{2,1,0:T(8,128)(2,1)S(1)}, u32[]{:S(2)}, u32[]{:S(2)}) %all-to-all-start.2) | async-done | bytes 1310752 | tf_op jit(solution)/shard_map/all_to_all | solution.py:635
  109.1 2.1 %collective-permute-start.6 = (bf16[32,8,512]{2,1,0:T(8,128)(2,1)}, bf16[32,8,512]{2,1,0:T(8,128)(2,1)S(1)}, u32[]{:S(2)}, u32[]{:S(2)}) collective-permute-start(bf16[32,8,512]{2,1,0:T(8,128)(2,1)} %get-tuple-element.95), channel_id=1, source_target_pairs={{0,32},{32,0},{64,96},{96,64},{1,33},{33,1},{65,97},{97,65},{2,34}... | collective-permute-start | bytes 786440 | tf_op jit(solution)/shard_map/ppermute | solution.py:631
  111.2 1.4 collective-permute-done.6
  112.5 1.7 %fusion.1 = bf16[32,40,512]{2,1,0:T(8,128)(2,1)} fusion(bf16[32,40,512]{2,1,0:T(8,128)(2,1)} %get-tuple-element.93, bf16[32,8,512]{2,1,0:T(8,128)(2,1)S(1)} %collective-permute-done.6, bf16[32,8,512]{2,1,0:T(8,128)(2,1)} %get-tuple-element.94), kind=kLoop, calls=%fused_computation.3 | loop fusion | flops 524288 | bytes 786432 | tf_op jit(solution)/shard_map/dynamic_update_slice | solution.py:683
  114.2 4.7 %all-to-all-start.3 = ((bf16[32,40,512]{2,1,0:T(8,128)(2,1)}), bf16[32,40,512]{2,1,0:T(8,128)(2,1)S(1)}, u32[]{:S(2)}, u32[]{:S(2)}) async-start(bf16[32,40,512]{2,1,0:T(8,128)(2,1)} %fusion.1), calls=%async_computation.3 | async-start | bytes 2621440 | tf_op jit(solution)/shard_map/all_to_all | solution.py:635
  118.9 3.1 %collective-permute-start.7 = (bf16[2,128,1024]{2,1,0:T(8,128)(2,1)}, bf16[2,128,1024]{2,1,0:T(8,128)(2,1)}, u32[]{:S(2)}, u32[]{:S(2)}) collective-permute-start(bf16[2,128,1024]{2,1,0:T(8,128)(2,1)} %get-tuple-element.99), channel_id=1, source_target_pairs={{0,1},{1,2},{2,3},{3,4},{4,5},{5,6},{6,7},{7,8},{8,9},{9,10},{10,1... | collective-permute-start | bytes 1572872 | tf_op jit(solution)/shard_map/ppermute | solution.py:627
  122.1 7.1 %collective-permute-start.8 = (bf16[2,128,1024]{2,1,0:T(8,128)(2,1)S(1)}, bf16[2,128,1024]{2,1,0:T(8,128)(2,1)}, u32[]{:S(2)}, u32[]{:S(2)}) collective-permute-start(bf16[2,128,1024]{2,1,0:T(8,128)(2,1)S(1)} %copy-done.8), channel_id=1, source_target_pairs={{1,0},{2,1},{3,2},{4,3},{5,4},{6,5},{7,6},{8,7},{9,8},{10,9},{11,1... | collective-permute-start | bytes 1572872 | tf_op jit(solution)/shard_map/ppermute | solution.py:627
  129.1 12.3 %diag_backward.1 = (bf16[512,1024]{1,0:T(8,128)(2,1)}, bf16[512,1024]{1,0:T(8,128)(2,1)}, f32[2,512,1024]{2,1,0:T(8,128)}) custom-call(bf16[512,1024]{1,0:T(8,128)(2,1)} %q_ref.7, bf16[512,1024]{1,0:T(8,128)(2,1)} %k_ref.7, bf16[512,1024]{1,0:T(8,128)(2,1)} %v_ref.7, bf16[8,512,1024]{2,1,0:T(8,128)(2,1)} %get-tuple-element.56.weights_ref, ...), custom_call_target="tpu_custom_call" | custom-call | tf_op jit(solution)/shard_map/diag_backward/pallas_call | solution.py:688
  141.5 0.0 all-to-all-done.3.refs_1_
  141.5 0.4 collect.1
  141.8 0.6 copy-done
  142.5 1.6 %collective-permute-start.9 = (f32[8,1024]{1,0:T(8,128)S(1)}, f32[8,1024]{1,0:T(8,128)S(1)}, u32[]{:S(2)}, u32[]{:S(2)}) collective-permute-start(f32[8,1024]{1,0:T(8,128)S(1)} %get-tuple-element.105.top_ref), channel_id=1, source_target_pairs={{0,64},{32,96},{64,0},{96,32},{1,65},{33,97},{65,1},{97,33},{2,66}... | collective-permute-start | bytes 98312 | tf_op jit(solution)/shard_map/ppermute | solution.py:631
  144.1 6.8 %collective-permute-done.7.prev_ref = bf16[2,128,1024]{2,1,0:T(8,128)(2,1)} collective-permute-done((bf16[2,128,1024]{2,1,0:T(8,128)(2,1)}, bf16[2,128,1024]{2,1,0:T(8,128)(2,1)}, u32[]{:S(2)}, u32[]{:S(2)}) %collective-permute-start.7) | collective-permute-done | bytes 524320 | tf_op jit(solution)/shard_map/ppermute | solution.py:627
  150.9 0.0 collective-permute-done.8.next_ref
  150.9 0.0 collective-permute-done.9.swapped_ref
  150.9 0.6 copy-done.11
  151.5 6.8 %finish.1 = (bf16[512,1024]{1,0:T(8,128)(2,1)}, bf16[512,1024]{1,0:T(8,128)(2,1)}) custom-call(f32[2,512,1024]{2,1,0:T(8,128)} %get-tuple-element.97.diag_ref, f32[2,128,1024]{2,1,0:T(8,128)} %get-tuple-element.98.near_pooled_ref, bf16[2,128,1024]{2,1,0:T(8,128)(2,1)} %collective-permute-done.7.prev_ref, ...), custom_call_target="tpu_custom_call" | custom-call | tf_op jit(solution)/shard_map/finish/pallas_call | solution.py:694
  (27 shorter events, 0.1 us)
Async XLA Ops:
  5.3 8.2 %copy-start.12 = (bf16[2,2,1024]{2,1,0:T(2,128)(2,1)S(1)}, bf16[2,2,1024]{2,1,0:T(2,128)(2,1)}, u32[]{:S(2)}) copy-start(bf16[2,2,1024]{2,1,0:T(2,128)(2,1)} %get-tuple-element.61) | copy-start | bytes 24580
  5.3 8.2 %collective-permute-start = (bf16[2,2,1024]{2,1,0:T(2,128)(2,1)}, bf16[2,2,1024]{2,1,0:T(2,128)(2,1)S(1)}, u32[]{:S(2)}, u32[]{:S(2)}) collective-permute-start(bf16[2,2,1024]{2,1,0:T(2,128)(2,1)} %get-tuple-element.61), channel_id=1, source_target_pairs={{0,64},{32,96},{64,0},{96,32},{1,65},{33,97},{65,1},{97,33},{2,66}... | collective-permute-start | bytes 24584 | tf_op jit(solution)/shard_map/ppermute | solution.py:631
  14.4 8.8 %copy-start.13 = (bf16[2,128,1024]{2,1,0:T(8,128)(2,1)S(1)}, bf16[2,128,1024]{2,1,0:T(8,128)(2,1)}, u32[]{:S(2)}) copy-start(bf16[2,128,1024]{2,1,0:T(8,128)(2,1)} %get-tuple-element.66) | copy-start | bytes 1572868
  14.4 40.0 %all-to-all-start = ((bf16[32,40,512]{2,1,0:T(8,128)(2,1)}), bf16[32,40,512]{2,1,0:T(8,128)(2,1)S(1)}, u32[]{:S(2)}, u32[]{:S(2)}) async-start(bf16[32,40,512]{2,1,0:T(8,128)(2,1)} %broadcast_dynamic-update-slice_fusion), calls=%async_computation | async-start | bytes 2621440 | tf_op jit(solution)/shard_map/all_to_all | solution.py:635
  23.1 26.9 %collective-permute-start.2 = (bf16[2,128,1024]{2,1,0:T(8,128)(2,1)S(1)}, bf16[2,128,1024]{2,1,0:T(8,128)(2,1)S(1)}, u32[]{:S(2)}, u32[]{:S(2)}) collective-permute-start(bf16[2,128,1024]{2,1,0:T(8,128)(2,1)S(1)} %copy-done.13), channel_id=1, source_target_pairs={{1,0},{2,1},{3,2},{4,3},{5,4},{6,5},{7,6},{8,7},{9,8},{10,9},{11,1... | collective-permute-start | bytes 1572872 | tf_op jit(solution)/shard_map/ppermute | solution.py:627
  32.0 22.4 %collective-permute-start.1 = (bf16[2,128,1024]{2,1,0:T(8,128)(2,1)S(1)}, bf16[2,128,1024]{2,1,0:T(8,128)(2,1)S(1)}, u32[]{:S(2)}, u32[]{:S(2)}) collective-permute-start(bf16[2,128,1024]{2,1,0:T(8,128)(2,1)S(1)} %copy-done.13), channel_id=1, source_target_pairs={{0,1},{1,2},{2,3},{3,4},{4,5},{5,6},{6,7},{7,8},{8,9},{9,10},{10,1... | collective-permute-start | bytes 1572872 | tf_op jit(solution)/shard_map/ppermute | solution.py:627
  50.1 5.1 %copy-start.4 = (bf16[2,128,1024]{2,1,0:T(8,128)(2,1)}, bf16[2,128,1024]{2,1,0:T(8,128)(2,1)S(1)}, u32[]{:S(2)}) copy-start(bf16[2,128,1024]{2,1,0:T(8,128)(2,1)S(1)} %collective-permute-done.2.after_ref) | copy-start | bytes 1572868
  54.4 0.8 copy-start.5
  54.4 4.8 %copy-start.3 = (bf16[32,40,512]{2,1,0:T(8,128)(2,1)}, bf16[32,40,512]{2,1,0:T(8,128)(2,1)S(1)}, u32[]{:S(2)}) copy-start(bf16[32,40,512]{2,1,0:T(8,128)(2,1)S(1)} %all-to-all-done.group_ref) | copy-start | bytes 3932164
  55.2 23.3 %all-to-all-start.1 = ((bf16[32,40,512]{2,1,0:T(8,128)(2,1)}), bf16[32,40,512]{2,1,0:T(8,128)(2,1)S(1)}, u32[]{:S(2)}, u32[]{:S(2)}) async-start(bf16[32,40,512]{2,1,0:T(8,128)(2,1)} %broadcast_dynamic-update-slice_fusion.1), calls=%async_computation.1 | async-start | bytes 2621440 | tf_op jit(solution)/shard_map/all_to_all | solution.py:635
  59.2 1.6 %copy-start.7 = (bf16[32,8,512]{2,1,0:T(8,128)(2,1)}, bf16[32,8,512]{2,1,0:T(8,128)(2,1)S(1)}, u32[]{:S(2)}) copy-start(bf16[32,8,512]{2,1,0:T(8,128)(2,1)S(1)} %slice.15.mine_ref) | copy-start | bytes 786436
  59.2 1.6 %collective-permute-start.4 = (bf16[32,8,512]{2,1,0:T(8,128)(2,1)S(1)}, bf16[32,8,512]{2,1,0:T(8,128)(2,1)S(1)}, u32[]{:S(2)}, u32[]{:S(2)}) collective-permute-start(bf16[32,8,512]{2,1,0:T(8,128)(2,1)S(1)} %slice.15.mine_ref), channel_id=1, source_target_pairs={{0,32},{32,0},{64,96},{96,64},{1,33},{33,1},{65,97},{97,65},{2,34}... | collective-permute-start | bytes 786440 | tf_op jit(solution)/shard_map/ppermute | solution.py:631
  60.8 0.7 copy-start.10
  78.1 2.1 %collective-permute-start.5 = (bf16[32,8,512]{2,1,0:T(8,128)(2,1)}, bf16[32,8,512]{2,1,0:T(8,128)(2,1)S(1)}, u32[]{:S(2)}, u32[]{:S(2)}) collective-permute-start(bf16[32,8,512]{2,1,0:T(8,128)(2,1)} %get-tuple-element.75), channel_id=1, source_target_pairs={{0,32},{32,0},{64,96},{96,64},{1,33},{33,1},{65,97},{97,65},{2,34}... | collective-permute-start | bytes 786440 | tf_op jit(solution)/shard_map/ppermute | solution.py:631
  78.5 3.4 %copy-start.2 = (bf16[32,40,512]{2,1,0:T(8,128)(2,1)}, bf16[32,40,512]{2,1,0:T(8,128)(2,1)S(1)}, u32[]{:S(2)}) copy-start(bf16[32,40,512]{2,1,0:T(8,128)(2,1)S(1)} %all-to-all-done.1.group_ref) | copy-start | bytes 3932164
  78.5 3.4 %copy-start.6 = (bf16[32,8,512]{2,1,0:T(8,128)(2,1)}, bf16[32,8,512]{2,1,0:T(8,128)(2,1)S(1)}, u32[]{:S(2)}) copy-start(bf16[32,8,512]{2,1,0:T(8,128)(2,1)S(1)} %slice.18.mine_ref) | copy-start | bytes 786436
  78.5 3.3 %collective-permute-start.3 = (bf16[32,8,512]{2,1,0:T(8,128)(2,1)S(1)}, bf16[32,8,512]{2,1,0:T(8,128)(2,1)S(1)}, u32[]{:S(2)}, u32[]{:S(2)}) collective-permute-start(bf16[32,8,512]{2,1,0:T(8,128)(2,1)S(1)} %slice.18.mine_ref), channel_id=1, source_target_pairs={{0,32},{32,0},{64,96},{96,64},{1,33},{33,1},{65,97},{97,65},{2,34}... | collective-permute-start | bytes 786440 | tf_op jit(solution)/shard_map/ppermute | solution.py:631
  81.9 0.7 copy-start.9
  82.6 26.5 %all-to-all-start.2 = ((bf16[32,40,512]{2,1,0:T(8,128)(2,1)}), bf16[32,40,512]{2,1,0:T(8,128)(2,1)S(1)}, u32[]{:S(2)}, u32[]{:S(2)}) async-start(bf16[32,40,512]{2,1,0:T(8,128)(2,1)} %fusion), calls=%async_computation.2 | async-start | bytes 2621440 | tf_op jit(solution)/shard_map/all_to_all | solution.py:635
  109.1 3.5 %collective-permute-start.6 = (bf16[32,8,512]{2,1,0:T(8,128)(2,1)}, bf16[32,8,512]{2,1,0:T(8,128)(2,1)S(1)}, u32[]{:S(2)}, u32[]{:S(2)}) collective-permute-start(bf16[32,8,512]{2,1,0:T(8,128)(2,1)} %get-tuple-element.95), channel_id=1, source_target_pairs={{0,32},{32,0},{64,96},{96,64},{1,33},{33,1},{65,97},{97,65},{2,34}... | collective-permute-start | bytes 786440 | tf_op jit(solution)/shard_map/ppermute | solution.py:631
  114.2 7.8 %copy-start.8 = (bf16[2,128,1024]{2,1,0:T(8,128)(2,1)S(1)}, bf16[2,128,1024]{2,1,0:T(8,128)(2,1)}, u32[]{:S(2)}) copy-start(bf16[2,128,1024]{2,1,0:T(8,128)(2,1)} %get-tuple-element.100) | copy-start | bytes 1572868
  114.2 27.2 %all-to-all-start.3 = ((bf16[32,40,512]{2,1,0:T(8,128)(2,1)}), bf16[32,40,512]{2,1,0:T(8,128)(2,1)S(1)}, u32[]{:S(2)}, u32[]{:S(2)}) async-start(bf16[32,40,512]{2,1,0:T(8,128)(2,1)} %fusion.1), calls=%async_computation.3 | async-start | bytes 2621440 | tf_op jit(solution)/shard_map/all_to_all | solution.py:635
  118.9 32.0 %collective-permute-start.7 = (bf16[2,128,1024]{2,1,0:T(8,128)(2,1)}, bf16[2,128,1024]{2,1,0:T(8,128)(2,1)}, u32[]{:S(2)}, u32[]{:S(2)}) collective-permute-start(bf16[2,128,1024]{2,1,0:T(8,128)(2,1)} %get-tuple-element.99), channel_id=1, source_target_pairs={{0,1},{1,2},{2,3},{3,4},{4,5},{5,6},{6,7},{7,8},{8,9},{9,10},{10,1... | collective-permute-start | bytes 1572872 | tf_op jit(solution)/shard_map/ppermute | solution.py:627
  122.1 28.8 %collective-permute-start.8 = (bf16[2,128,1024]{2,1,0:T(8,128)(2,1)S(1)}, bf16[2,128,1024]{2,1,0:T(8,128)(2,1)}, u32[]{:S(2)}, u32[]{:S(2)}) collective-permute-start(bf16[2,128,1024]{2,1,0:T(8,128)(2,1)S(1)} %copy-done.8), channel_id=1, source_target_pairs={{1,0},{2,1},{3,2},{4,3},{5,4},{6,5},{7,6},{8,7},{9,8},{10,9},{11,1... | collective-permute-start | bytes 1572872 | tf_op jit(solution)/shard_map/ppermute | solution.py:627
  141.8 0.7 copy-start
  142.5 8.4 %copy-start.1 = (f32[8,1024]{1,0:T(8,128)}, f32[8,1024]{1,0:T(8,128)S(1)}, u32[]{:S(2)}) copy-start(f32[8,1024]{1,0:T(8,128)S(1)} %get-tuple-element.105.top_ref) | copy-start | bytes 98308
  142.5 8.4 %collective-permute-start.9 = (f32[8,1024]{1,0:T(8,128)S(1)}, f32[8,1024]{1,0:T(8,128)S(1)}, u32[]{:S(2)}, u32[]{:S(2)}) collective-permute-start(f32[8,1024]{1,0:T(8,128)S(1)} %get-tuple-element.105.top_ref), channel_id=1, source_target_pairs={{0,64},{32,96},{64,0},{96,32},{1,65},{33,97},{65,1},{97,33},{2,66}... | collective-permute-start | bytes 98312 | tf_op jit(solution)/shard_map/ppermute | solution.py:631
  150.9 0.6 copy-start.11
